TPU v7x, 512 devices: a whole 4x8x8 slice. The times are simulated.
512 devices in a mesh: seq: 32 (over z_hi, x, core), head: 16 (over z_lo, y).
Axes of the slice: x: 4, y: 8, z: 8 (z_hi: 4, z_lo: 2; z = z_hi * 2 + z_lo), core: 2. Of those that a mesh axis runs over, the one named last changes fastest.
Arguments:
- queries: bfloat16 [1024, 128, 576], P('seq', 'head'), may hold values from -1024 to 1024
- latents: bfloat16 [4096, 576], P('seq'), may hold values from -6 to 6
- out_grad: bfloat16 [1024, 128, 512], P('seq', 'head'), may hold values from -6 to 6
- layer_out: bfloat16 [1024, 128, 512], P('seq', 'head'), may hold values from -4 to 4
- query_start: int32 [32], P('seq'), may hold values from 0 to 4095, as said below
Outputs:
- query_grad: bfloat16 [1024, 128, 576], P('seq', 'head')
- latent_grad: float32 [4096, 576], P(('seq', 'head'))
Inputs may be any that keep to these rules, and one draw needn't show every extreme that they name: Shard i holds the 32 queries at consecutive positions from query_start[i]; queries past the last latent position see every latent row.
All inputs are finite; a program needn't handle non-finite values.
Results may differ from a plain program's by a relative error of at most 0.0049.
Values may be sent and summed in bfloat16 or wider, within the bound.
No kernel may reach another device: no remote copies, remote signals or barrier semaphores. Data moves between devices by JAX's collectives and lax.ppermute only.
A program may use at most 64 MiB of HBM per device.

v0:
```python
import jax
import jax.numpy as jnp
from jax import lax
from jax.sharding import PartitionSpec as P

score_scale = 192 ** (-0.5)
masked_score = -1e30


def shifted(block, axis, distance):
    devices = range(lax.axis_size(axis))
    route = [((i - distance) % len(devices), i) for i in devices]
    return lax.ppermute(block, axis, route)


def visible_mask(first_key, key_rows, query_pos):
    key_pos = first_key + lax.iota(jnp.int32, key_rows)
    return key_pos[:, None] <= query_pos[None, :]


def score_block(block_rows, query_rows):
    return (
        lax.dot_general(
            block_rows, query_rows, (((1,), (1,)), ((), ())), preferred_element_type=jnp.float32
        )
        * score_scale
    )


def norm_step(running, block_rows, first_row, query_rows, query_pos):
    run_max, run_sum = running
    shown = visible_mask(first_row, block_rows.shape[0], query_pos)
    scores = jnp.where(shown, score_block(block_rows, query_rows), masked_score)
    new_max = jnp.maximum(run_max, jnp.max(scores, axis=0))
    weights = jnp.where(shown, jnp.exp(scores - new_max[None, :]), 0.0)
    run_sum = jnp.sum(weights, axis=0)
    return (new_max, run_sum)


def grad_block(block_rows, first_row, query_rows, grad_rows, row_delta, log_norm, query_pos):
    shown = visible_mask(first_row, block_rows.shape[0], query_pos)
    scores = score_block(block_rows, query_rows)
    weights = jnp.where(
        shown, jnp.exp(jnp.where(shown, scores - log_norm[None, :], masked_score)), 0.0
    )
    value_width = grad_rows.shape[1]
    prob_grad = lax.dot_general(
        block_rows[:, :value_width],
        grad_rows,
        (((1,), (1,)), ((), ())),
        preferred_element_type=jnp.float32,
    )
    dscore = (score_scale * weights * (prob_grad - row_delta[None, :])).astype(jnp.bfloat16)
    key_term = jnp.dot(dscore, query_rows, preferred_element_type=jnp.float32)
    value_term = jnp.dot(
        weights.astype(jnp.bfloat16), grad_rows, preferred_element_type=jnp.float32
    )
    key_term = key_term + jnp.pad(value_term, ((0, 0), (0, block_rows.shape[1] - value_width)))
    query_term = lax.dot_general(
        dscore, block_rows, (((0,), (0,)), ((), ())), preferred_element_type=jnp.float32
    )
    return (key_term, query_term)


def per_device(queries, latents, out_grad, layer_out, query_start):
    query_count, head_count, key_width = queries.shape
    row_count = query_count * head_count
    query_rows = queries.reshape(row_count, key_width)
    grad_rows = out_grad.reshape(row_count, out_grad.shape[2])
    row_delta = jnp.sum(
        out_grad.astype(jnp.float32) * layer_out.astype(jnp.float32), axis=2
    ).reshape(row_count)
    query_pos = query_start[0] + lax.iota(jnp.int32, row_count) // head_count
    key_count = latents.shape[0]
    cycle_size = lax.axis_size("seq")
    my_index = lax.axis_index("seq")
    start_state = (
        jnp.full((row_count,), masked_score, jnp.float32),
        jnp.zeros((row_count,), jnp.float32),
    )
    block_rows = lax.all_gather(latents, "seq", axis=0, tiled=True)
    running = start_state
    running = norm_step(running, block_rows, jnp.int32(0), query_rows, query_pos)
    add_stored = block_rows
    (run_max, run_sum), stored = (running, add_stored)
    log_norm = run_max + jnp.log(run_sum)

    def visit(first_row, rows, grad_sum, query_sum):
        block_rows = lax.dynamic_slice_in_dim(stored, first_row, rows, 0)
        key_term, query_term = grad_block(
            block_rows, first_row, query_rows, grad_rows, row_delta, log_norm, query_pos
        )
        return (grad_sum + key_term, query_sum + query_term)

    query_start_sum = jnp.zeros((row_count, key_width), jnp.float32)

    def cycle_turn(turn_index, state):
        grad_sum, query_sum = state
        owner_index = (my_index - turn_index - 1) % cycle_size
        grad_sum, query_sum = visit(owner_index * key_count, key_count, grad_sum, query_sum)
        return (shifted(grad_sum, "seq", 1), query_sum)

    start_sum = jnp.zeros((key_count, key_width), jnp.float32)
    grad_sum, query_sum = lax.fori_loop(0, cycle_size - 1, cycle_turn, (start_sum, query_start_sum))
    owned_sum, query_sum = visit(my_index * key_count, key_count, grad_sum, query_sum)
    latent_grad = lax.psum_scatter(owned_sum, "head", scatter_dimension=0, tiled=True)
    query_grad = query_sum.astype(jnp.bfloat16).reshape(query_count, head_count, key_width)
    return (query_grad, latent_grad)


def solution(mesh):
    placed = (
        P("seq", "head", None),
        P("seq", None),
        P("seq", "head", None),
        P("seq", "head", None),
        P("seq"),
    )
    return jax.shard_map(
        per_device,
        mesh=mesh,
        in_specs=placed,
        out_specs=(P("seq", "head", None), P(("seq", "head"), None)),
        check_vma=False,
    )
```

profile of v0, /device:TPU:2, one launch (start us, length us, event | category | flops | bytes accessed | tf_op | source)
XLA Modules:
  0.0 738.1 jit_solution(2161569260429799532)
XLA Ops:
  11.1 75.9 %all-gather.2.cloned.1.call-done = bf16[4096,576]{1,0:T(8,128)(2,1)} async-done(((bf16[128,576]{1,0:T(8,128)(2,1)}), bf16[4096,576]{1,0:T(8,128)(2,1)}) %all-gather.2.cloned.1.call-update) | async-done | bytes 4718608 | tf_op jit(solution)/shard_map/all_gather | solution.py:81
  87.0 4.4 fusion.41
  94.0 479.8 %while.19 = (s32[]{:T(128)}, f32[128,576]{0,1:T(8,128)S(1)}, f32[256,576]{0,1:T(8,128)S(1)}, s32[]{:T(128)}, bf16[4096,576]{1,0:T(8,128)(2,1)}, /*index=5*/bf16[...) while((s32[]{:T(128)}, f32[128,576]{0,1:T(8,128)S(1)}, ...), condition=%wide.wide.region_4.5_spmd.clone, body=%wide.wide.region_3.4_spmd.clone.sunk | while | flops 181127568 | bytes 5641630 | solution.py:104
  97.6 2.2 collective-permute-start
  101.1 4.6 collective-permute-done
  109.2 1.9 collective-permute-start
  112.4 4.8 collective-permute-done
  120.9 1.9 collective-permute-start
  124.1 4.8 collective-permute-done
  132.5 1.9 collective-permute-start
  135.7 8.6 %collective-permute-done = f32[128,576]{0,1:T(8,128)S(1)} collective-permute-done((f32[128,576]{0,1:T(8,128)S(1)}, f32[128,576]{0,1:T(8,128)S(1)}, u32[]{:S(2)}, u32[]{:S(2)}) %collective-permute-start) | collective-permute-done | bytes 294944 | tf_op jit(solution)/shard_map/while/body/eval_jaxpr/ppermute | solution.py:13
  147.9 1.9 collective-permute-start
  151.1 9.0 %collective-permute-done = f32[128,576]{0,1:T(8,128)S(1)} collective-permute-done((f32[128,576]{0,1:T(8,128)S(1)}, f32[128,576]{0,1:T(8,128)S(1)}, u32[]{:S(2)}, u32[]{:S(2)}) %collective-permute-start) | collective-permute-done | bytes 294944 | tf_op jit(solution)/shard_map/while/body/eval_jaxpr/ppermute | solution.py:13
  163.7 1.9 collective-permute-start
  167.0 9.0 %collective-permute-done = f32[128,576]{0,1:T(8,128)S(1)} collective-permute-done((f32[128,576]{0,1:T(8,128)S(1)}, f32[128,576]{0,1:T(8,128)S(1)}, u32[]{:S(2)}, u32[]{:S(2)}) %collective-permute-start) | collective-permute-done | bytes 294944 | tf_op jit(solution)/shard_map/while/body/eval_jaxpr/ppermute | solution.py:13
  179.6 1.9 collective-permute-start
  182.8 9.0 %collective-permute-done = f32[128,576]{0,1:T(8,128)S(1)} collective-permute-done((f32[128,576]{0,1:T(8,128)S(1)}, f32[128,576]{0,1:T(8,128)S(1)}, u32[]{:S(2)}, u32[]{:S(2)}) %collective-permute-start) | collective-permute-done | bytes 294944 | tf_op jit(solution)/shard_map/while/body/eval_jaxpr/ppermute | solution.py:13
  195.4 1.9 collective-permute-start
  198.7 9.0 %collective-permute-done = f32[128,576]{0,1:T(8,128)S(1)} collective-permute-done((f32[128,576]{0,1:T(8,128)S(1)}, f32[128,576]{0,1:T(8,128)S(1)}, u32[]{:S(2)}, u32[]{:S(2)}) %collective-permute-start) | collective-permute-done | bytes 294944 | tf_op jit(solution)/shard_map/while/body/eval_jaxpr/ppermute | solution.py:13
  211.3 1.9 collective-permute-start
  214.5 9.0 %collective-permute-done = f32[128,576]{0,1:T(8,128)S(1)} collective-permute-done((f32[128,576]{0,1:T(8,128)S(1)}, f32[128,576]{0,1:T(8,128)S(1)}, u32[]{:S(2)}, u32[]{:S(2)}) %collective-permute-start) | collective-permute-done | bytes 294944 | tf_op jit(solution)/shard_map/while/body/eval_jaxpr/ppermute | solution.py:13
  227.1 1.9 collective-permute-start
  230.3 9.0 %collective-permute-done = f32[128,576]{0,1:T(8,128)S(1)} collective-permute-done((f32[128,576]{0,1:T(8,128)S(1)}, f32[128,576]{0,1:T(8,128)S(1)}, u32[]{:S(2)}, u32[]{:S(2)}) %collective-permute-start) | collective-permute-done | bytes 294944 | tf_op jit(solution)/shard_map/while/body/eval_jaxpr/ppermute | solution.py:13
  243.0 1.9 collective-permute-start
  246.2 9.0 %collective-permute-done = f32[128,576]{0,1:T(8,128)S(1)} collective-permute-done((f32[128,576]{0,1:T(8,128)S(1)}, f32[128,576]{0,1:T(8,128)S(1)}, u32[]{:S(2)}, u32[]{:S(2)}) %collective-permute-start) | collective-permute-done | bytes 294944 | tf_op jit(solution)/shard_map/while/body/eval_jaxpr/ppermute | solution.py:13
  258.8 1.9 collective-permute-start
  262.0 9.0 %collective-permute-done = f32[128,576]{0,1:T(8,128)S(1)} collective-permute-done((f32[128,576]{0,1:T(8,128)S(1)}, f32[128,576]{0,1:T(8,128)S(1)}, u32[]{:S(2)}, u32[]{:S(2)}) %collective-permute-start) | collective-permute-done | bytes 294944 | tf_op jit(solution)/shard_map/while/body/eval_jaxpr/ppermute | solution.py:13
  274.6 1.9 collective-permute-start
  277.9 9.0 %collective-permute-done = f32[128,576]{0,1:T(8,128)S(1)} collective-permute-done((f32[128,576]{0,1:T(8,128)S(1)}, f32[128,576]{0,1:T(8,128)S(1)}, u32[]{:S(2)}, u32[]{:S(2)}) %collective-permute-start) | collective-permute-done | bytes 294944 | tf_op jit(solution)/shard_map/while/body/eval_jaxpr/ppermute | solution.py:13
  290.5 1.9 collective-permute-start
  293.7 9.0 %collective-permute-done = f32[128,576]{0,1:T(8,128)S(1)} collective-permute-done((f32[128,576]{0,1:T(8,128)S(1)}, f32[128,576]{0,1:T(8,128)S(1)}, u32[]{:S(2)}, u32[]{:S(2)}) %collective-permute-start) | collective-permute-done | bytes 294944 | tf_op jit(solution)/shard_map/while/body/eval_jaxpr/ppermute | solution.py:13
  306.3 1.9 collective-permute-start
  309.5 9.1 %collective-permute-done = f32[128,576]{0,1:T(8,128)S(1)} collective-permute-done((f32[128,576]{0,1:T(8,128)S(1)}, f32[128,576]{0,1:T(8,128)S(1)}, u32[]{:S(2)}, u32[]{:S(2)}) %collective-permute-start) | collective-permute-done | bytes 294944 | tf_op jit(solution)/shard_map/while/body/eval_jaxpr/ppermute | solution.py:13
  322.3 1.9 collective-permute-start
  325.5 9.1 %collective-permute-done = f32[128,576]{0,1:T(8,128)S(1)} collective-permute-done((f32[128,576]{0,1:T(8,128)S(1)}, f32[128,576]{0,1:T(8,128)S(1)}, u32[]{:S(2)}, u32[]{:S(2)}) %collective-permute-start) | collective-permute-done | bytes 294944 | tf_op jit(solution)/shard_map/while/body/eval_jaxpr/ppermute | solution.py:13
  338.2 1.9 collective-permute-start
  341.4 9.1 %collective-permute-done = f32[128,576]{0,1:T(8,128)S(1)} collective-permute-done((f32[128,576]{0,1:T(8,128)S(1)}, f32[128,576]{0,1:T(8,128)S(1)}, u32[]{:S(2)}, u32[]{:S(2)}) %collective-permute-start) | collective-permute-done | bytes 294944 | tf_op jit(solution)/shard_map/while/body/eval_jaxpr/ppermute | solution.py:13
  354.1 1.9 collective-permute-start
  357.4 9.1 %collective-permute-done = f32[128,576]{0,1:T(8,128)S(1)} collective-permute-done((f32[128,576]{0,1:T(8,128)S(1)}, f32[128,576]{0,1:T(8,128)S(1)}, u32[]{:S(2)}, u32[]{:S(2)}) %collective-permute-start) | collective-permute-done | bytes 294944 | tf_op jit(solution)/shard_map/while/body/eval_jaxpr/ppermute | solution.py:13
  370.1 1.9 collective-permute-start
  373.3 9.1 %collective-permute-done = f32[128,576]{0,1:T(8,128)S(1)} collective-permute-done((f32[128,576]{0,1:T(8,128)S(1)}, f32[128,576]{0,1:T(8,128)S(1)}, u32[]{:S(2)}, u32[]{:S(2)}) %collective-permute-start) | collective-permute-done | bytes 294944 | tf_op jit(solution)/shard_map/while/body/eval_jaxpr/ppermute | solution.py:13
  386.0 1.9 collective-permute-start
  389.2 9.1 %collective-permute-done = f32[128,576]{0,1:T(8,128)S(1)} collective-permute-done((f32[128,576]{0,1:T(8,128)S(1)}, f32[128,576]{0,1:T(8,128)S(1)}, u32[]{:S(2)}, u32[]{:S(2)}) %collective-permute-start) | collective-permute-done | bytes 294944 | tf_op jit(solution)/shard_map/while/body/eval_jaxpr/ppermute | solution.py:13
  402.0 1.9 collective-permute-start
  405.2 9.1 %collective-permute-done = f32[128,576]{0,1:T(8,128)S(1)} collective-permute-done((f32[128,576]{0,1:T(8,128)S(1)}, f32[128,576]{0,1:T(8,128)S(1)}, u32[]{:S(2)}, u32[]{:S(2)}) %collective-permute-start) | collective-permute-done | bytes 294944 | tf_op jit(solution)/shard_map/while/body/eval_jaxpr/ppermute | solution.py:13
  417.9 1.9 collective-permute-start
  421.1 9.1 %collective-permute-done = f32[128,576]{0,1:T(8,128)S(1)} collective-permute-done((f32[128,576]{0,1:T(8,128)S(1)}, f32[128,576]{0,1:T(8,128)S(1)}, u32[]{:S(2)}, u32[]{:S(2)}) %collective-permute-start) | collective-permute-done | bytes 294944 | tf_op jit(solution)/shard_map/while/body/eval_jaxpr/ppermute | solution.py:13
  433.8 1.9 collective-permute-start
  437.1 9.1 %collective-permute-done = f32[128,576]{0,1:T(8,128)S(1)} collective-permute-done((f32[128,576]{0,1:T(8,128)S(1)}, f32[128,576]{0,1:T(8,128)S(1)}, u32[]{:S(2)}, u32[]{:S(2)}) %collective-permute-start) | collective-permute-done | bytes 294944 | tf_op jit(solution)/shard_map/while/body/eval_jaxpr/ppermute | solution.py:13
  449.8 1.9 collective-permute-start
  453.0 9.1 %collective-permute-done = f32[128,576]{0,1:T(8,128)S(1)} collective-permute-done((f32[128,576]{0,1:T(8,128)S(1)}, f32[128,576]{0,1:T(8,128)S(1)}, u32[]{:S(2)}, u32[]{:S(2)}) %collective-permute-start) | collective-permute-done | bytes 294944 | tf_op jit(solution)/shard_map/while/body/eval_jaxpr/ppermute | solution.py:13
  465.7 1.9 collective-permute-start
  468.9 9.1 %collective-permute-done = f32[128,576]{0,1:T(8,128)S(1)} collective-permute-done((f32[128,576]{0,1:T(8,128)S(1)}, f32[128,576]{0,1:T(8,128)S(1)}, u32[]{:S(2)}, u32[]{:S(2)}) %collective-permute-start) | collective-permute-done | bytes 294944 | tf_op jit(solution)/shard_map/while/body/eval_jaxpr/ppermute | solution.py:13
  481.7 1.9 collective-permute-start
  484.9 9.1 %collective-permute-done = f32[128,576]{0,1:T(8,128)S(1)} collective-permute-done((f32[128,576]{0,1:T(8,128)S(1)}, f32[128,576]{0,1:T(8,128)S(1)}, u32[]{:S(2)}, u32[]{:S(2)}) %collective-permute-start) | collective-permute-done | bytes 294944 | tf_op jit(solution)/shard_map/while/body/eval_jaxpr/ppermute | solution.py:13
  497.6 1.9 collective-permute-start
  500.8 9.1 %collective-permute-done = f32[128,576]{0,1:T(8,128)S(1)} collective-permute-done((f32[128,576]{0,1:T(8,128)S(1)}, f32[128,576]{0,1:T(8,128)S(1)}, u32[]{:S(2)}, u32[]{:S(2)}) %collective-permute-start) | collective-permute-done | bytes 294944 | tf_op jit(solution)/shard_map/while/body/eval_jaxpr/ppermute | solution.py:13
  516.8 9.1 %collective-permute-done = f32[128,576]{0,1:T(8,128)S(1)} collective-permute-done((f32[128,576]{0,1:T(8,128)S(1)}, f32[128,576]{0,1:T(8,128)S(1)}, u32[]{:S(2)}, u32[]{:S(2)}) %collective-permute-start) | collective-permute-done | bytes 294944 | tf_op jit(solution)/shard_map/while/body/eval_jaxpr/ppermute | solution.py:13
  532.7 9.1 %collective-permute-done = f32[128,576]{0,1:T(8,128)S(1)} collective-permute-done((f32[128,576]{0,1:T(8,128)S(1)}, f32[128,576]{0,1:T(8,128)S(1)}, u32[]{:S(2)}, u32[]{:S(2)}) %collective-permute-start) | collective-permute-done | bytes 294944 | tf_op jit(solution)/shard_map/while/body/eval_jaxpr/ppermute | solution.py:13
  545.4 1.9 collective-permute-start
  548.7 9.1 %collective-permute-done = f32[128,576]{0,1:T(8,128)S(1)} collective-permute-done((f32[128,576]{0,1:T(8,128)S(1)}, f32[128,576]{0,1:T(8,128)S(1)}, u32[]{:S(2)}, u32[]{:S(2)}) %collective-permute-start) | collective-permute-done | bytes 294944 | tf_op jit(solution)/shard_map/while/body/eval_jaxpr/ppermute | solution.py:13
  561.4 1.9 collective-permute-start
  564.6 9.1 %collective-permute-done = f32[128,576]{0,1:T(8,128)S(1)} collective-permute-done((f32[128,576]{0,1:T(8,128)S(1)}, f32[128,576]{0,1:T(8,128)S(1)}, u32[]{:S(2)}, u32[]{:S(2)}) %collective-permute-start) | collective-permute-done | bytes 294944 | tf_op jit(solution)/shard_map/while/body/eval_jaxpr/ppermute | solution.py:13
  580.1 149.8 %all-reduce.5.cloned.1.call-done = f32[128,576]{1,0:T(8,128)} async-done(((f32[128,576]{1,0:T(8,128)}), f32[128,576]{1,0:T(8,128)}) %all-reduce.5.cloned.1.call-update) | async-done | bytes 294928
  (249 shorter events, 166.1 us)
Async XLA Ops:
  7.2 79.9 %all-gather.2.cloned.1.call-start = ((), (), s32[]{:S(2)}) async-start(), calls=%async_computation | async-start | bytes 5406720 | tf_op jit(solution)/shard_map/all_gather | solution.py:81
  8.9 720.9 %all-reduce.5.cloned.1.call-start = ((), (), s32[]{:S(2)}) async-start(), calls=%async_computation.1 | async-start | bytes 655360
  10.2 81.2 %copy-start.2 = (f32[32,8]{1,0:T(8,128)}, f32[32,8]{1,0:T(8,128)S(1)}, u32[]{:S(2)}) copy-start(f32[32,8]{1,0:T(8,128)S(1)} %multiply_reduce_fusion) | copy-start | bytes 3076
  11.1 81.5 %copy-start = (bf16[32,8,576]{2,1,0:T(8,128)(2,1)S(1)}, bf16[32,8,576]{2,1,0:T(8,128)(2,1)}, u32[]{:S(2)}) copy-start(bf16[32,8,576]{2,1,0:T(8,128)(2,1)} %param.7) | copy-start | bytes 884740
  11.1 82.7 %copy-start.1 = (bf16[32,8,512]{2,1,0:T(8,128)(2,1)S(1)}, bf16[32,8,512]{2,1,0:T(8,128)(2,1)}, u32[]{:S(2)}) copy-start(bf16[32,8,512]{2,1,0:T(8,128)(2,1)} %param.9) | copy-start | bytes 786436
  97.6 8.0 %collective-permute-start = (f32[128,576]{0,1:T(8,128)S(1)}, f32[128,576]{0,1:T(8,128)S(1)}, u32[]{:S(2)}, u32[]{:S(2)}) collective-permute-start(f32[128,576]{0,1:T(8,128)S(1)} %fusion.95), channel_id=1, source_target_pairs={{496,0},{0,16},{16,32},{32,48},{48,64},{64,80},{80,96},{96,112},{1... | collective-permute-start | bytes 884744 | tf_op jit(solution)/shard_map/while/body/eval_jaxpr/ppermute | solution.py:13
  109.2 8.0 %collective-permute-start = (f32[128,576]{0,1:T(8,128)S(1)}, f32[128,576]{0,1:T(8,128)S(1)}, u32[]{:S(2)}, u32[]{:S(2)}) collective-permute-start(f32[128,576]{0,1:T(8,128)S(1)} %fusion.95), channel_id=1, source_target_pairs={{496,0},{0,16},{16,32},{32,48},{48,64},{64,80},{80,96},{96,112},{1... | collective-permute-start | bytes 884744 | tf_op jit(solution)/shard_map/while/body/eval_jaxpr/ppermute | solution.py:13
  120.9 8.0 %collective-permute-start = (f32[128,576]{0,1:T(8,128)S(1)}, f32[128,576]{0,1:T(8,128)S(1)}, u32[]{:S(2)}, u32[]{:S(2)}) collective-permute-start(f32[128,576]{0,1:T(8,128)S(1)} %fusion.95), channel_id=1, source_target_pairs={{496,0},{0,16},{16,32},{32,48},{48,64},{64,80},{80,96},{96,112},{1... | collective-permute-start | bytes 884744 | tf_op jit(solution)/shard_map/while/body/eval_jaxpr/ppermute | solution.py:13
  132.5 11.8 %collective-permute-start = (f32[128,576]{0,1:T(8,128)S(1)}, f32[128,576]{0,1:T(8,128)S(1)}, u32[]{:S(2)}, u32[]{:S(2)}) collective-permute-start(f32[128,576]{0,1:T(8,128)S(1)} %fusion.95), channel_id=1, source_target_pairs={{496,0},{0,16},{16,32},{32,48},{48,64},{64,80},{80,96},{96,112},{1... | collective-permute-start | bytes 884744 | tf_op jit(solution)/shard_map/while/body/eval_jaxpr/ppermute | solution.py:13
  147.9 12.3 %collective-permute-start = (f32[128,576]{0,1:T(8,128)S(1)}, f32[128,576]{0,1:T(8,128)S(1)}, u32[]{:S(2)}, u32[]{:S(2)}) collective-permute-start(f32[128,576]{0,1:T(8,128)S(1)} %fusion.95), channel_id=1, source_target_pairs={{496,0},{0,16},{16,32},{32,48},{48,64},{64,80},{80,96},{96,112},{1... | collective-permute-start | bytes 884744 | tf_op jit(solution)/shard_map/while/body/eval_jaxpr/ppermute | solution.py:13
  163.7 12.3 %collective-permute-start = (f32[128,576]{0,1:T(8,128)S(1)}, f32[128,576]{0,1:T(8,128)S(1)}, u32[]{:S(2)}, u32[]{:S(2)}) collective-permute-start(f32[128,576]{0,1:T(8,128)S(1)} %fusion.95), channel_id=1, source_target_pairs={{496,0},{0,16},{16,32},{32,48},{48,64},{64,80},{80,96},{96,112},{1... | collective-permute-start | bytes 884744 | tf_op jit(solution)/shard_map/while/body/eval_jaxpr/ppermute | solution.py:13
  179.6 12.3 %collective-permute-start = (f32[128,576]{0,1:T(8,128)S(1)}, f32[128,576]{0,1:T(8,128)S(1)}, u32[]{:S(2)}, u32[]{:S(2)}) collective-permute-start(f32[128,576]{0,1:T(8,128)S(1)} %fusion.95), channel_id=1, source_target_pairs={{496,0},{0,16},{16,32},{32,48},{48,64},{64,80},{80,96},{96,112},{1... | collective-permute-start | bytes 884744 | tf_op jit(solution)/shard_map/while/body/eval_jaxpr/ppermute | solution.py:13
  195.4 12.3 %collective-permute-start = (f32[128,576]{0,1:T(8,128)S(1)}, f32[128,576]{0,1:T(8,128)S(1)}, u32[]{:S(2)}, u32[]{:S(2)}) collective-permute-start(f32[128,576]{0,1:T(8,128)S(1)} %fusion.95), channel_id=1, source_target_pairs={{496,0},{0,16},{16,32},{32,48},{48,64},{64,80},{80,96},{96,112},{1... | collective-permute-start | bytes 884744 | tf_op jit(solution)/shard_map/while/body/eval_jaxpr/ppermute | solution.py:13
  211.3 12.3 %collective-permute-start = (f32[128,576]{0,1:T(8,128)S(1)}, f32[128,576]{0,1:T(8,128)S(1)}, u32[]{:S(2)}, u32[]{:S(2)}) collective-permute-start(f32[128,576]{0,1:T(8,128)S(1)} %fusion.95), channel_id=1, source_target_pairs={{496,0},{0,16},{16,32},{32,48},{48,64},{64,80},{80,96},{96,112},{1... | collective-permute-start | bytes 884744 | tf_op jit(solution)/shard_map/while/body/eval_jaxpr/ppermute | solution.py:13
  227.1 12.3 %collective-permute-start = (f32[128,576]{0,1:T(8,128)S(1)}, f32[128,576]{0,1:T(8,128)S(1)}, u32[]{:S(2)}, u32[]{:S(2)}) collective-permute-start(f32[128,576]{0,1:T(8,128)S(1)} %fusion.95), channel_id=1, source_target_pairs={{496,0},{0,16},{16,32},{32,48},{48,64},{64,80},{80,96},{96,112},{1... | collective-permute-start | bytes 884744 | tf_op jit(solution)/shard_map/while/body/eval_jaxpr/ppermute | solution.py:13
  243.0 12.3 %collective-permute-start = (f32[128,576]{0,1:T(8,128)S(1)}, f32[128,576]{0,1:T(8,128)S(1)}, u32[]{:S(2)}, u32[]{:S(2)}) collective-permute-start(f32[128,576]{0,1:T(8,128)S(1)} %fusion.95), channel_id=1, source_target_pairs={{496,0},{0,16},{16,32},{32,48},{48,64},{64,80},{80,96},{96,112},{1... | collective-permute-start | bytes 884744 | tf_op jit(solution)/shard_map/while/body/eval_jaxpr/ppermute | solution.py:13
  258.8 12.3 %collective-permute-start = (f32[128,576]{0,1:T(8,128)S(1)}, f32[128,576]{0,1:T(8,128)S(1)}, u32[]{:S(2)}, u32[]{:S(2)}) collective-permute-start(f32[128,576]{0,1:T(8,128)S(1)} %fusion.95), channel_id=1, source_target_pairs={{496,0},{0,16},{16,32},{32,48},{48,64},{64,80},{80,96},{96,112},{1... | collective-permute-start | bytes 884744 | tf_op jit(solution)/shard_map/while/body/eval_jaxpr/ppermute | solution.py:13
  274.6 12.3 %collective-permute-start = (f32[128,576]{0,1:T(8,128)S(1)}, f32[128,576]{0,1:T(8,128)S(1)}, u32[]{:S(2)}, u32[]{:S(2)}) collective-permute-start(f32[128,576]{0,1:T(8,128)S(1)} %fusion.95), channel_id=1, source_target_pairs={{496,0},{0,16},{16,32},{32,48},{48,64},{64,80},{80,96},{96,112},{1... | collective-permute-start | bytes 884744 | tf_op jit(solution)/shard_map/while/body/eval_jaxpr/ppermute | solution.py:13
  290.5 12.3 %collective-permute-start = (f32[128,576]{0,1:T(8,128)S(1)}, f32[128,576]{0,1:T(8,128)S(1)}, u32[]{:S(2)}, u32[]{:S(2)}) collective-permute-start(f32[128,576]{0,1:T(8,128)S(1)} %fusion.95), channel_id=1, source_target_pairs={{496,0},{0,16},{16,32},{32,48},{48,64},{64,80},{80,96},{96,112},{1... | collective-permute-start | bytes 884744 | tf_op jit(solution)/shard_map/while/body/eval_jaxpr/ppermute | solution.py:13
  306.3 12.3 %collective-permute-start = (f32[128,576]{0,1:T(8,128)S(1)}, f32[128,576]{0,1:T(8,128)S(1)}, u32[]{:S(2)}, u32[]{:S(2)}) collective-permute-start(f32[128,576]{0,1:T(8,128)S(1)} %fusion.95), channel_id=1, source_target_pairs={{496,0},{0,16},{16,32},{32,48},{48,64},{64,80},{80,96},{96,112},{1... | collective-permute-start | bytes 884744 | tf_op jit(solution)/shard_map/while/body/eval_jaxpr/ppermute | solution.py:13
  322.3 12.4 %collective-permute-start = (f32[128,576]{0,1:T(8,128)S(1)}, f32[128,576]{0,1:T(8,128)S(1)}, u32[]{:S(2)}, u32[]{:S(2)}) collective-permute-start(f32[128,576]{0,1:T(8,128)S(1)} %fusion.95), channel_id=1, source_target_pairs={{496,0},{0,16},{16,32},{32,48},{48,64},{64,80},{80,96},{96,112},{1... | collective-permute-start | bytes 884744 | tf_op jit(solution)/shard_map/while/body/eval_jaxpr/ppermute | solution.py:13
  338.2 12.4 %collective-permute-start = (f32[128,576]{0,1:T(8,128)S(1)}, f32[128,576]{0,1:T(8,128)S(1)}, u32[]{:S(2)}, u32[]{:S(2)}) collective-permute-start(f32[128,576]{0,1:T(8,128)S(1)} %fusion.95), channel_id=1, source_target_pairs={{496,0},{0,16},{16,32},{32,48},{48,64},{64,80},{80,96},{96,112},{1... | collective-permute-start | bytes 884744 | tf_op jit(solution)/shard_map/while/body/eval_jaxpr/ppermute | solution.py:13
  354.1 12.4 %collective-permute-start = (f32[128,576]{0,1:T(8,128)S(1)}, f32[128,576]{0,1:T(8,128)S(1)}, u32[]{:S(2)}, u32[]{:S(2)}) collective-permute-start(f32[128,576]{0,1:T(8,128)S(1)} %fusion.95), channel_id=1, source_target_pairs={{496,0},{0,16},{16,32},{32,48},{48,64},{64,80},{80,96},{96,112},{1... | collective-permute-start | bytes 884744 | tf_op jit(solution)/shard_map/while/body/eval_jaxpr/ppermute | solution.py:13
  370.1 12.4 %collective-permute-start = (f32[128,576]{0,1:T(8,128)S(1)}, f32[128,576]{0,1:T(8,128)S(1)}, u32[]{:S(2)}, u32[]{:S(2)}) collective-permute-start(f32[128,576]{0,1:T(8,128)S(1)} %fusion.95), channel_id=1, source_target_pairs={{496,0},{0,16},{16,32},{32,48},{48,64},{64,80},{80,96},{96,112},{1... | collective-permute-start | bytes 884744 | tf_op jit(solution)/shard_map/while/body/eval_jaxpr/ppermute | solution.py:13
  386.0 12.4 %collective-permute-start = (f32[128,576]{0,1:T(8,128)S(1)}, f32[128,576]{0,1:T(8,128)S(1)}, u32[]{:S(2)}, u32[]{:S(2)}) collective-permute-start(f32[128,576]{0,1:T(8,128)S(1)} %fusion.95), channel_id=1, source_target_pairs={{496,0},{0,16},{16,32},{32,48},{48,64},{64,80},{80,96},{96,112},{1... | collective-permute-start | bytes 884744 | tf_op jit(solution)/shard_map/while/body/eval_jaxpr/ppermute | solution.py:13
  402.0 12.4 %collective-permute-start = (f32[128,576]{0,1:T(8,128)S(1)}, f32[128,576]{0,1:T(8,128)S(1)}, u32[]{:S(2)}, u32[]{:S(2)}) collective-permute-start(f32[128,576]{0,1:T(8,128)S(1)} %fusion.95), channel_id=1, source_target_pairs={{496,0},{0,16},{16,32},{32,48},{48,64},{64,80},{80,96},{96,112},{1... | collective-permute-start | bytes 884744 | tf_op jit(solution)/shard_map/while/body/eval_jaxpr/ppermute | solution.py:13
  417.9 12.4 %collective-permute-start = (f32[128,576]{0,1:T(8,128)S(1)}, f32[128,576]{0,1:T(8,128)S(1)}, u32[]{:S(2)}, u32[]{:S(2)}) collective-permute-start(f32[128,576]{0,1:T(8,128)S(1)} %fusion.95), channel_id=1, source_target_pairs={{496,0},{0,16},{16,32},{32,48},{48,64},{64,80},{80,96},{96,112},{1... | collective-permute-start | bytes 884744 | tf_op jit(solution)/shard_map/while/body/eval_jaxpr/ppermute | solution.py:13
  433.8 12.4 %collective-permute-start = (f32[128,576]{0,1:T(8,128)S(1)}, f32[128,576]{0,1:T(8,128)S(1)}, u32[]{:S(2)}, u32[]{:S(2)}) collective-permute-start(f32[128,576]{0,1:T(8,128)S(1)} %fusion.95), channel_id=1, source_target_pairs={{496,0},{0,16},{16,32},{32,48},{48,64},{64,80},{80,96},{96,112},{1... | collective-permute-start | bytes 884744 | tf_op jit(solution)/shard_map/while/body/eval_jaxpr/ppermute | solution.py:13
  449.8 12.4 %collective-permute-start = (f32[128,576]{0,1:T(8,128)S(1)}, f32[128,576]{0,1:T(8,128)S(1)}, u32[]{:S(2)}, u32[]{:S(2)}) collective-permute-start(f32[128,576]{0,1:T(8,128)S(1)} %fusion.95), channel_id=1, source_target_pairs={{496,0},{0,16},{16,32},{32,48},{48,64},{64,80},{80,96},{96,112},{1... | collective-permute-start | bytes 884744 | tf_op jit(solution)/shard_map/while/body/eval_jaxpr/ppermute | solution.py:13
  465.7 12.4 %collective-permute-start = (f32[128,576]{0,1:T(8,128)S(1)}, f32[128,576]{0,1:T(8,128)S(1)}, u32[]{:S(2)}, u32[]{:S(2)}) collective-permute-start(f32[128,576]{0,1:T(8,128)S(1)} %fusion.95), channel_id=1, source_target_pairs={{496,0},{0,16},{16,32},{32,48},{48,64},{64,80},{80,96},{96,112},{1... | collective-permute-start | bytes 884744 | tf_op jit(solution)/shard_map/while/body/eval_jaxpr/ppermute | solution.py:13
  481.7 12.4 %collective-permute-start = (f32[128,576]{0,1:T(8,128)S(1)}, f32[128,576]{0,1:T(8,128)S(1)}, u32[]{:S(2)}, u32[]{:S(2)}) collective-permute-start(f32[128,576]{0,1:T(8,128)S(1)} %fusion.95), channel_id=1, source_target_pairs={{496,0},{0,16},{16,32},{32,48},{48,64},{64,80},{80,96},{96,112},{1... | collective-permute-start | bytes 884744 | tf_op jit(solution)/shard_map/while/body/eval_jaxpr/ppermute | solution.py:13
  497.6 12.4 %collective-permute-start = (f32[128,576]{0,1:T(8,128)S(1)}, f32[128,576]{0,1:T(8,128)S(1)}, u32[]{:S(2)}, u32[]{:S(2)}) collective-permute-start(f32[128,576]{0,1:T(8,128)S(1)} %fusion.95), channel_id=1, source_target_pairs={{496,0},{0,16},{16,32},{32,48},{48,64},{64,80},{80,96},{96,112},{1... | collective-permute-start | bytes 884744 | tf_op jit(solution)/shard_map/while/body/eval_jaxpr/ppermute | solution.py:13
  513.6 12.4 %collective-permute-start = (f32[128,576]{0,1:T(8,128)S(1)}, f32[128,576]{0,1:T(8,128)S(1)}, u32[]{:S(2)}, u32[]{:S(2)}) collective-permute-start(f32[128,576]{0,1:T(8,128)S(1)} %fusion.95), channel_id=1, source_target_pairs={{496,0},{0,16},{16,32},{32,48},{48,64},{64,80},{80,96},{96,112},{1... | collective-permute-start | bytes 884744 | tf_op jit(solution)/shard_map/while/body/eval_jaxpr/ppermute | solution.py:13
  529.5 12.4 %collective-permute-start = (f32[128,576]{0,1:T(8,128)S(1)}, f32[128,576]{0,1:T(8,128)S(1)}, u32[]{:S(2)}, u32[]{:S(2)}) collective-permute-start(f32[128,576]{0,1:T(8,128)S(1)} %fusion.95), channel_id=1, source_target_pairs={{496,0},{0,16},{16,32},{32,48},{48,64},{64,80},{80,96},{96,112},{1... | collective-permute-start | bytes 884744 | tf_op jit(solution)/shard_map/while/body/eval_jaxpr/ppermute | solution.py:13
  545.4 12.4 %collective-permute-start = (f32[128,576]{0,1:T(8,128)S(1)}, f32[128,576]{0,1:T(8,128)S(1)}, u32[]{:S(2)}, u32[]{:S(2)}) collective-permute-start(f32[128,576]{0,1:T(8,128)S(1)} %fusion.95), channel_id=1, source_target_pairs={{496,0},{0,16},{16,32},{32,48},{48,64},{64,80},{80,96},{96,112},{1... | collective-permute-start | bytes 884744 | tf_op jit(solution)/shard_map/while/body/eval_jaxpr/ppermute | solution.py:13
  561.4 12.4 %collective-permute-start = (f32[128,576]{0,1:T(8,128)S(1)}, f32[128,576]{0,1:T(8,128)S(1)}, u32[]{:S(2)}, u32[]{:S(2)}) collective-permute-start(f32[128,576]{0,1:T(8,128)S(1)} %fusion.95), channel_id=1, source_target_pairs={{496,0},{0,16},{16,32},{32,48},{48,64},{64,80},{80,96},{96,112},{1... | collective-permute-start | bytes 884744 | tf_op jit(solution)/shard_map/while/body/eval_jaxpr/ppermute | solution.py:13
Sparse Core Ops, SparseCore 0:
  11.7 75.2 all-gather.1
  576.1 153.7 all-reduce.4
where the time goes:
time: 741 us; the launch traced here: 738 us
  waiting for transfers between devices  494 us (67%)
  matrix products  138 us (19%)
  starting transfers between devices  59.9 us (8%)
  other arithmetic  22.5 us (3%)
  between operations  15.5 us (2%)
    ppermute x31, waiting for transfers between devices, shifted(): return lax.ppermute(block, axis, route)  269 us
    unnamed x3, waiting for transfers between devices  150 us
    all_gather x1, waiting for transfers between devices, per_device(): block_rows = lax.all_gather(latents, 'seq', axis=0, tiled=True)  75.9 us
    ppermute x31, starting transfers between devices, shifted(): return lax.ppermute(block, axis, route)  59.8 us
    dot_general x33, matrix products, score_block(): lax.dot_general(block_rows, query_rows, (((1,), (1,)), ((), ())), preferr...  42.6 us
    dot_general x32, matrix products, grad_block(): lax.dot_general(dscore, block_rows, (((0,), (0,)), ((), ())), preferred_e...  40.9 us
    dot_general x32, matrix products, grad_block(): lax.dot_general(block_rows[:, :value_width], grad_rows, (((1,), (1,)), ((...  36.5 us
    add x32, other arithmetic, per_device(): query_pos = query_start[0] + lax.iota(jnp.int32, row_count) // head_count  20.1 us
  transfers between devices with their start and end apart: 33, of which 33 were waited for; matrix products, arithmetic and copies ran while one was open for 6% of the time, Pallas kernels for 0%

commit v1 on v0

v1 whole, which is shorter than its diff:
```python
import jax
import jax.numpy as jnp
from jax import lax
from jax.experimental import pallas as pl
from jax.experimental.pallas import tpu as pltpu
from jax.sharding import Mesh, PartitionSpec as P

score_scale = 192 ** (-0.5)
masked_score = -1e30
least_top = -1e29

ROWS = 256
WIDE = 640
VALUES = 512
PACK = 1152
KEYS = 1024
TILE = 128
TEAM = 4

FINE = ("zh", "x", "c", "zl", "yh", "y0")


def prep_kernel(start_ref, q_ref, do_ref, lo_ref, out_ref):
    grad = do_ref[...]
    delta = jnp.sum(
        grad.astype(jnp.float32) * lo_ref[...].astype(jnp.float32), axis=1, keepdims=True
    )
    first = delta.astype(jnp.bfloat16).astype(jnp.float32)
    second = (delta - first).astype(jnp.bfloat16).astype(jnp.float32)
    third = delta - first - second
    pos = start_ref[0] + lax.broadcasted_iota(jnp.int32, (ROWS, 64), 0) // 8
    lane = lax.broadcasted_iota(jnp.int32, (ROWS, 64), 1)
    extra = jnp.where(lane == 0, first, 0.0)
    extra = jnp.where(lane == 1, second, extra)
    extra = jnp.where(lane == 2, third, extra)
    extra = jnp.where(lane == 3, (pos // 64).astype(jnp.float32), extra)
    extra = jnp.where(lane == 4, (pos % 64).astype(jnp.float32), extra)
    out_ref[:, :VALUES] = grad
    out_ref[:, VALUES:VALUES + 512] = q_ref[:, :512]
    out_ref[:, VALUES + 512:] = jnp.concatenate(
        [q_ref[:, 512:576], extra.astype(jnp.bfloat16)], axis=1
    )


def dot_nt(a, b):
    return lax.dot_general(a, b, (((1,), (1,)), ((), ())), preferred_element_type=jnp.float32)


def row_facts(block_ref):
    kind = lax.broadcasted_iota(jnp.int32, (8, 128), 0)
    lane = lax.broadcasted_iota(jnp.int32, (8, 128), 1) - 64
    pick = jnp.where((kind == 0) & (lane >= 0) & (lane <= 2), 1.0, 0.0)
    pick = jnp.where((kind == 1) & (lane == 3), 64.0, pick)
    pick = jnp.where((kind == 1) & (lane == 4), 1.0, pick)
    facts = dot_nt(pick.astype(jnp.bfloat16), block_ref[:, 1024:])
    return facts[0:1], facts[1:2]


def score_kernel(place_ref, lat_ref, x0, x1, x2, x3, p_ref, t_ref, stat_ref):
    blocks = (x0, x1, x2, x3)
    core, odd = place_ref[0] // 2, place_ref[0] % 2
    facts = [row_facts(b) for b in blocks]

    def scores(tile, tops):
        rows = pl.ds(pl.multiple_of(tile * TILE, TILE), TILE)
        n = lax.broadcasted_iota(jnp.int32, (TILE, 1), 0)
        key_pos = (
            (n // 32) * 1024 + (tile // 2) * 256 + core * 128 + (tile % 2) * 64
            + ((n // 8) % 4) * 16 + odd * 8 + n % 8
        ).astype(jnp.float32)
        keys = lat_ref[rows, :]
        new = []
        for k, block in enumerate(blocks):
            s = dot_nt(keys, block[:, VALUES:]) * score_scale
            s = jnp.where(key_pos <= facts[k][1], s, masked_score)
            p_ref[rows, k * ROWS:(k + 1) * ROWS] = s
            new.append(jnp.maximum(tops[k], jnp.max(s, axis=0, keepdims=True)))
        return tuple(new)

    tops = lax.fori_loop(
        0, KEYS // TILE, scores, (jnp.full((1, ROWS), least_top, jnp.float32),) * TEAM
    )

    def weigh(tile, sums):
        rows = pl.ds(pl.multiple_of(tile * TILE, TILE), TILE)
        values = lat_ref[rows, :VALUES]
        new = []
        for k, block in enumerate(blocks):
            cols = slice(k * ROWS, (k + 1) * ROWS)
            p = jnp.exp(p_ref[rows, cols] - tops[k])
            pg = dot_nt(values, block[:, :VALUES])
            p_ref[rows, cols] = p
            t_ref[rows, cols] = p * (pg - facts[k][0])
            new.append(sums[k] + jnp.sum(p, axis=0, keepdims=True))
        return tuple(new)

    sums = lax.fori_loop(
        0, KEYS // TILE, weigh, (jnp.zeros((1, ROWS), jnp.float32),) * TEAM
    )
    stat_ref[...] = jnp.concatenate(tops + sums, axis=0)


def grad_kernel(
    place_ref, own_ref, all_ref, lat_ref, x0, x1, x2, x3, p_ref, t_ref,
    key_ref, near_ref, far_ref, ds_ref,
):
    blocks = (x0, x1, x2, x3)
    place = place_ref[0]
    factors = []
    for k in range(TEAM):
        spots = [place ^ other ^ k for other in range(TEAM)]
        tops = [all_ref[o, pl.ds(spots[o], 1), :] for o in range(TEAM)]
        sums = [all_ref[o, pl.ds(TEAM + spots[o], 1), :] for o in range(TEAM)]
        top = jnp.maximum(jnp.maximum(tops[0], tops[1]), jnp.maximum(tops[2], tops[3]))
        total = sum(z * jnp.exp(m - top) for m, z in zip(tops, sums))
        factors.append(jnp.exp(own_ref[k:k + 1, :] - top) / total)

    def keys(tile, _):
        rows = pl.ds(pl.multiple_of(tile * TILE, TILE), TILE)
        low = high = None
        for k, block in enumerate(blocks):
            cols = slice(k * ROWS, (k + 1) * ROWS)
            w = (p_ref[rows, cols] * factors[k]).astype(jnp.bfloat16)
            ds = (t_ref[rows, cols] * (factors[k] * score_scale)).astype(jnp.bfloat16)
            ds_ref[rows, cols] = ds
            part = jnp.dot(
                ds, block[:, VALUES:VALUES + 512], preferred_element_type=jnp.float32
            ) + jnp.dot(w, block[:, :VALUES], preferred_element_type=jnp.float32)
            tail = jnp.dot(ds, block[:, 1024:], preferred_element_type=jnp.float32)
            low = part if low is None else low + part
            high = tail if high is None else high + tail
        key_ref[rows, :512] = low.astype(key_ref.dtype)
        key_ref[rows, 512:] = high.astype(key_ref.dtype)
        return 0

    lax.fori_loop(0, KEYS // TILE, keys, 0)
    for k in range(TEAM):
        out = lax.dot_general(
            ds_ref[:, k * ROWS:(k + 1) * ROWS], lat_ref[...],
            (((0,), (0,)), ((), ())), preferred_element_type=jnp.float32,
        )
        ref = near_ref if k < 2 else far_ref
        ref[(k % 2) * ROWS:(k % 2 + 1) * ROWS, :] = out[:, :576].astype(ref.dtype)


def whole(n):
    return [pl.BlockSpec(memory_space=pltpu.VMEM)] * n


SMEM = pl.BlockSpec(memory_space=pltpu.SMEM)
LIMIT = pltpu.CompilerParams(vmem_limit_bytes=48 * 1024 * 1024)


def swap(block, axis):
    return lax.ppermute(block, axis, [(0, 1), (1, 0)])


def exchange(pieces, axes):
    return lax.all_to_all(pieces, axes, 0, 0, tiled=True)


def per_device(queries, latents, out_grad, layer_out, query_start):
    place = (lax.axis_index("c") * 2 + lax.axis_index("y0")).astype(jnp.int32).reshape(1)
    head = lax.axis_index(("zl", "yh", "y0"))

    piece = lax.dynamic_slice_in_dim(latents, head * 8, 8, 0)
    piece = jnp.pad(piece, ((0, 0), (0, WIDE - 576)))
    tile = exchange(jnp.broadcast_to(piece[None], (16, 8, WIDE)), ("zh", "yh"))
    tile = tile.reshape(TILE, WIDE)
    lat = exchange(jnp.broadcast_to(tile[None], (8, TILE, WIDE)), ("x", "zl"))
    lat = lat.reshape(KEYS, WIDE)

    x0 = pl.pallas_call(
        prep_kernel,
        out_shape=jax.ShapeDtypeStruct((ROWS, PACK), jnp.bfloat16),
        in_specs=[SMEM] + whole(3),
        out_specs=whole(1)[0],
        name="prep",
    )(
        query_start,
        queries.reshape(ROWS, 576),
        out_grad.reshape(ROWS, VALUES),
        layer_out.reshape(ROWS, VALUES),
    )
    x1 = swap(x0, "y0")
    x2 = swap(x0, "c")
    x3 = swap(x1, "c")

    square = jax.ShapeDtypeStruct((KEYS, TEAM * ROWS), jnp.float32)
    p, t, stats = pl.pallas_call(
        score_kernel,
        out_shape=(square, square, jax.ShapeDtypeStruct((2 * TEAM, ROWS), jnp.float32)),
        in_specs=[SMEM] + whole(5),
        out_specs=tuple(whole(3)),
        compiler_params=LIMIT,
        name="scores",
    )(place, lat, x0, x1, x2, x3)
    team_stats = lax.all_gather(stats, ("c", "y0"), axis=0, tiled=False)

    key_part, near, far = pl.pallas_call(
        grad_kernel,
        out_shape=(
            jax.ShapeDtypeStruct((KEYS, WIDE), jnp.bfloat16),
            jax.ShapeDtypeStruct((2 * ROWS, 576), jnp.float32),
            jax.ShapeDtypeStruct((2 * ROWS, 576), jnp.bfloat16),
        ),
        in_specs=[SMEM] + whole(9),
        out_specs=tuple(whole(3)),
        scratch_shapes=[pltpu.VMEM((KEYS, TEAM * ROWS), jnp.bfloat16)],
        compiler_params=LIMIT,
        name="grads",
    )(place, stats, team_stats, lat, x0, x1, x2, x3, p, t)

    parts = exchange(key_part.reshape(8, TILE, WIDE), ("x", "zl"))
    tile_sum = jnp.sum(parts.astype(jnp.float32), axis=0)
    parts = exchange(tile_sum.reshape(16, 8, WIDE), ("zh", "yh"))
    latent_grad = jnp.sum(parts, axis=0)[:, :576]

    both = near + swap(far, "c").astype(jnp.float32)
    query_sum = both[:ROWS] + swap(both[ROWS:].astype(jnp.bfloat16), "y0").astype(jnp.float32)
    query_grad = query_sum.astype(jnp.bfloat16).reshape(queries.shape)
    return (query_grad, latent_grad)


def solution(mesh):
    fine = Mesh(mesh.devices.reshape(4, 4, 2, 2, 4, 2), FINE)
    seq, head = FINE[:3], FINE[3:]
    placed = (
        P(seq, head, None),
        P(seq, None),
        P(seq, head, None),
        P(seq, head, None),
        P(seq),
    )
    return jax.shard_map(
        per_device,
        mesh=fine,
        in_specs=placed,
        out_specs=(P(seq, head, None), P(FINE, None)),
        check_vma=False,
    )
```

time: 741 us -> 140 us (0.19)
  the two profiles are of different devices: /device:TPU:2 before, /device:TPU:56 now
where the time goes in v1:
time: 140 us
  waiting for transfers between devices  38 us (27%)
  blocking collectives  34.6 us (25%)
  starting transfers between devices  31 us (22%)
  Pallas kernels  23.9 us (17%)
  local copies, waits for them, and re-layouts  8.19 us (6%)
  other arithmetic  2.44 us (2%)
  between operations  1.41 us (1%)
    ppermute x5, waiting for transfers between devices, swap(): return lax.ppermute(block, axis, [(0, 1), (1, 0)])  25.9 us
    all_to_all x1, blocking collectives, exchange(): return lax.all_to_all(pieces, axes, 0, 0, tiled=True)  25 us
    all_to_all x3, starting transfers between devices, exchange(): return lax.all_to_all(pieces, axes, 0, 0, tiled=True)  17.7 us
    ppermute x5, starting transfers between devices, swap(): return lax.ppermute(block, axis, [(0, 1), (1, 0)])  13.3 us
    all_to_all x3, waiting for transfers between devices, exchange(): return lax.all_to_all(pieces, axes, 0, 0, tiled=True)  12.1 us
    pallas_call x1, Pallas kernels, per_device(): pl.pallas_call(score_kernel, out_shape=(square, square, jax.ShapeDtypeStr...  11.8 us
    pallas_call x1, Pallas kernels, per_device(): pl.pallas_call(grad_kernel, out_shape=(jax.ShapeDtypeStruct((KEYS, WIDE),...  9.89 us
    all_gather x1, blocking collectives, per_device(): team_stats = lax.all_gather(stats, ('c', 'y0'), axis=0, tiled=False)  9.55 us
  transfers between devices with their start and end apart: 8, of which 5 were waited for; matrix products, arithmetic and copies ran while one was open for 2% of the time, Pallas kernels for 2%

profile of v1, /device:TPU:56, one launch (start us, length us, event | category | flops | bytes accessed | tf_op | source)
XLA Modules:
  0.0 139.6 jit_solution(3962731135409912558)
XLA Ops:
  0.6 0.0 copy-start
  0.7 0.9 copy-done
  1.5 0.1 constant_dynamic-slice_fusion
  1.7 0.1 copy.14
  1.8 25.0 %all_to_all.20 = bf16[16,8,640]{2,1,0:T(8,128)(2,1)S(1)} all-to-all(bf16[16,8,640]{2,1,0:T(8,128)(2,1)S(1)} %broadcast_in_dim.6), channel_id=1, replica_groups=mesh['zh'=4,'x'=4,'c'=2,'zl'=2,'yh'=4,'y0'=2] {'zh','yh'}, dimensions={0} | all-to-all | bytes 327680 | tf_op jit(solution)/shard_map/all_to_all | solution.py:159
  26.8 1.2 broadcast_in_dim.15
  28.0 5.0 %all-to-all-start.1 = ((bf16[8,128,640]{2,1,0:T(8,128)(2,1)}), bf16[8,128,640]{2,1,0:T(8,128)(2,1)S(1)}, u32[]{:S(2)}, u32[]{:S(2)}) async-start(bf16[8,128,640]{2,1,0:T(8,128)(2,1)} %broadcast_in_dim.15), calls=%async_computation.1 | async-start | bytes 2621440 | tf_op jit(solution)/shard_map/all_to_all | solution.py:159
  33.7 2.2 %prep.1.x0 = bf16[256,1152]{1,0:T(8,128)(2,1)} custom-call(s32[1]{0:T(128)S(6)} %copy.15.start_ref, bf16[256,576]{1,0:T(8,128)(2,1)} %bitcast.18, bf16[256,512]{1,0:T(8,128)(2,1)} %bitcast.19, bf16[256,512]{1,0:T(8,128)(2,1)} %bitcast.20), custom_call_target="tpu_custom_call" | custom-call | tf_op jit(solution)/shard_map/prep/pallas_call | solution.py:173
  35.9 4.0 %collective-permute-start = (bf16[256,1152]{1,0:T(8,128)(2,1)}, bf16[256,1152]{1,0:T(8,128)(2,1)S(1)}, u32[]{:S(2)}, u32[]{:S(2)}) collective-permute-start(bf16[256,1152]{1,0:T(8,128)(2,1)} %prep.1.x0), channel_id=1, source_target_pairs={{0,1},{1,0},{2,3},{3,2},{4,5},{5,4},{6,7},{7,6},{8,9},{9,8},{10,11... | collective-permute-start | bytes 1769480 | tf_op jit(solution)/shard_map/ppermute | solution.py:155
  39.9 1.9 %collective-permute-start.1 = (bf16[256,1152]{1,0:T(8,128)(2,1)}, bf16[256,1152]{1,0:T(8,128)(2,1)S(1)}, u32[]{:S(2)}, u32[]{:S(2)}) collective-permute-start(bf16[256,1152]{1,0:T(8,128)(2,1)} %prep.1.x0), channel_id=1, source_target_pairs={{0,16},{16,0},{1,17},{17,1},{2,18},{18,2},{3,19},{19,3},{4,20},{20... | collective-permute-start | bytes 1769480 | tf_op jit(solution)/shard_map/ppermute | solution.py:155
  41.8 10.2 %collective-permute-done.x1 = bf16[256,1152]{1,0:T(8,128)(2,1)S(1)} collective-permute-done((bf16[256,1152]{1,0:T(8,128)(2,1)}, bf16[256,1152]{1,0:T(8,128)(2,1)S(1)}, u32[]{:S(2)}, u32[]{:S(2)}) %collective-permute-start) | collective-permute-done | bytes 589856 | tf_op jit(solution)/shard_map/ppermute | solution.py:155
  52.0 1.9 %collective-permute-start.2 = (bf16[256,1152]{1,0:T(8,128)(2,1)S(1)}, bf16[256,1152]{1,0:T(8,128)(2,1)S(1)}, u32[]{:S(2)}, u32[]{:S(2)}) collective-permute-start(bf16[256,1152]{1,0:T(8,128)(2,1)S(1)} %collective-permute-done.x1), channel_id=1, source_target_pairs={{0,16},{16,0},{1,17},{17,1},{2,18},{18,2},{3,19},{19,3},{4,20},{20... | collective-permute-start | bytes 1769480 | tf_op jit(solution)/shard_map/ppermute | solution.py:155
  54.0 0.0 collective-permute-done.1.x2
  54.0 2.0 %collective-permute-done.2.x3 = bf16[256,1152]{1,0:T(8,128)(2,1)S(1)} collective-permute-done((bf16[256,1152]{1,0:T(8,128)(2,1)S(1)}, bf16[256,1152]{1,0:T(8,128)(2,1)S(1)}, u32[]{:S(2)}, u32[]{:S(2)}) %collective-permute-start.2) | collective-permute-done | bytes 589856 | tf_op jit(solution)/shard_map/ppermute | solution.py:155
  55.9 0.0 all-to-all-done.1
  55.9 0.0 copy-start.1
  55.9 0.0 copy-start.2
  55.9 1.5 %copy-done.2 = bf16[256,1152]{1,0:T(8,128)(2,1)S(1)} copy-done((bf16[256,1152]{1,0:T(8,128)(2,1)S(1)}, bf16[256,1152]{1,0:T(8,128)(2,1)}, u32[]{:S(2)}) %copy-start.2) | copy-done | bytes 589848
  57.4 0.0 copy-start.3
  57.4 11.8 %scores.1 = (f32[1024,1024]{1,0:T(8,128)}, f32[1024,1024]{1,0:T(8,128)}, f32[8,256]{1,0:T(8,128)S(1)}) custom-call(s32[1]{0:T(128)} %bitcast.place_ref, bf16[1024,640]{1,0:T(8,128)(2,1)S(1)} %bitcast.12, bf16[256,1152]{1,0:T(8,128)(2,1)S(1)} %copy-done.2, bf16[256,1152]{1,0:T(8,128)(2,1)S(1)} %collective-permute-done.x1, ...), custom_call_target="tpu_custom_call" | custom-call | tf_op jit(solution)/shard_map/scores/pallas_call | solution.py:190
  69.2 0.0 copy-done.1
  69.2 9.6 %all-gather = f32[32,256]{1,0:T(8,128)S(1)} all-gather(f32[8,256]{1,0:T(8,128)S(1)} %get-tuple-element.8.own_ref), channel_id=2, replica_groups=mesh['zh'=4,'x'=4,'c'=2,'zl'=2,'yh'=4,'y0'=2] {'c','y0'}, dimensions={0}, use_global_device_ids=true | all-gather | bytes 40960 | tf_op jit(solution)/shard_map/all_gather | solution.py:198
  78.8 0.0 copy-done.3
  78.8 9.9 %grads.1 = (bf16[1024,640]{1,0:T(8,128)(2,1)S(1)}, f32[512,576]{1,0:T(8,128)S(1)}, bf16[512,576]{1,0:T(8,128)(2,1)S(1)}) custom-call(s32[1]{0:T(128)} %bitcast.place_ref, f32[8,256]{1,0:T(8,128)S(1)} %get-tuple-element.8.own_ref, f32[4,8,256]{2,1,0:T(8,128)S(1)} %bitcast.15, bf16[1024,640]{1,0:T(8,128)(2,1)} %bitcast.13, bf16[256,1152]{1,0:T(8,128)(2,1)S(1)} %copy-done.3, ...), custom_call_target="tpu_custom_call" | custom-call | tf_op jit(solution)/shard_map/grads/pallas_call | solution.py:200
  88.7 0.0 copy-start.4
  88.7 1.1 copy-done.4
  89.8 0.0 copy-start.5
  89.8 0.9 copy-done.5
  90.6 0.0 copy-start.6
  90.6 5.6 %all-to-all-start.2 = ((bf16[8,128,640]{2,1,0:T(8,128)(2,1)}), bf16[8,128,640]{2,1,0:T(8,128)(2,1)S(1)}, u32[]{:S(2)}, u32[]{:S(2)}) async-start(bf16[8,128,640]{2,1,0:T(8,128)(2,1)} %bitcast.14), calls=%async_computation.2 | async-start | bytes 2621440 | tf_op jit(solution)/shard_map/all_to_all | solution.py:159
  96.2 0.0 copy-done.6
  96.2 1.1 copy.12
  97.2 1.9 %collective-permute-start.3 = (bf16[512,576]{0,1:T(8,128)(2,1)}, bf16[512,576]{0,1:T(8,128)(2,1)}, u32[]{:S(2)}, u32[]{:S(2)}) collective-permute-start(bf16[512,576]{0,1:T(8,128)(2,1)} %copy.12), channel_id=1, source_target_pairs={{0,16},{16,0},{1,17},{17,1},{2,18},{18,2},{3,19},{19,3},{4,20},{20... | collective-permute-start | bytes 1769480 | tf_op jit(solution)/shard_map/ppermute | solution.py:155
  99.2 2.3 %collective-permute-done.3 = bf16[512,576]{0,1:T(8,128)(2,1)} collective-permute-done((bf16[512,576]{0,1:T(8,128)(2,1)}, bf16[512,576]{0,1:T(8,128)(2,1)}, u32[]{:S(2)}, u32[]{:S(2)}) %collective-permute-start.3) | collective-permute-done | bytes 589856 | tf_op jit(solution)/shard_map/ppermute | solution.py:155
  101.5 1.4 copy.13
  102.8 12.1 %all-to-all-done.2 = bf16[8,128,640]{2,1,0:T(8,128)(2,1)S(1)} async-done(((bf16[8,128,640]{2,1,0:T(8,128)(2,1)}), bf16[8,128,640]{2,1,0:T(8,128)(2,1)S(1)}, u32[]{:S(2)}, u32[]{:S(2)}) %all-to-all-start.2) | async-done | bytes 1310752 | tf_op jit(solution)/shard_map/all_to_all | solution.py:159
  115.0 0.9 convert_reduce_fusion
  115.8 7.1 %all-to-all-start.3 = ((f32[16,8,640]{2,1,0:T(8,128)}), f32[16,8,640]{2,1,0:T(8,128)S(1)}, u32[]{:S(2)}, u32[]{:S(2)}) async-start(f32[16,8,640]{2,1,0:T(8,128)} %bitcast.16), calls=%async_computation.3 | async-start | bytes 655360 | tf_op jit(solution)/shard_map/all_to_all | solution.py:159
  123.0 0.1 convert_add_fusion
  123.2 3.6 %collective-permute-start.4 = (bf16[256,576]{1,0:T(8,128)(2,1)S(1)}, bf16[256,576]{1,0:T(8,128)(2,1)S(1)}, u32[]{:S(2)}, u32[]{:S(2)}) collective-permute-start(bf16[256,576]{1,0:T(8,128)(2,1)S(1)} %slice.22), channel_id=1, source_target_pairs={{0,1},{1,0},{2,3},{3,2},{4,5},{5,4},{6,7},{7,6},{8,9},{9,8},{10,11... | collective-permute-start | bytes 884744 | tf_op jit(solution)/shard_map/ppermute | solution.py:155
  126.8 11.4 %collective-permute-done.4 = bf16[256,576]{1,0:T(8,128)(2,1)S(1)} collective-permute-done((bf16[256,576]{1,0:T(8,128)(2,1)S(1)}, bf16[256,576]{1,0:T(8,128)(2,1)S(1)}, u32[]{:S(2)}, u32[]{:S(2)}) %collective-permute-start.4) | collective-permute-done | bytes 294944 | tf_op jit(solution)/shard_map/ppermute | solution.py:155
  138.2 0.8 fusion.1
  139.0 0.0 all-to-all-done.3
  139.0 0.6 reduce_sum.19
  (3 shorter events, 0.1 us)
Async XLA Ops:
  0.6 0.9 copy-start
  28.0 27.9 %all-to-all-start.1 = ((bf16[8,128,640]{2,1,0:T(8,128)(2,1)}), bf16[8,128,640]{2,1,0:T(8,128)(2,1)S(1)}, u32[]{:S(2)}, u32[]{:S(2)}) async-start(bf16[8,128,640]{2,1,0:T(8,128)(2,1)} %broadcast_in_dim.15), calls=%async_computation.1 | async-start | bytes 2621440 | tf_op jit(solution)/shard_map/all_to_all | solution.py:159
  35.9 16.1 %collective-permute-start = (bf16[256,1152]{1,0:T(8,128)(2,1)}, bf16[256,1152]{1,0:T(8,128)(2,1)S(1)}, u32[]{:S(2)}, u32[]{:S(2)}) collective-permute-start(bf16[256,1152]{1,0:T(8,128)(2,1)} %prep.1.x0), channel_id=1, source_target_pairs={{0,1},{1,0},{2,3},{3,2},{4,5},{5,4},{6,7},{7,6},{8,9},{9,8},{10,11... | collective-permute-start | bytes 1769480 | tf_op jit(solution)/shard_map/ppermute | solution.py:155
  39.9 14.1 %collective-permute-start.1 = (bf16[256,1152]{1,0:T(8,128)(2,1)}, bf16[256,1152]{1,0:T(8,128)(2,1)S(1)}, u32[]{:S(2)}, u32[]{:S(2)}) collective-permute-start(bf16[256,1152]{1,0:T(8,128)(2,1)} %prep.1.x0), channel_id=1, source_target_pairs={{0,16},{16,0},{1,17},{17,1},{2,18},{18,2},{3,19},{19,3},{4,20},{20... | collective-permute-start | bytes 1769480 | tf_op jit(solution)/shard_map/ppermute | solution.py:155
  52.0 3.9 %collective-permute-start.2 = (bf16[256,1152]{1,0:T(8,128)(2,1)S(1)}, bf16[256,1152]{1,0:T(8,128)(2,1)S(1)}, u32[]{:S(2)}, u32[]{:S(2)}) collective-permute-start(bf16[256,1152]{1,0:T(8,128)(2,1)S(1)} %collective-permute-done.x1), channel_id=1, source_target_pairs={{0,16},{16,0},{1,17},{17,1},{2,18},{18,2},{3,19},{19,3},{4,20},{20... | collective-permute-start | bytes 1769480 | tf_op jit(solution)/shard_map/ppermute | solution.py:155
  55.9 13.3 %copy-start.1 = (bf16[8,128,640]{2,1,0:T(8,128)(2,1)}, bf16[8,128,640]{2,1,0:T(8,128)(2,1)S(1)}, u32[]{:S(2)}) copy-start(bf16[8,128,640]{2,1,0:T(8,128)(2,1)S(1)} %all-to-all-done.1) | copy-start | bytes 3932164
  55.9 1.5 %copy-start.2 = (bf16[256,1152]{1,0:T(8,128)(2,1)S(1)}, bf16[256,1152]{1,0:T(8,128)(2,1)}, u32[]{:S(2)}) copy-start(bf16[256,1152]{1,0:T(8,128)(2,1)} %prep.1.x0) | copy-start | bytes 1769476
  57.4 21.4 %copy-start.3 = (bf16[256,1152]{1,0:T(8,128)(2,1)S(1)}, bf16[256,1152]{1,0:T(8,128)(2,1)}, u32[]{:S(2)}) copy-start(bf16[256,1152]{1,0:T(8,128)(2,1)} %prep.1.x0) | copy-start | bytes 1769476
  88.7 1.1 copy-start.4
  89.8 0.9 copy-start.5
  90.6 5.6 %copy-start.6 = (bf16[512,576]{1,0:T(8,128)(2,1)S(1)}, bf16[512,576]{1,0:T(8,128)(2,1)}, u32[]{:S(2)}) copy-start(bf16[512,576]{1,0:T(8,128)(2,1)} %copy-done.5) | copy-start | bytes 1769476
  90.6 24.3 %all-to-all-start.2 = ((bf16[8,128,640]{2,1,0:T(8,128)(2,1)}), bf16[8,128,640]{2,1,0:T(8,128)(2,1)S(1)}, u32[]{:S(2)}, u32[]{:S(2)}) async-start(bf16[8,128,640]{2,1,0:T(8,128)(2,1)} %bitcast.14), calls=%async_computation.2 | async-start | bytes 2621440 | tf_op jit(solution)/shard_map/all_to_all | solution.py:159
  97.2 4.2 %collective-permute-start.3 = (bf16[512,576]{0,1:T(8,128)(2,1)}, bf16[512,576]{0,1:T(8,128)(2,1)}, u32[]{:S(2)}, u32[]{:S(2)}) collective-permute-start(bf16[512,576]{0,1:T(8,128)(2,1)} %copy.12), channel_id=1, source_target_pairs={{0,16},{16,0},{1,17},{17,1},{2,18},{18,2},{3,19},{19,3},{4,20},{20... | collective-permute-start | bytes 1769480 | tf_op jit(solution)/shard_map/ppermute | solution.py:155
  115.8 23.1 %all-to-all-start.3 = ((f32[16,8,640]{2,1,0:T(8,128)}), f32[16,8,640]{2,1,0:T(8,128)S(1)}, u32[]{:S(2)}, u32[]{:S(2)}) async-start(f32[16,8,640]{2,1,0:T(8,128)} %bitcast.16), calls=%async_computation.3 | async-start | bytes 655360 | tf_op jit(solution)/shard_map/all_to_all | solution.py:159
  123.2 15.0 %collective-permute-start.4 = (bf16[256,576]{1,0:T(8,128)(2,1)S(1)}, bf16[256,576]{1,0:T(8,128)(2,1)S(1)}, u32[]{:S(2)}, u32[]{:S(2)}) collective-permute-start(bf16[256,576]{1,0:T(8,128)(2,1)S(1)} %slice.22), channel_id=1, source_target_pairs={{0,1},{1,0},{2,3},{3,2},{4,5},{5,4},{6,7},{7,6},{8,9},{9,8},{10,11... | collective-permute-start | bytes 884744 | tf_op jit(solution)/shard_map/ppermute | solution.py:155

commit v2 on v1

v2 whole, which is shorter than its diff:
```python
import jax
import jax.numpy as jnp
from jax import lax
from jax.experimental import pallas as pl
from jax.experimental.pallas import tpu as pltpu
from jax.sharding import Mesh, PartitionSpec as P

score_scale = 192 ** (-0.5)
masked_score = -1e30
least_top = -1e29

ROWS = 256
WIDE = 640
VALUES = 512
PACK = 1152
KEYS = 1024
TILE = 256
PIECE = 64
TEAM = 4

FINE = ("zh", "x", "c", "zl", "yh", "y0")


def prep_kernel(start_ref, q_ref, do_ref, lo_ref, out_ref):
    grad = do_ref[...]
    delta = jnp.sum(
        grad.astype(jnp.float32) * lo_ref[...].astype(jnp.float32), axis=1, keepdims=True
    )
    first = delta.astype(jnp.bfloat16).astype(jnp.float32)
    second = (delta - first).astype(jnp.bfloat16).astype(jnp.float32)
    third = delta - first - second
    pos = start_ref[0] + lax.broadcasted_iota(jnp.int32, (ROWS, 64), 0) // 8
    lane = lax.broadcasted_iota(jnp.int32, (ROWS, 64), 1)
    extra = jnp.where(lane == 0, first, 0.0)
    extra = jnp.where(lane == 1, second, extra)
    extra = jnp.where(lane == 2, third, extra)
    extra = jnp.where(lane == 3, (pos // 64).astype(jnp.float32), extra)
    extra = jnp.where(lane == 4, (pos % 64).astype(jnp.float32), extra)
    out_ref[:, :VALUES] = grad
    out_ref[:, VALUES:VALUES + 512] = q_ref[:, :512]
    out_ref[:, VALUES + 512:] = jnp.concatenate(
        [q_ref[:, 512:576], extra.astype(jnp.bfloat16)], axis=1
    )


def dot_nt(a, b):
    return lax.dot_general(a, b, (((1,), (1,)), ((), ())), preferred_element_type=jnp.float32)


def row_facts(block_ref):
    kind = lax.broadcasted_iota(jnp.int32, (8, 128), 0)
    lane = lax.broadcasted_iota(jnp.int32, (8, 128), 1) - 64
    pick = jnp.where((kind == 0) & (lane >= 0) & (lane <= 2), 1.0, 0.0)
    pick = jnp.where((kind == 1) & (lane == 3), 64.0, pick)
    pick = jnp.where((kind == 1) & (lane == 4), 1.0, pick)
    facts = dot_nt(pick.astype(jnp.bfloat16), block_ref[:, 1024:])
    return facts[0:1], facts[1:2]


def spread_kernel(place_ref, lat_ref, out_ref):
    odd = place_ref[0] % 2 == 1
    rows = lat_ref[...].reshape(8, 2, 8, 576)
    mine = jnp.where(odd, rows[:, 1], rows[:, 0]).reshape(PIECE, 576)
    mine = jnp.concatenate([mine, jnp.zeros((PIECE, 64), jnp.bfloat16)], axis=1)
    for peer in range(16):
        out_ref[peer] = mine


def tile_rows(tile):
    return pl.ds(pl.multiple_of(tile * TILE, TILE), TILE)


def block_cols(k):
    return slice(k * ROWS, (k + 1) * ROWS)


def score_kernel(place_ref, lat_ref, x0, x1, x2, x3, p_ref, stat_ref):
    blocks = (x0, x1, x2, x3)
    core, odd = place_ref[0] // 2, place_ref[0] % 2
    poses = [row_facts(b)[1] for b in blocks]

    def scores(tile, tops):
        rows = tile_rows(tile)
        n = lax.broadcasted_iota(jnp.int32, (TILE, 1), 0)
        key_pos = (
            (n // 64) * 1024 + tile * 256 + core * 128 + ((n // 8) % 8) * 16 + odd * 8 + n % 8
        ).astype(jnp.float32)
        keys = lat_ref[rows, :]
        new = []
        for k, block in enumerate(blocks):
            s = dot_nt(keys, block[:, VALUES:]) * score_scale
            s = jnp.where(key_pos <= poses[k], s, masked_score)
            p_ref[rows, block_cols(k)] = s
            new.append(jnp.maximum(tops[k], jnp.max(s, axis=0, keepdims=True)))
        return tuple(new)

    tops = lax.fori_loop(
        0, KEYS // TILE, scores, (jnp.full((1, ROWS), least_top, jnp.float32),) * TEAM
    )

    def weigh(tile, sums):
        rows = tile_rows(tile)
        new = []
        for k in range(TEAM):
            p = jnp.exp(p_ref[rows, block_cols(k)] - tops[k])
            p_ref[rows, block_cols(k)] = p
            new.append(sums[k] + jnp.sum(p, axis=0, keepdims=True))
        return tuple(new)

    sums = lax.fori_loop(
        0, KEYS // TILE, weigh, (jnp.zeros((1, ROWS), jnp.float32),) * TEAM
    )
    stat_ref[...] = jnp.concatenate(tops + sums, axis=0)


def value_kernel(lat_ref, x0, x1, x2, x3, p_ref, t_ref):
    blocks = (x0, x1, x2, x3)
    deltas = [row_facts(b)[0] for b in blocks]

    def values(tile, _):
        rows = tile_rows(tile)
        held = lat_ref[rows, :VALUES]
        for k, block in enumerate(blocks):
            pg = dot_nt(held, block[:, :VALUES])
            t_ref[rows, block_cols(k)] = p_ref[rows, block_cols(k)] * (pg - deltas[k])
        return 0

    lax.fori_loop(0, KEYS // TILE, values, 0)


def key_kernel(
    place_ref, own_ref, here_ref, there_ref, x0, x1, x2, x3, p_ref, t_ref, key_ref, ds_ref
):
    blocks = (x0, x1, x2, x3)
    core = place_ref[0] // 2
    factors = []
    for k in range(TEAM):
        tops, sums = [], []
        for ref, y in ((here_ref, 0), (there_ref, 1)):
            for c in range(2):
                spot = (2 * c + y) ^ k
                tops.append(ref[core ^ c, spot:spot + 1, :])
                sums.append(ref[core ^ c, TEAM + spot:TEAM + spot + 1, :])
        top = jnp.maximum(jnp.maximum(tops[0], tops[1]), jnp.maximum(tops[2], tops[3]))
        total = sum(z * jnp.exp(m - top) for m, z in zip(tops, sums))
        factors.append(jnp.exp(own_ref[k:k + 1, :] - top) / total)

    def keys(tile, _):
        rows = tile_rows(tile)
        low = high = None
        for k, block in enumerate(blocks):
            cols = block_cols(k)
            w = (p_ref[rows, cols] * factors[k]).astype(jnp.bfloat16)
            ds = (t_ref[rows, cols] * (factors[k] * score_scale)).astype(jnp.bfloat16)
            ds_ref[rows, cols] = ds
            part = jnp.dot(
                ds, block[:, VALUES:VALUES + 512], preferred_element_type=jnp.float32
            ) + jnp.dot(w, block[:, :VALUES], preferred_element_type=jnp.float32)
            tail = jnp.dot(ds, block[:, 1024:], preferred_element_type=jnp.float32)
            low = part if low is None else low + part
            high = tail if high is None else high + tail
        both = jnp.concatenate([low, high], axis=1).astype(key_ref.dtype)
        for zl in range(2):
            for zh in range(4):
                key_ref[2 * tile + zl, 32 * zh:32 * zh + 32, :] = both[
                    64 * zh + 32 * zl:64 * zh + 32 * zl + 32
                ]
        return 0

    lax.fori_loop(0, KEYS // TILE, keys, 0)


def query_kernel(lat_ref, ds_ref, near_ref, far_ref):
    for k in range(TEAM):
        out = lax.dot_general(
            ds_ref[:, block_cols(k)], lat_ref[...],
            (((0,), (0,)), ((), ())), preferred_element_type=jnp.float32,
        )
        ref = near_ref if k < 2 else far_ref
        ref[(k % 2) * ROWS:(k % 2 + 1) * ROWS, :] = out.astype(ref.dtype)


def whole(n):
    return [pl.BlockSpec(memory_space=pltpu.VMEM)] * n


SMEM = pl.BlockSpec(memory_space=pltpu.SMEM)


def swap(block, axis):
    return lax.ppermute(block, axis, [(0, 1), (1, 0)])


def exchange(pieces, axes):
    return lax.all_to_all(pieces, axes, 0, 0, tiled=True)


def call(kernel, out_shape, smem, vmem, name, limit=16):
    single = not isinstance(out_shape, tuple)
    return pl.pallas_call(
        kernel,
        out_shape=out_shape,
        in_specs=[SMEM] * smem + whole(vmem),
        out_specs=whole(1)[0] if single else tuple(whole(len(out_shape))),
        compiler_params=pltpu.CompilerParams(vmem_limit_bytes=limit * 1024 * 1024),
        name=name,
    )


def per_device(queries, latents, out_grad, layer_out, query_start):
    place = (lax.axis_index("c") * 2 + lax.axis_index("y0")).astype(jnp.int32).reshape(1)
    shape = jax.ShapeDtypeStruct

    pieces = call(spread_kernel, shape((16, PIECE, WIDE), jnp.bfloat16), 1, 1, "spread")(
        place, latents
    )
    lat = exchange(pieces, ("x", "zh")).reshape(KEYS, WIDE)

    x0 = call(prep_kernel, shape((ROWS, PACK), jnp.bfloat16), 1, 3, "prep")(
        query_start,
        queries.reshape(ROWS, 576),
        out_grad.reshape(ROWS, VALUES),
        layer_out.reshape(ROWS, VALUES),
    )
    x1 = swap(x0, "y0")
    x2 = swap(x0, "c")
    x3 = swap(x1, "c")
    x = (x0, x1, x2, x3)

    square = shape((KEYS, TEAM * ROWS), jnp.float32)
    p, stats = call(
        score_kernel, (square, shape((2 * TEAM, ROWS), jnp.float32)), 1, 5, "scores"
    )(place, lat, *x)
    here = lax.all_gather(stats, "c", axis=0, tiled=False)
    there = swap(here, "y0")
    t = call(value_kernel, square, 0, 6, "values")(lat, *x, p)

    key_part, ds = call(
        key_kernel,
        (
            shape((8, 128, WIDE), jnp.bfloat16),
            shape((KEYS, TEAM * ROWS), jnp.bfloat16),
        ),
        1, 9, "keys",
    )(place, stats, here, there, *x, p, t)
    parts = exchange(key_part, ("x", "zl"))

    near, far = call(
        query_kernel,
        (shape((2 * ROWS, WIDE), jnp.float32), shape((2 * ROWS, WIDE), jnp.bfloat16)),
        0, 2, "query",
    )(lat, ds)
    both = near + swap(far, "c").astype(jnp.float32)
    from_pair = swap(both[ROWS:].astype(jnp.bfloat16), "y0")
    parts, from_pair = lax.optimization_barrier((parts, from_pair))
    query_sum = both[:ROWS] + from_pair.astype(jnp.float32)
    query_grad = query_sum[:, :576].astype(jnp.bfloat16).reshape(queries.shape)

    tile_sum = jnp.sum(parts.astype(jnp.float32), axis=0)
    parts = exchange(tile_sum.reshape(16, 8, WIDE), ("zh", "yh"))
    latent_grad = jnp.sum(parts, axis=0)[:, :576]
    return (query_grad, latent_grad)


def solution(mesh):
    fine = Mesh(mesh.devices.reshape(4, 4, 2, 2, 4, 2), FINE)
    seq, head = FINE[:3], FINE[3:]
    placed = (
        P(seq, head, None),
        P(seq, None),
        P(seq, head, None),
        P(seq, head, None),
        P(seq),
    )
    return jax.shard_map(
        per_device,
        mesh=fine,
        in_specs=placed,
        out_specs=(P(seq, head, None), P(FINE, None)),
        check_vma=False,
    )
```

time: 140 us -> 118 us (0.84)
  the two profiles are of different devices: /device:TPU:56 before, /device:TPU:2 now
where the time goes in v2:
time: 118 us
  waiting for transfers between devices  49 us (42%)
  starting transfers between devices  44 us (37%)
  Pallas kernels  12.3 us (10%)
  local copies, waits for them, and re-layouts  5.46 us (5%)
  other arithmetic  3.77 us (3%)
  blocking collectives  1.81 us (2%)
  between operations  1.46 us (1%)
    all_to_all x3, starting transfers between devices, exchange(): return lax.all_to_all(pieces, axes, 0, 0, tiled=True)  27.8 us
    all_to_all x3, waiting for transfers between devices, exchange(): return lax.all_to_all(pieces, axes, 0, 0, tiled=True)  25.8 us
    ppermute x6, waiting for transfers between devices, swap(): return lax.ppermute(block, axis, [(0, 1), (1, 0)])  23.2 us
    ppermute x6, starting transfers between devices, swap(): return lax.ppermute(block, axis, [(0, 1), (1, 0)])  16.2 us
    unnamed x19, local copies, waits for them, and re-layouts  5.38 us
    pallas_call x1, Pallas kernels, per_device(): call(key_kernel, (shape((8, 128, WIDE), jnp.bfloat16), shape((KEYS, TEAM...  3.45 us
    pallas_call x1, Pallas kernels, per_device(): call(score_kernel, (square, shape((2 * TEAM, ROWS), jnp.float32)), 1, 5,...  3.35 us
  transfers between devices with their start and end apart: 9, of which 7 were waited for; matrix products, arithmetic and copies ran while one was open for 1% of the time, Pallas kernels for 4%

profile of v2, /device:TPU:2, one launch (start us, length us, event | category | flops | bytes accessed | tf_op | source)
XLA Modules:
  0.0 117.8 jit_solution(6060062601406521515)
XLA Ops:
  0.6 1.1 copy.8.lat_ref
  1.7 1.3 %spread.1 = bf16[16,64,640]{2,1,0:T(8,128)(2,1)} custom-call(s32[1]{0:T(128)} %bitcast.place_ref, bf16[128,576]{1,0:T(8,128)(2,1)S(1)} %copy.8.lat_ref), custom_call_target="tpu_custom_call" | custom-call | tf_op jit(solution)/shard_map/spread/pallas_call | solution.py:214
  3.0 0.0 copy-start.6
  3.0 0.0 copy-start.7
  3.0 0.0 copy-start.8
  3.0 13.4 %all-to-all-start = ((bf16[16,64,640]{2,1,0:T(8,128)(2,1)}), bf16[16,64,640]{2,1,0:T(8,128)(2,1)S(1)}, u32[]{:S(2)}, u32[]{:S(2)}) async-start(bf16[16,64,640]{2,1,0:T(8,128)(2,1)} %spread.1), calls=%async_computation | async-start | bytes 2621440 | tf_op jit(solution)/shard_map/all_to_all | solution.py:195
  17.1 0.0 copy-done.6
  17.1 0.0 copy-done.7
  17.1 0.0 copy-done.8
  17.1 0.3 prep.1.x0
  17.4 3.5 %collective-permute-start = (bf16[256,1152]{1,0:T(8,128)(2,1)S(1)}, bf16[256,1152]{1,0:T(8,128)(2,1)S(1)}, u32[]{:S(2)}, u32[]{:S(2)}) collective-permute-start(bf16[256,1152]{1,0:T(8,128)(2,1)S(1)} %prep.1.x0), channel_id=1, source_target_pairs={{0,1},{1,0},{2,3},{3,2},{4,5},{5,4},{6,7},{7,6},{8,9},{9,8},{10,11... | collective-permute-start | bytes 1769480 | tf_op jit(solution)/shard_map/ppermute | solution.py:191
  20.9 1.9 %collective-permute-start.1 = (bf16[256,1152]{1,0:T(8,128)(2,1)S(1)}, bf16[256,1152]{1,0:T(8,128)(2,1)S(1)}, u32[]{:S(2)}, u32[]{:S(2)}) collective-permute-start(bf16[256,1152]{1,0:T(8,128)(2,1)S(1)} %prep.1.x0), channel_id=1, source_target_pairs={{0,16},{16,0},{1,17},{17,1},{2,18},{18,2},{3,19},{19,3},{4,20},{20... | collective-permute-start | bytes 1769480 | tf_op jit(solution)/shard_map/ppermute | solution.py:191
  22.8 11.0 %collective-permute-done.x1 = bf16[256,1152]{1,0:T(8,128)(2,1)S(1)} collective-permute-done((bf16[256,1152]{1,0:T(8,128)(2,1)S(1)}, bf16[256,1152]{1,0:T(8,128)(2,1)S(1)}, u32[]{:S(2)}, u32[]{:S(2)}) %collective-permute-start) | collective-permute-done | bytes 589856 | tf_op jit(solution)/shard_map/ppermute | solution.py:191
  33.8 1.9 %collective-permute-start.2 = (bf16[256,1152]{1,0:T(8,128)(2,1)S(1)}, bf16[256,1152]{1,0:T(8,128)(2,1)S(1)}, u32[]{:S(2)}, u32[]{:S(2)}) collective-permute-start(bf16[256,1152]{1,0:T(8,128)(2,1)S(1)} %collective-permute-done.x1), channel_id=1, source_target_pairs={{0,16},{16,0},{1,17},{17,1},{2,18},{18,2},{3,19},{19,3},{4,20},{20... | collective-permute-start | bytes 1769480 | tf_op jit(solution)/shard_map/ppermute | solution.py:191
  35.7 0.0 collective-permute-done.1.x2
  35.7 2.0 %collective-permute-done.2.x3 = bf16[256,1152]{1,0:T(8,128)(2,1)S(1)} collective-permute-done((bf16[256,1152]{1,0:T(8,128)(2,1)S(1)}, bf16[256,1152]{1,0:T(8,128)(2,1)S(1)}, u32[]{:S(2)}, u32[]{:S(2)}) %collective-permute-start.2) | collective-permute-done | bytes 589856 | tf_op jit(solution)/shard_map/ppermute | solution.py:191
  37.7 0.0 copy-start
  37.7 0.8 copy-done
  38.5 11.6 %all-to-all-done = bf16[16,64,640]{2,1,0:T(8,128)(2,1)S(1)} async-done(((bf16[16,64,640]{2,1,0:T(8,128)(2,1)}), bf16[16,64,640]{2,1,0:T(8,128)(2,1)S(1)}, u32[]{:S(2)}, u32[]{:S(2)}) %all-to-all-start) | async-done | bytes 1310752 | tf_op jit(solution)/shard_map/all_to_all | solution.py:195
  50.2 0.0 copy-start.1
  50.2 1.1 copy-done.1
  51.2 0.0 copy-start.2
  51.2 3.4 %scores.1 = (f32[1024,1024]{1,0:T(8,128)S(1)}, f32[8,256]{1,0:T(8,128)S(1)}) custom-call(s32[1]{0:T(128)} %bitcast.place_ref, bf16[1024,640]{1,0:T(8,128)(2,1)S(1)} %bitcast.10, bf16[256,1152]{1,0:T(8,128)(2,1)S(1)} %prep.1.x0, bf16[256,1152]{1,0:T(8,128)(2,1)S(1)} %collective-permute-done.x1, bf16[256,1152]{1,0:T(8,128)(2,1)S(1)} %collective-permute-done.1.x2, ...), custom_call_target="tpu_custom_call" | custom-call | tf_op jit(solution)/shard_map/scores/pallas_call | solution.py:231
  54.6 1.8 %all-gather = f32[16,256]{1,0:T(8,128)S(1)} all-gather(f32[8,256]{1,0:T(8,128)S(1)} %get-tuple-element.10.own_ref), channel_id=2, replica_groups=mesh['zh'=4,'x'=4,'c'=2,'zl'=2,'yh'=4,'y0'=2] {'c'}, dimensions={0}, use_global_device_ids=true | all-gather | bytes 24576 | tf_op jit(solution)/shard_map/all_gather | solution.py:234
  56.4 3.5 %collective-permute-start.3 = (f32[2,8,256]{2,1,0:T(8,128)S(1)}, f32[2,8,256]{2,1,0:T(8,128)S(1)}, u32[]{:S(2)}, u32[]{:S(2)}) collective-permute-start(f32[2,8,256]{2,1,0:T(8,128)S(1)} %bitcast.16), channel_id=1, source_target_pairs={{0,1},{1,0},{2,3},{3,2},{4,5},{5,4},{6,7},{7,6},{8,9},{9,8},{10,11... | collective-permute-start | bytes 49160 | tf_op jit(solution)/shard_map/ppermute | solution.py:191
  59.9 0.0 copy-done.2
  59.9 2.1 %values.1.t_ref = f32[1024,1024]{1,0:T(8,128)S(1)} custom-call(bf16[1024,640]{1,0:T(8,128)(2,1)S(1)} %bitcast.11, bf16[256,1152]{1,0:T(8,128)(2,1)S(1)} %prep.1.x0, bf16[256,1152]{1,0:T(8,128)(2,1)S(1)} %collective-permute-done.x1, bf16[256,1152]{1,0:T(8,128)(2,1)S(1)} %collective-permute-done.1.x2, bf16[256,1152]{1,0:T(8,128)(2,1)S(1)} %copy-done.2, ...), custom_call_target="tpu_custom_call" | custom-call | tf_op jit(solution)/shard_map/values/pallas_call | solution.py:236
  62.0 0.1 collective-permute-done.3.there_ref
  62.0 3.5 %keys.1 = (bf16[8,128,640]{2,1,0:T(8,128)(2,1)S(1)}, bf16[1024,1024]{1,0:T(8,128)(2,1)S(1)}) custom-call(s32[1]{0:T(128)} %bitcast.place_ref, f32[8,256]{1,0:T(8,128)S(1)} %get-tuple-element.10.own_ref, f32[2,8,256]{2,1,0:T(8,128)S(1)} %bitcast.17, f32[2,8,256]{2,1,0:T(8,128)S(1)} %collective-permute-done.3.there_ref, bf16[256,1152]{1,0:T(8,128)(2,1)S(1)} %prep.1.x0, ...), custom_call_target="tpu_custom_call" | custom-call | tf_op jit(solution)/shard_map/keys/pallas_call | solution.py:238
  65.5 0.0 copy-start.3
  65.5 1.3 %copy-done.3 = bf16[1024,1024]{1,0:T(8,128)(2,1)} copy-done((bf16[1024,1024]{1,0:T(8,128)(2,1)}, bf16[1024,1024]{1,0:T(8,128)(2,1)S(1)}, u32[]{:S(2)}) %copy-start.3) | copy-done | bytes 2097176
  66.8 0.0 copy-start.5
  66.8 1.1 copy-done.5
  67.9 0.0 copy-start.4
  67.9 7.2 %all-to-all-start.1 = ((bf16[8,128,640]{2,1,0:T(8,128)(2,1)}), bf16[8,128,640]{2,1,0:T(8,128)(2,1)}, u32[]{:S(2)}, u32[]{:S(2)}) async-start(bf16[8,128,640]{2,1,0:T(8,128)(2,1)} %copy-done.5), calls=%async_computation.1 | async-start | bytes 2621440 | tf_op jit(solution)/shard_map/all_to_all | solution.py:195
  75.1 0.0 copy-done.4
  75.1 1.8 %query.1 = (f32[512,640]{1,0:T(8,128)S(1)}, bf16[512,640]{1,0:T(8,128)(2,1)S(1)}) custom-call(bf16[1024,640]{1,0:T(8,128)(2,1)S(1)} %bitcast.12, bf16[1024,1024]{1,0:T(8,128)(2,1)S(1)} %copy-done.4), custom_call_target="tpu_custom_call" | custom-call | tf_op jit(solution)/shard_map/query/pallas_call | solution.py:248
  76.9 1.9 %collective-permute-start.4 = (bf16[512,640]{1,0:T(8,128)(2,1)S(1)}, bf16[512,640]{1,0:T(8,128)(2,1)S(1)}, u32[]{:S(2)}, u32[]{:S(2)}) collective-permute-start(bf16[512,640]{1,0:T(8,128)(2,1)S(1)} %get-tuple-element.14), channel_id=1, source_target_pairs={{0,16},{16,0},{1,17},{17,1},{2,18},{18,2},{3,19},{19,3},{4,20},{20... | collective-permute-start | bytes 1966088 | tf_op jit(solution)/shard_map/ppermute | solution.py:191
  78.9 2.1 %collective-permute-done.4 = bf16[512,640]{1,0:T(8,128)(2,1)S(1)} collective-permute-done((bf16[512,640]{1,0:T(8,128)(2,1)S(1)}, bf16[512,640]{1,0:T(8,128)(2,1)S(1)}, u32[]{:S(2)}, u32[]{:S(2)}) %collective-permute-start.4) | collective-permute-done | bytes 655392 | tf_op jit(solution)/shard_map/ppermute | solution.py:191
  80.9 0.1 convert_add_fusion
  81.1 3.5 %collective-permute-start.5 = (bf16[256,640]{1,0:T(8,128)(2,1)S(1)}, bf16[256,640]{1,0:T(8,128)(2,1)S(1)}, u32[]{:S(2)}, u32[]{:S(2)}) collective-permute-start(bf16[256,640]{1,0:T(8,128)(2,1)S(1)} %slice.30), channel_id=1, source_target_pairs={{0,1},{1,0},{2,3},{3,2},{4,5},{5,4},{6,7},{7,6},{8,9},{9,8},{10,11... | collective-permute-start | bytes 983048 | tf_op jit(solution)/shard_map/ppermute | solution.py:191
  84.6 8.2 %collective-permute-done.5 = bf16[256,640]{1,0:T(8,128)(2,1)S(1)} collective-permute-done((bf16[256,640]{1,0:T(8,128)(2,1)S(1)}, bf16[256,640]{1,0:T(8,128)(2,1)S(1)}, u32[]{:S(2)}, u32[]{:S(2)}) %collective-permute-start.5) | collective-permute-done | bytes 327712 | tf_op jit(solution)/shard_map/ppermute | solution.py:191
  92.7 0.0 all-to-all-done.1
  92.7 2.2 %convert_reduce_fusion = f32[128,640]{1,0:T(8,128)} fusion(bf16[8,128,640]{2,1,0:T(8,128)(2,1)} %all-to-all-done.1), kind=kLoop, calls=%fused_computation | loop fusion | flops 1228800 | bytes 1638400 | tf_op jit(solution)/shard_map/reduce_sum | solution.py:259
  95.0 7.2 %all-to-all-start.2 = ((f32[16,8,640]{2,1,0:T(8,128)}), f32[16,8,640]{2,1,0:T(8,128)S(1)}, u32[]{:S(2)}, u32[]{:S(2)}) async-start(f32[16,8,640]{2,1,0:T(8,128)} %bitcast.7), calls=%async_computation.2 | async-start | bytes 655360 | tf_op jit(solution)/shard_map/all_to_all | solution.py:195
  102.2 0.8 fusion.1
  103.0 14.2 %all-to-all-done.2 = f32[16,8,640]{2,1,0:T(8,128)S(1)} async-done(((f32[16,8,640]{2,1,0:T(8,128)}), f32[16,8,640]{2,1,0:T(8,128)S(1)}, u32[]{:S(2)}, u32[]{:S(2)}) %all-to-all-start.2) | async-done | bytes 327712 | tf_op jit(solution)/shard_map/all_to_all | solution.py:195
  117.2 0.6 reduce_sum.19
  (2 shorter events, 0.1 us)
Async XLA Ops:
  3.0 14.1 %copy-start.6 = (bf16[32,8,576]{2,1,0:T(8,128)(2,1)S(1)}, bf16[32,8,576]{2,1,0:T(8,128)(2,1)}, u32[]{:S(2)}) copy-start(bf16[32,8,576]{2,1,0:T(8,128)(2,1)} %param.5) | copy-start | bytes 884740
  3.0 14.1 %copy-start.7 = (bf16[32,8,512]{2,1,0:T(8,128)(2,1)S(1)}, bf16[32,8,512]{2,1,0:T(8,128)(2,1)}, u32[]{:S(2)}) copy-start(bf16[32,8,512]{2,1,0:T(8,128)(2,1)} %param.7) | copy-start | bytes 786436
  3.0 14.1 %copy-start.8 = (bf16[32,8,512]{2,1,0:T(8,128)(2,1)S(1)}, bf16[32,8,512]{2,1,0:T(8,128)(2,1)}, u32[]{:S(2)}) copy-start(bf16[32,8,512]{2,1,0:T(8,128)(2,1)} %param.8) | copy-start | bytes 786436
  3.0 47.2 %all-to-all-start = ((bf16[16,64,640]{2,1,0:T(8,128)(2,1)}), bf16[16,64,640]{2,1,0:T(8,128)(2,1)S(1)}, u32[]{:S(2)}, u32[]{:S(2)}) async-start(bf16[16,64,640]{2,1,0:T(8,128)(2,1)} %spread.1), calls=%async_computation | async-start | bytes 2621440 | tf_op jit(solution)/shard_map/all_to_all | solution.py:195
  17.4 16.4 %collective-permute-start = (bf16[256,1152]{1,0:T(8,128)(2,1)S(1)}, bf16[256,1152]{1,0:T(8,128)(2,1)S(1)}, u32[]{:S(2)}, u32[]{:S(2)}) collective-permute-start(bf16[256,1152]{1,0:T(8,128)(2,1)S(1)} %prep.1.x0), channel_id=1, source_target_pairs={{0,1},{1,0},{2,3},{3,2},{4,5},{5,4},{6,7},{7,6},{8,9},{9,8},{10,11... | collective-permute-start | bytes 1769480 | tf_op jit(solution)/shard_map/ppermute | solution.py:191
  20.9 14.8 %collective-permute-start.1 = (bf16[256,1152]{1,0:T(8,128)(2,1)S(1)}, bf16[256,1152]{1,0:T(8,128)(2,1)S(1)}, u32[]{:S(2)}, u32[]{:S(2)}) collective-permute-start(bf16[256,1152]{1,0:T(8,128)(2,1)S(1)} %prep.1.x0), channel_id=1, source_target_pairs={{0,16},{16,0},{1,17},{17,1},{2,18},{18,2},{3,19},{19,3},{4,20},{20... | collective-permute-start | bytes 1769480 | tf_op jit(solution)/shard_map/ppermute | solution.py:191
  33.8 3.9 %collective-permute-start.2 = (bf16[256,1152]{1,0:T(8,128)(2,1)S(1)}, bf16[256,1152]{1,0:T(8,128)(2,1)S(1)}, u32[]{:S(2)}, u32[]{:S(2)}) collective-permute-start(bf16[256,1152]{1,0:T(8,128)(2,1)S(1)} %collective-permute-done.x1), channel_id=1, source_target_pairs={{0,16},{16,0},{1,17},{17,1},{2,18},{18,2},{3,19},{19,3},{4,20},{20... | collective-permute-start | bytes 1769480 | tf_op jit(solution)/shard_map/ppermute | solution.py:191
  37.7 0.8 copy-start
  50.2 1.1 copy-start.1
  51.2 8.7 %copy-start.2 = (bf16[256,1152]{1,0:T(8,128)(2,1)S(1)}, bf16[256,1152]{1,0:T(8,128)(2,1)}, u32[]{:S(2)}) copy-start(bf16[256,1152]{1,0:T(8,128)(2,1)} %copy-done) | copy-start | bytes 1769476
  56.4 5.6 %collective-permute-start.3 = (f32[2,8,256]{2,1,0:T(8,128)S(1)}, f32[2,8,256]{2,1,0:T(8,128)S(1)}, u32[]{:S(2)}, u32[]{:S(2)}) collective-permute-start(f32[2,8,256]{2,1,0:T(8,128)S(1)} %bitcast.16), channel_id=1, source_target_pairs={{0,1},{1,0},{2,3},{3,2},{4,5},{5,4},{6,7},{7,6},{8,9},{9,8},{10,11... | collective-permute-start | bytes 49160 | tf_op jit(solution)/shard_map/ppermute | solution.py:191
  65.5 1.3 %copy-start.3 = (bf16[1024,1024]{1,0:T(8,128)(2,1)}, bf16[1024,1024]{1,0:T(8,128)(2,1)S(1)}, u32[]{:S(2)}) copy-start(bf16[1024,1024]{1,0:T(8,128)(2,1)S(1)} %get-tuple-element.12.ds_ref) | copy-start | bytes 6291460
  66.8 1.1 copy-start.5
  67.9 7.2 %copy-start.4 = (bf16[1024,1024]{1,0:T(8,128)(2,1)S(1)}, bf16[1024,1024]{1,0:T(8,128)(2,1)}, u32[]{:S(2)}) copy-start(bf16[1024,1024]{1,0:T(8,128)(2,1)} %copy-done.3) | copy-start | bytes 6291460
  67.9 24.8 %all-to-all-start.1 = ((bf16[8,128,640]{2,1,0:T(8,128)(2,1)}), bf16[8,128,640]{2,1,0:T(8,128)(2,1)}, u32[]{:S(2)}, u32[]{:S(2)}) async-start(bf16[8,128,640]{2,1,0:T(8,128)(2,1)} %copy-done.5), calls=%async_computation.1 | async-start | bytes 2621440 | tf_op jit(solution)/shard_map/all_to_all | solution.py:195
  76.9 4.0 %collective-permute-start.4 = (bf16[512,640]{1,0:T(8,128)(2,1)S(1)}, bf16[512,640]{1,0:T(8,128)(2,1)S(1)}, u32[]{:S(2)}, u32[]{:S(2)}) collective-permute-start(bf16[512,640]{1,0:T(8,128)(2,1)S(1)} %get-tuple-element.14), channel_id=1, source_target_pairs={{0,16},{16,0},{1,17},{17,1},{2,18},{18,2},{3,19},{19,3},{4,20},{20... | collective-permute-start | bytes 1966088 | tf_op jit(solution)/shard_map/ppermute | solution.py:191
  81.1 11.6 %collective-permute-start.5 = (bf16[256,640]{1,0:T(8,128)(2,1)S(1)}, bf16[256,640]{1,0:T(8,128)(2,1)S(1)}, u32[]{:S(2)}, u32[]{:S(2)}) collective-permute-start(bf16[256,640]{1,0:T(8,128)(2,1)S(1)} %slice.30), channel_id=1, source_target_pairs={{0,1},{1,0},{2,3},{3,2},{4,5},{5,4},{6,7},{7,6},{8,9},{9,8},{10,11... | collective-permute-start | bytes 983048 | tf_op jit(solution)/shard_map/ppermute | solution.py:191
  95.0 22.2 %all-to-all-start.2 = ((f32[16,8,640]{2,1,0:T(8,128)}), f32[16,8,640]{2,1,0:T(8,128)S(1)}, u32[]{:S(2)}, u32[]{:S(2)}) async-start(f32[16,8,640]{2,1,0:T(8,128)} %bitcast.7), calls=%async_computation.2 | async-start | bytes 655360 | tf_op jit(solution)/shard_map/all_to_all | solution.py:195

commit v3 on v2

--- a/solution.py
+++ b/solution.py
@@ -16,9 +16,11 @@
 KEYS = 1024
 TILE = 256
 PIECE = 64
+FOLD = 288
 TEAM = 4
 
-FINE = ("zh", "x", "c", "zl", "yh", "y0")
+FINE = ("zh", "x", "c", "zl", "ya", "yb", "y0")
+SIZES = (4, 4, 2, 2, 2, 2, 2)
 
 
 def prep_kernel(start_ref, q_ref, do_ref, lo_ref, out_ref):
@@ -59,11 +61,22 @@
 
 def spread_kernel(place_ref, lat_ref, out_ref):
     odd = place_ref[0] % 2 == 1
-    rows = lat_ref[...].reshape(8, 2, 8, 576)
+    rows = lat_ref[...].T.reshape(8, 2, 8, 576)
     mine = jnp.where(odd, rows[:, 1], rows[:, 0]).reshape(PIECE, 576)
-    mine = jnp.concatenate([mine, jnp.zeros((PIECE, 64), jnp.bfloat16)], axis=1)
+    folded = jnp.concatenate(
+        [mine[:, 128 * j:128 * j + 128] for j in range(4)]
+        + [jnp.concatenate([mine[:32, 512:], mine[32:, 512:]], axis=1)],
+        axis=0,
+    )
     for peer in range(16):
-        out_ref[peer] = mine
+        out_ref[peer] = folded
+
+
+def unfold(piece_ref):
+    parts = [piece_ref[64 * j:64 * j + 64] for j in range(4)]
+    tail = piece_ref[256:288]
+    tail = jnp.concatenate([tail[:, :64], tail[:, 64:]], axis=0)
+    return jnp.concatenate(parts + [tail, jnp.zeros((PIECE, 64), jnp.bfloat16)], axis=1)
 
 
 def tile_rows(tile):
@@ -74,7 +87,7 @@
     return slice(k * ROWS, (k + 1) * ROWS)
 
 
-def score_kernel(place_ref, lat_ref, x0, x1, x2, x3, p_ref, stat_ref):
+def score_kernel(place_ref, piece_ref, x0, x1, x2, x3, p_ref, stat_ref, lat_ref):
     blocks = (x0, x1, x2, x3)
     core, odd = place_ref[0] // 2, place_ref[0] % 2
     poses = [row_facts(b)[1] for b in blocks]
@@ -85,7 +98,8 @@
         key_pos = (
             (n // 64) * 1024 + tile * 256 + core * 128 + ((n // 8) % 8) * 16 + odd * 8 + n % 8
         ).astype(jnp.float32)
-        keys = lat_ref[rows, :]
+        keys = jnp.concatenate([unfold(piece_ref.at[4 * tile + zh]) for zh in range(4)], axis=0)
+        lat_ref[rows, :] = keys
         new = []
         for k, block in enumerate(blocks):
             s = dot_nt(keys, block[:, VALUES:]) * score_scale
@@ -128,22 +142,35 @@
     lax.fori_loop(0, KEYS // TILE, values, 0)
 
 
-def key_kernel(
-    place_ref, own_ref, here_ref, there_ref, x0, x1, x2, x3, p_ref, t_ref, key_ref, ds_ref
-):
-    blocks = (x0, x1, x2, x3)
+def row_factors(place_ref, own_ref, team_ref):
     core = place_ref[0] // 2
     factors = []
     for k in range(TEAM):
         tops, sums = [], []
-        for ref, y in ((here_ref, 0), (there_ref, 1)):
+        for y in range(2):
             for c in range(2):
-                spot = (2 * c + y) ^ k
-                tops.append(ref[core ^ c, spot:spot + 1, :])
-                sums.append(ref[core ^ c, TEAM + spot:TEAM + spot + 1, :])
+                spot = 8 * y + ((2 * c + y) ^ k)
+                tops.append(team_ref[core ^ c, spot:spot + 1, :])
+                sums.append(team_ref[core ^ c, TEAM + spot:TEAM + spot + 1, :])
         top = jnp.maximum(jnp.maximum(tops[0], tops[1]), jnp.maximum(tops[2], tops[3]))
         total = sum(z * jnp.exp(m - top) for m, z in zip(tops, sums))
         factors.append(jnp.exp(own_ref[k:k + 1, :] - top) / total)
+    return factors
+
+
+def key_kernel(
+    place_ref, own_ref, team_ref, x0, x1, x2, x3, p_ref, t_ref, key_ref, ds_ref,
+    held_ref, held_ds, sems,
+):
+    blocks = (x0, x1, x2, x3)
+    factors = row_factors(place_ref, own_ref, team_ref)
+
+    def leave(tile):
+        part, rows = pl.ds(tile * 4, 4), tile_rows(tile)
+        return (
+            pltpu.make_async_copy(held_ref.at[part], key_ref.at[part], sems.at[0, tile]),
+            pltpu.make_async_copy(held_ds.at[rows], ds_ref.at[rows], sems.at[1, tile]),
+        )
 
     def keys(tile, _):
         rows = tile_rows(tile)
@@ -152,22 +179,29 @@
             cols = block_cols(k)
             w = (p_ref[rows, cols] * factors[k]).astype(jnp.bfloat16)
             ds = (t_ref[rows, cols] * (factors[k] * score_scale)).astype(jnp.bfloat16)
-            ds_ref[rows, cols] = ds
+            held_ds[rows, cols] = ds
             part = jnp.dot(
                 ds, block[:, VALUES:VALUES + 512], preferred_element_type=jnp.float32
             ) + jnp.dot(w, block[:, :VALUES], preferred_element_type=jnp.float32)
             tail = jnp.dot(ds, block[:, 1024:], preferred_element_type=jnp.float32)
             low = part if low is None else low + part
             high = tail if high is None else high + tail
-        both = jnp.concatenate([low, high], axis=1).astype(key_ref.dtype)
+        both = jnp.concatenate([low, high], axis=1)
         for zl in range(2):
-            for zh in range(4):
-                key_ref[2 * tile + zl, 32 * zh:32 * zh + 32, :] = both[
-                    64 * zh + 32 * zl:64 * zh + 32 * zl + 32
+            for yb in range(2):
+                firsts = [
+                    64 * zh + 8 * (4 * zl + 2 * ya + yb) for zh in range(4) for ya in range(2)
                 ]
+                piece = jnp.concatenate([both[n:n + 8] for n in firsts], axis=0)
+                held_ref[4 * tile + 2 * zl + yb] = piece.astype(held_ref.dtype)
+        for copy in leave(tile):
+            copy.start()
         return 0
 
     lax.fori_loop(0, KEYS // TILE, keys, 0)
+    for tile in range(KEYS // TILE):
+        for copy in leave(tile):
+            copy.wait()
 
 
 def query_kernel(lat_ref, ds_ref, near_ref, far_ref):
@@ -211,10 +245,10 @@
     place = (lax.axis_index("c") * 2 + lax.axis_index("y0")).astype(jnp.int32).reshape(1)
     shape = jax.ShapeDtypeStruct
 
-    pieces = call(spread_kernel, shape((16, PIECE, WIDE), jnp.bfloat16), 1, 1, "spread")(
-        place, latents
-    )
-    lat = exchange(pieces, ("x", "zh")).reshape(KEYS, WIDE)
+    pieces = call(spread_kernel, shape((16, FOLD, 128), jnp.bfloat16), 1, 1, "spread")(
+        place, latents.T
+    )
+    pieces = exchange(pieces, ("x", "zh"))
 
     x0 = call(prep_kernel, shape((ROWS, PACK), jnp.bfloat16), 1, 3, "prep")(
         query_start,
@@ -228,22 +262,37 @@
     x = (x0, x1, x2, x3)
 
     square = shape((KEYS, TEAM * ROWS), jnp.float32)
-    p, stats = call(
-        score_kernel, (square, shape((2 * TEAM, ROWS), jnp.float32)), 1, 5, "scores"
-    )(place, lat, *x)
-    here = lax.all_gather(stats, "c", axis=0, tiled=False)
-    there = swap(here, "y0")
+    p, stats, lat = call(
+        score_kernel,
+        (
+            square,
+            shape((2 * TEAM, ROWS), jnp.float32),
+            shape((KEYS, WIDE), jnp.bfloat16),
+        ),
+        1, 5, "scores",
+    )(place, pieces, *x)
+    there = swap(stats, "y0")
     t = call(value_kernel, square, 0, 6, "values")(lat, *x, p)
-
-    key_part, ds = call(
+    there, t = lax.optimization_barrier((there, t))
+    team = lax.all_gather(jnp.concatenate([stats, there], axis=0), "c", axis=0, tiled=False)
+
+    key_part, ds = pl.pallas_call(
         key_kernel,
-        (
-            shape((8, 128, WIDE), jnp.bfloat16),
-            shape((KEYS, TEAM * ROWS), jnp.bfloat16),
+        out_shape=(
+            pltpu.HBM((16, PIECE, WIDE), jnp.bfloat16),
+            pltpu.HBM((KEYS, TEAM * ROWS), jnp.bfloat16),
         ),
-        1, 9, "keys",
-    )(place, stats, here, there, *x, p, t)
-    parts = exchange(key_part, ("x", "zl"))
+        in_specs=[SMEM] + whole(8),
+        out_specs=(pl.BlockSpec(memory_space=pltpu.HBM),) * 2,
+        scratch_shapes=[
+            pltpu.VMEM((16, PIECE, WIDE), jnp.bfloat16),
+            pltpu.VMEM((KEYS, TEAM * ROWS), jnp.bfloat16),
+            pltpu.SemaphoreType.DMA((2, KEYS // TILE)),
+        ],
+        compiler_params=pltpu.CompilerParams(vmem_limit_bytes=16 * 1024 * 1024),
+        name="keys",
+    )(place, stats, team, *x, p, t)
+    parts = exchange(key_part, ("x", "zl", "yb"))
 
     near, far = call(
         query_kernel,
@@ -257,13 +306,13 @@
     query_grad = query_sum[:, :576].astype(jnp.bfloat16).reshape(queries.shape)
 
     tile_sum = jnp.sum(parts.astype(jnp.float32), axis=0)
-    parts = exchange(tile_sum.reshape(16, 8, WIDE), ("zh", "yh"))
+    parts = exchange(tile_sum.reshape(8, 8, WIDE), ("zh", "ya"))
     latent_grad = jnp.sum(parts, axis=0)[:, :576]
     return (query_grad, latent_grad)
 
 
 def solution(mesh):
-    fine = Mesh(mesh.devices.reshape(4, 4, 2, 2, 4, 2), FINE)
+    fine = Mesh(mesh.devices.reshape(SIZES), FINE)
     seq, head = FINE[:3], FINE[3:]
     placed = (
         P(seq, head, None),

time: 118 us -> 125 us (1.059)
  waiting for transfers between devices: 49 us -> 58 us
  local copies, waits for them, and re-layouts: 5.46 us -> 2.59 us
  other arithmetic: 3.77 us -> 2.37 us
    ppermute x6, waiting for transfers between devices: 23.2 us -> 36.3 us  [swap(): return lax.ppermute(block, axis, [(0, 1), (1, 0)])]
    all_to_all x3, waiting for transfers between devices: 25.8 us -> 21.7 us  [exchange(): return lax.all_to_all(pieces, axes, 0, 0, tiled=True)]
    unnamed x19 -> x14, local copies, waits for them, and re-layouts: 5.38 us -> 2.51 us
    reduce_sum x1, other arithmetic: 2.24 us -> 0.85 us  [per_device(): tile_sum = jnp.sum(parts.astype(jnp.float32), axis=0)]
  transfers between devices with their start and end apart: 9 -> 9, of which waited for: 7 -> 6; matrix products, arithmetic and copies ran while one was open for 1% -> 1% of each run, Pallas kernels for 4% -> 3%
where the time goes in v3:
time: 125 us; the launch traced here: 124 us
  waiting for transfers between devices  58 us (46%)
  starting transfers between devices  44.3 us (35%)
  Pallas kernels  13.5 us (11%)
  local copies, waits for them, and re-layouts  2.59 us (2%)
  other arithmetic  2.37 us (2%)
  blocking collectives  1.83 us (1%)
  between operations  1.48 us (1%)
    ppermute x6, waiting for transfers between devices, swap(): return lax.ppermute(block, axis, [(0, 1), (1, 0)])  36.3 us
    all_to_all x3, starting transfers between devices, exchange(): return lax.all_to_all(pieces, axes, 0, 0, tiled=True)  28.2 us
    all_to_all x3, waiting for transfers between devices, exchange(): return lax.all_to_all(pieces, axes, 0, 0, tiled=True)  21.7 us
    ppermute x6, starting transfers between devices, swap(): return lax.ppermute(block, axis, [(0, 1), (1, 0)])  16.1 us
    pallas_call x1, Pallas kernels, per_device(): pl.pallas_call(key_kernel, out_shape=(pltpu.HBM((16, PIECE, WIDE), jnp.bf...  4.5 us
    pallas_call x1, Pallas kernels, per_device(): call(score_kernel, (square, shape((2 * TEAM, ROWS), jnp.float32), shape((...  3.41 us
    unnamed x14, local copies, waits for them, and re-layouts  2.51 us
  transfers between devices with their start and end apart: 9, of which 6 were waited for; matrix products, arithmetic and copies ran while one was open for 1% of the time, Pallas kernels for 3%

profile of v3, /device:TPU:2, one launch (start us, length us, event | category | flops | bytes accessed | tf_op | source)
XLA Modules:
  0.0 124.1 jit_solution(1309347216793744722)
XLA Ops:
  0.6 0.0 copy-start.6
  0.6 0.9 copy-done.6
  1.5 1.3 %spread.1 = bf16[16,288,128]{2,1,0:T(8,128)(2,1)} custom-call(s32[1]{0:T(128)} %bitcast.place_ref, bf16[576,128]{1,0:T(8,128)(2,1)S(1)} %bitcast.13), custom_call_target="tpu_custom_call" | custom-call | tf_op jit(solution)/shard_map/spread/pallas_call | solution.py:248
  2.9 0.0 copy-start.3
  2.9 0.0 copy-start.4
  2.9 0.0 copy-start.5
  2.9 13.4 %all-to-all-start = ((bf16[16,288,128]{2,1,0:T(8,128)(2,1)}), bf16[16,288,128]{2,1,0:T(8,128)(2,1)S(1)}, u32[]{:S(2)}, u32[]{:S(2)}) async-start(bf16[16,288,128]{2,1,0:T(8,128)(2,1)} %spread.1), calls=%async_computation | async-start | bytes 2359296 | tf_op jit(solution)/shard_map/all_to_all | solution.py:229
  17.0 0.0 copy-done.3
  17.0 0.0 copy-done.4
  17.0 0.0 copy-done.5
  17.0 0.3 prep.1.x0
  17.3 3.5 %collective-permute-start = (bf16[256,1152]{1,0:T(8,128)(2,1)S(1)}, bf16[256,1152]{1,0:T(8,128)(2,1)S(1)}, u32[]{:S(2)}, u32[]{:S(2)}) collective-permute-start(bf16[256,1152]{1,0:T(8,128)(2,1)S(1)} %prep.1.x0), channel_id=1, source_target_pairs={{0,1},{1,0},{2,3},{3,2},{4,5},{5,4},{6,7},{7,6},{8,9},{9,8},{10,11... | collective-permute-start | bytes 1769480 | tf_op jit(solution)/shard_map/ppermute | solution.py:225
  20.8 1.9 %collective-permute-start.1 = (bf16[256,1152]{1,0:T(8,128)(2,1)S(1)}, bf16[256,1152]{1,0:T(8,128)(2,1)S(1)}, u32[]{:S(2)}, u32[]{:S(2)}) collective-permute-start(bf16[256,1152]{1,0:T(8,128)(2,1)S(1)} %prep.1.x0), channel_id=1, source_target_pairs={{0,16},{16,0},{1,17},{17,1},{2,18},{18,2},{3,19},{19,3},{4,20},{20... | collective-permute-start | bytes 1769480 | tf_op jit(solution)/shard_map/ppermute | solution.py:225
  22.7 11.0 %collective-permute-done.x1 = bf16[256,1152]{1,0:T(8,128)(2,1)S(1)} collective-permute-done((bf16[256,1152]{1,0:T(8,128)(2,1)S(1)}, bf16[256,1152]{1,0:T(8,128)(2,1)S(1)}, u32[]{:S(2)}, u32[]{:S(2)}) %collective-permute-start) | collective-permute-done | bytes 589856 | tf_op jit(solution)/shard_map/ppermute | solution.py:225
  33.7 1.9 %collective-permute-start.2 = (bf16[256,1152]{1,0:T(8,128)(2,1)S(1)}, bf16[256,1152]{1,0:T(8,128)(2,1)S(1)}, u32[]{:S(2)}, u32[]{:S(2)}) collective-permute-start(bf16[256,1152]{1,0:T(8,128)(2,1)S(1)} %collective-permute-done.x1), channel_id=1, source_target_pairs={{0,16},{16,0},{1,17},{17,1},{2,18},{18,2},{3,19},{19,3},{4,20},{20... | collective-permute-start | bytes 1769480 | tf_op jit(solution)/shard_map/ppermute | solution.py:225
  35.6 0.0 collective-permute-done.1.x2
  35.6 2.0 %collective-permute-done.2.x3 = bf16[256,1152]{1,0:T(8,128)(2,1)S(1)} collective-permute-done((bf16[256,1152]{1,0:T(8,128)(2,1)S(1)}, bf16[256,1152]{1,0:T(8,128)(2,1)S(1)}, u32[]{:S(2)}, u32[]{:S(2)}) %collective-permute-start.2) | collective-permute-done | bytes 589856 | tf_op jit(solution)/shard_map/ppermute | solution.py:225
  37.6 9.5 %all-to-all-done.piece_ref = bf16[16,288,128]{2,1,0:T(8,128)(2,1)S(1)} async-done(((bf16[16,288,128]{2,1,0:T(8,128)(2,1)}), bf16[16,288,128]{2,1,0:T(8,128)(2,1)S(1)}, u32[]{:S(2)}, u32[]{:S(2)}) %all-to-all-start) | async-done | bytes 1179680 | tf_op jit(solution)/shard_map/all_to_all | solution.py:229
  47.1 3.4 %scores.1 = (f32[1024,1024]{1,0:T(8,128)S(1)}, f32[8,256]{1,0:T(8,128)S(1)}, bf16[1024,640]{1,0:T(8,128)(2,1)S(1)}) custom-call(s32[1]{0:T(128)} %bitcast.place_ref, bf16[16,288,128]{2,1,0:T(8,128)(2,1)S(1)} %all-to-all-done.piece_ref, bf16[256,1152]{1,0:T(8,128)(2,1)S(1)} %prep.1.x0, bf16[256,1152]{1,0:T(8,128)(2,1)S(1)} %collective-permute-done.x1, ...), custom_call_target="tpu_custom_call" | custom-call | tf_op jit(solution)/shard_map/scores/pallas_call | solution.py:265
  50.5 0.0 copy-start
  50.5 3.5 %collective-permute-start.3 = (f32[8,256]{1,0:T(8,128)S(1)}, f32[8,256]{1,0:T(8,128)S(1)}, u32[]{:S(2)}, u32[]{:S(2)}) collective-permute-start(f32[8,256]{1,0:T(8,128)S(1)} %get-tuple-element.14.own_ref), channel_id=1, source_target_pairs={{0,1},{1,0},{2,3},{3,2},{4,5},{5,4},{6,7},{7,6},{8,9},{9,8},{10,11... | collective-permute-start | bytes 24584 | tf_op jit(solution)/shard_map/ppermute | solution.py:225
  54.0 2.1 %values.1.t_ref = f32[1024,1024]{1,0:T(8,128)S(1)} custom-call(bf16[1024,640]{1,0:T(8,128)(2,1)S(1)} %get-tuple-element.13.lat_ref, bf16[256,1152]{1,0:T(8,128)(2,1)S(1)} %prep.1.x0, bf16[256,1152]{1,0:T(8,128)(2,1)S(1)} %collective-permute-done.x1, bf16[256,1152]{1,0:T(8,128)(2,1)S(1)} %collective-permute-done.1.x2, ...), custom_call_target="tpu_custom_call" | custom-call | tf_op jit(solution)/shard_map/values/pallas_call | solution.py:275
  56.1 0.0 copy-done
  56.1 0.0 collective-permute-done.3
  56.1 1.8 %all-gather = f32[32,256]{1,0:T(8,128)S(1)} all-gather(f32[16,256]{1,0:T(8,128)S(1)} %pad_maximum_fusion), channel_id=2, replica_groups=mesh['zh'=4,'x'=4,'c'=2,'zl'=2,'ya'=2,'yb'=2,'y0'=2] {'c'}, dimensions={0}, use_global_device_ids=true | all-gather | bytes 49152 | tf_op jit(solution)/shard_map/all_gather | solution.py:277
  58.0 4.5 %keys.1 = (bf16[16,64,640]{2,1,0:T(8,128)(2,1)}, bf16[1024,1024]{1,0:T(8,128)(2,1)}) custom-call(s32[1]{0:T(128)} %bitcast.place_ref, f32[8,256]{1,0:T(8,128)S(1)} %get-tuple-element.14.own_ref, f32[2,16,256]{2,1,0:T(8,128)S(1)} %bitcast.14, bf16[256,1152]{1,0:T(8,128)(2,1)S(1)} %prep.1.x0, bf16[256,1152]{1,0:T(8,128)(2,1)S(1)} %collective-permute-done.x1, ...), custom_call_target="tpu_custom_call" | custom-call | tf_op jit(solution)/shard_map/keys/pallas_call | solution.py:279
  62.5 0.0 copy-start.1
  62.5 7.2 %all-to-all-start.1 = ((bf16[16,64,640]{2,1,0:T(8,128)(2,1)}), bf16[16,64,640]{2,1,0:T(8,128)(2,1)S(1)}, u32[]{:S(2)}, u32[]{:S(2)}) async-start(bf16[16,64,640]{2,1,0:T(8,128)(2,1)} %get-tuple-element.21), calls=%async_computation.1 | async-start | bytes 2621440 | tf_op jit(solution)/shard_map/all_to_all | solution.py:229
  69.7 0.0 copy-done.1
  69.7 0.0 copy-start.2
  69.7 1.6 %copy-done.2 = bf16[1024,1024]{1,0:T(8,128)(2,1)S(1)} copy-done((bf16[1024,1024]{1,0:T(8,128)(2,1)S(1)}, bf16[1024,1024]{1,0:T(8,128)(2,1)}, u32[]{:S(2)}) %copy-start.2) | copy-done | bytes 2097176
  71.3 1.9 %query.1 = (f32[512,640]{1,0:T(8,128)S(1)}, bf16[512,640]{1,0:T(8,128)(2,1)S(1)}) custom-call(bf16[1024,640]{1,0:T(8,128)(2,1)S(1)} %copy-done.1, bf16[1024,1024]{1,0:T(8,128)(2,1)S(1)} %copy-done.2), custom_call_target="tpu_custom_call" | custom-call | tf_op jit(solution)/shard_map/query/pallas_call | solution.py:297
  73.2 1.9 %collective-permute-start.4 = (bf16[512,640]{1,0:T(8,128)(2,1)S(1)}, bf16[512,640]{1,0:T(8,128)(2,1)S(1)}, u32[]{:S(2)}, u32[]{:S(2)}) collective-permute-start(bf16[512,640]{1,0:T(8,128)(2,1)S(1)} %get-tuple-element.20), channel_id=1, source_target_pairs={{0,16},{16,0},{1,17},{17,1},{2,18},{18,2},{3,19},{19,3},{4,20},{20... | collective-permute-start | bytes 1966088 | tf_op jit(solution)/shard_map/ppermute | solution.py:225
  75.1 2.1 %collective-permute-done.4 = bf16[512,640]{1,0:T(8,128)(2,1)S(1)} collective-permute-done((bf16[512,640]{1,0:T(8,128)(2,1)S(1)}, bf16[512,640]{1,0:T(8,128)(2,1)S(1)}, u32[]{:S(2)}, u32[]{:S(2)}) %collective-permute-start.4) | collective-permute-done | bytes 655392 | tf_op jit(solution)/shard_map/ppermute | solution.py:225
  77.2 0.1 convert_add_fusion
  77.3 3.4 %collective-permute-start.5 = (bf16[256,640]{1,0:T(8,128)(2,1)S(1)}, bf16[256,640]{1,0:T(8,128)(2,1)S(1)}, u32[]{:S(2)}, u32[]{:S(2)}) collective-permute-start(bf16[256,640]{1,0:T(8,128)(2,1)S(1)} %slice.30), channel_id=1, source_target_pairs={{0,1},{1,0},{2,3},{3,2},{4,5},{5,4},{6,7},{7,6},{8,9},{9,8},{10,11... | collective-permute-start | bytes 983048 | tf_op jit(solution)/shard_map/ppermute | solution.py:225
  80.7 21.3 %collective-permute-done.5 = bf16[256,640]{1,0:T(8,128)(2,1)S(1)} collective-permute-done((bf16[256,640]{1,0:T(8,128)(2,1)S(1)}, bf16[256,640]{1,0:T(8,128)(2,1)S(1)}, u32[]{:S(2)}, u32[]{:S(2)}) %collective-permute-start.5) | collective-permute-done | bytes 327712 | tf_op jit(solution)/shard_map/ppermute | solution.py:225
  102.0 0.0 all-to-all-done.1
  102.0 0.9 convert_reduce_fusion
  102.8 7.5 %all-to-all-start.2 = ((f32[8,8,640]{2,1,0:T(8,128)}), f32[8,8,640]{2,1,0:T(8,128)S(1)}, u32[]{:S(2)}, u32[]{:S(2)}) async-start(f32[8,8,640]{2,1,0:T(8,128)} %bitcast.7), calls=%async_computation.2 | async-start | bytes 327680 | tf_op jit(solution)/shard_map/all_to_all | solution.py:229
  110.4 0.8 fusion.1
  111.2 12.2 %all-to-all-done.2 = f32[8,8,640]{2,1,0:T(8,128)S(1)} async-done(((f32[8,8,640]{2,1,0:T(8,128)}), f32[8,8,640]{2,1,0:T(8,128)S(1)}, u32[]{:S(2)}, u32[]{:S(2)}) %all-to-all-start.2) | async-done | bytes 163872 | tf_op jit(solution)/shard_map/all_to_all | solution.py:229
  123.4 0.6 reduce_sum.19
  (3 shorter events, 0.1 us)
Async XLA Ops:
  0.6 0.9 copy-start.6
  2.9 14.1 %copy-start.3 = (bf16[32,8,576]{2,1,0:T(8,128)(2,1)S(1)}, bf16[32,8,576]{2,1,0:T(8,128)(2,1)}, u32[]{:S(2)}) copy-start(bf16[32,8,576]{2,1,0:T(8,128)(2,1)} %param.5) | copy-start | bytes 884740
  2.9 14.1 %copy-start.4 = (bf16[32,8,512]{2,1,0:T(8,128)(2,1)S(1)}, bf16[32,8,512]{2,1,0:T(8,128)(2,1)}, u32[]{:S(2)}) copy-start(bf16[32,8,512]{2,1,0:T(8,128)(2,1)} %param.7) | copy-start | bytes 786436
  2.9 14.1 %copy-start.5 = (bf16[32,8,512]{2,1,0:T(8,128)(2,1)S(1)}, bf16[32,8,512]{2,1,0:T(8,128)(2,1)}, u32[]{:S(2)}) copy-start(bf16[32,8,512]{2,1,0:T(8,128)(2,1)} %param.8) | copy-start | bytes 786436
  2.9 44.2 %all-to-all-start = ((bf16[16,288,128]{2,1,0:T(8,128)(2,1)}), bf16[16,288,128]{2,1,0:T(8,128)(2,1)S(1)}, u32[]{:S(2)}, u32[]{:S(2)}) async-start(bf16[16,288,128]{2,1,0:T(8,128)(2,1)} %spread.1), calls=%async_computation | async-start | bytes 2359296 | tf_op jit(solution)/shard_map/all_to_all | solution.py:229
  17.3 16.4 %collective-permute-start = (bf16[256,1152]{1,0:T(8,128)(2,1)S(1)}, bf16[256,1152]{1,0:T(8,128)(2,1)S(1)}, u32[]{:S(2)}, u32[]{:S(2)}) collective-permute-start(bf16[256,1152]{1,0:T(8,128)(2,1)S(1)} %prep.1.x0), channel_id=1, source_target_pairs={{0,1},{1,0},{2,3},{3,2},{4,5},{5,4},{6,7},{7,6},{8,9},{9,8},{10,11... | collective-permute-start | bytes 1769480 | tf_op jit(solution)/shard_map/ppermute | solution.py:225
  20.8 14.8 %collective-permute-start.1 = (bf16[256,1152]{1,0:T(8,128)(2,1)S(1)}, bf16[256,1152]{1,0:T(8,128)(2,1)S(1)}, u32[]{:S(2)}, u32[]{:S(2)}) collective-permute-start(bf16[256,1152]{1,0:T(8,128)(2,1)S(1)} %prep.1.x0), channel_id=1, source_target_pairs={{0,16},{16,0},{1,17},{17,1},{2,18},{18,2},{3,19},{19,3},{4,20},{20... | collective-permute-start | bytes 1769480 | tf_op jit(solution)/shard_map/ppermute | solution.py:225
  33.7 3.9 %collective-permute-start.2 = (bf16[256,1152]{1,0:T(8,128)(2,1)S(1)}, bf16[256,1152]{1,0:T(8,128)(2,1)S(1)}, u32[]{:S(2)}, u32[]{:S(2)}) collective-permute-start(bf16[256,1152]{1,0:T(8,128)(2,1)S(1)} %collective-permute-done.x1), channel_id=1, source_target_pairs={{0,16},{16,0},{1,17},{17,1},{2,18},{18,2},{3,19},{19,3},{4,20},{20... | collective-permute-start | bytes 1769480 | tf_op jit(solution)/shard_map/ppermute | solution.py:225
  50.5 5.6 %copy-start = (bf16[1024,640]{1,0:T(8,128)(2,1)}, bf16[1024,640]{1,0:T(8,128)(2,1)S(1)}, u32[]{:S(2)}) copy-start(bf16[1024,640]{1,0:T(8,128)(2,1)S(1)} %get-tuple-element.13.lat_ref) | copy-start | bytes 3932164
  50.5 5.6 %collective-permute-start.3 = (f32[8,256]{1,0:T(8,128)S(1)}, f32[8,256]{1,0:T(8,128)S(1)}, u32[]{:S(2)}, u32[]{:S(2)}) collective-permute-start(f32[8,256]{1,0:T(8,128)S(1)} %get-tuple-element.14.own_ref), channel_id=1, source_target_pairs={{0,1},{1,0},{2,3},{3,2},{4,5},{5,4},{6,7},{7,6},{8,9},{9,8},{10,11... | collective-permute-start | bytes 24584 | tf_op jit(solution)/shard_map/ppermute | solution.py:225
  62.5 7.2 %copy-start.1 = (bf16[1024,640]{1,0:T(8,128)(2,1)S(1)}, bf16[1024,640]{1,0:T(8,128)(2,1)}, u32[]{:S(2)}) copy-start(bf16[1024,640]{1,0:T(8,128)(2,1)} %copy-done) | copy-start | bytes 3932164
  62.5 39.5 %all-to-all-start.1 = ((bf16[16,64,640]{2,1,0:T(8,128)(2,1)}), bf16[16,64,640]{2,1,0:T(8,128)(2,1)S(1)}, u32[]{:S(2)}, u32[]{:S(2)}) async-start(bf16[16,64,640]{2,1,0:T(8,128)(2,1)} %get-tuple-element.21), calls=%async_computation.1 | async-start | bytes 2621440 | tf_op jit(solution)/shard_map/all_to_all | solution.py:229
  69.7 1.6 %copy-start.2 = (bf16[1024,1024]{1,0:T(8,128)(2,1)S(1)}, bf16[1024,1024]{1,0:T(8,128)(2,1)}, u32[]{:S(2)}) copy-start(bf16[1024,1024]{1,0:T(8,128)(2,1)} %get-tuple-element.18.ds_ref) | copy-start | bytes 6291460
  73.2 4.0 %collective-permute-start.4 = (bf16[512,640]{1,0:T(8,128)(2,1)S(1)}, bf16[512,640]{1,0:T(8,128)(2,1)S(1)}, u32[]{:S(2)}, u32[]{:S(2)}) collective-permute-start(bf16[512,640]{1,0:T(8,128)(2,1)S(1)} %get-tuple-element.20), channel_id=1, source_target_pairs={{0,16},{16,0},{1,17},{17,1},{2,18},{18,2},{3,19},{19,3},{4,20},{20... | collective-permute-start | bytes 1966088 | tf_op jit(solution)/shard_map/ppermute | solution.py:225
  77.3 24.7 %collective-permute-start.5 = (bf16[256,640]{1,0:T(8,128)(2,1)S(1)}, bf16[256,640]{1,0:T(8,128)(2,1)S(1)}, u32[]{:S(2)}, u32[]{:S(2)}) collective-permute-start(bf16[256,640]{1,0:T(8,128)(2,1)S(1)} %slice.30), channel_id=1, source_target_pairs={{0,1},{1,0},{2,3},{3,2},{4,5},{5,4},{6,7},{7,6},{8,9},{9,8},{10,11... | collective-permute-start | bytes 983048 | tf_op jit(solution)/shard_map/ppermute | solution.py:225
  102.8 20.6 %all-to-all-start.2 = ((f32[8,8,640]{2,1,0:T(8,128)}), f32[8,8,640]{2,1,0:T(8,128)S(1)}, u32[]{:S(2)}, u32[]{:S(2)}) async-start(f32[8,8,640]{2,1,0:T(8,128)} %bitcast.7), calls=%async_computation.2 | async-start | bytes 327680 | tf_op jit(solution)/shard_map/all_to_all | solution.py:229

commit v4 on v3

--- a/solution.py
+++ b/solution.py
@@ -19,8 +19,8 @@
 FOLD = 288
 TEAM = 4
 
-FINE = ("zh", "x", "c", "zl", "ya", "yb", "y0")
-SIZES = (4, 4, 2, 2, 2, 2, 2)
+FINE = ("zh", "x", "c", "zl", "yh", "y0")
+SIZES = (4, 4, 2, 2, 4, 2)
 
 
 def prep_kernel(start_ref, q_ref, do_ref, lo_ref, out_ref):
@@ -59,15 +59,19 @@
     return facts[0:1], facts[1:2]
 
 
+def fold(rows):
+    return jnp.concatenate(
+        [rows[:, 128 * j:128 * j + 128] for j in range(4)]
+        + [jnp.concatenate([rows[:32, 512:576], rows[32:, 512:576]], axis=1)],
+        axis=0,
+    )
+
+
 def spread_kernel(place_ref, lat_ref, out_ref):
     odd = place_ref[0] % 2 == 1
     rows = lat_ref[...].T.reshape(8, 2, 8, 576)
     mine = jnp.where(odd, rows[:, 1], rows[:, 0]).reshape(PIECE, 576)
-    folded = jnp.concatenate(
-        [mine[:, 128 * j:128 * j + 128] for j in range(4)]
-        + [jnp.concatenate([mine[:32, 512:], mine[32:, 512:]], axis=1)],
-        axis=0,
-    )
+    folded = fold(mine)
     for peer in range(16):
         out_ref[peer] = folded
 
@@ -187,13 +191,9 @@
             low = part if low is None else low + part
             high = tail if high is None else high + tail
         both = jnp.concatenate([low, high], axis=1)
-        for zl in range(2):
-            for yb in range(2):
-                firsts = [
-                    64 * zh + 8 * (4 * zl + 2 * ya + yb) for zh in range(4) for ya in range(2)
-                ]
-                piece = jnp.concatenate([both[n:n + 8] for n in firsts], axis=0)
-                held_ref[4 * tile + 2 * zl + yb] = piece.astype(held_ref.dtype)
+        both = both.astype(held_ref.dtype)
+        for zh in range(4):
+            held_ref[4 * tile + zh] = fold(both[PIECE * zh:PIECE * zh + PIECE])
         for copy in leave(tile):
             copy.start()
         return 0
@@ -212,6 +212,19 @@
         )
         ref = near_ref if k < 2 else far_ref
         ref[(k % 2) * ROWS:(k % 2 + 1) * ROWS, :] = out.astype(ref.dtype)
+
+
+def sum_kernel(part_ref, out_ref):
+    def total(rows):
+        return sum(part_ref[peer, rows].astype(jnp.float32) for peer in range(16))
+
+    for j in range(4):
+        chunk = total(slice(PIECE * j, PIECE * j + PIECE))
+        out_ref[:, 128 * j:128 * j + 128] = chunk.astype(out_ref.dtype)
+    tail = total(slice(4 * PIECE, FOLD))
+    tail = jnp.concatenate([tail[:, :64], tail[:, 64:]], axis=0)
+    tail = jnp.concatenate([tail, jnp.zeros_like(tail)], axis=1)
+    out_ref[:, 512:] = tail.astype(out_ref.dtype)
 
 
 def whole(n):
@@ -279,20 +292,20 @@
     key_part, ds = pl.pallas_call(
         key_kernel,
         out_shape=(
-            pltpu.HBM((16, PIECE, WIDE), jnp.bfloat16),
+            pltpu.HBM((16, FOLD, 128), jnp.bfloat16),
             pltpu.HBM((KEYS, TEAM * ROWS), jnp.bfloat16),
         ),
         in_specs=[SMEM] + whole(8),
         out_specs=(pl.BlockSpec(memory_space=pltpu.HBM),) * 2,
         scratch_shapes=[
-            pltpu.VMEM((16, PIECE, WIDE), jnp.bfloat16),
+            pltpu.VMEM((16, FOLD, 128), jnp.bfloat16),
             pltpu.VMEM((KEYS, TEAM * ROWS), jnp.bfloat16),
             pltpu.SemaphoreType.DMA((2, KEYS // TILE)),
         ],
         compiler_params=pltpu.CompilerParams(vmem_limit_bytes=16 * 1024 * 1024),
         name="keys",
     )(place, stats, team, *x, p, t)
-    parts = exchange(key_part, ("x", "zl", "yb"))
+    parts = exchange(key_part, ("x", "zh"))
 
     near, far = call(
         query_kernel,
@@ -305,9 +318,9 @@
     query_sum = both[:ROWS] + from_pair.astype(jnp.float32)
     query_grad = query_sum[:, :576].astype(jnp.bfloat16).reshape(queries.shape)
 
-    tile_sum = jnp.sum(parts.astype(jnp.float32), axis=0)
-    parts = exchange(tile_sum.reshape(8, 8, WIDE), ("zh", "ya"))
-    latent_grad = jnp.sum(parts, axis=0)[:, :576]
+    tile_sum = call(sum_kernel, shape((PIECE, WIDE), jnp.bfloat16), 0, 1, "sum")(parts)
+    parts = exchange(tile_sum.reshape(8, 8, WIDE), ("zl", "yh"))
+    latent_grad = jnp.sum(parts.astype(jnp.float32), axis=0)[:, :576]
     return (query_grad, latent_grad)
 
 

time: 125 us -> 120 us (0.960)
  the two profiles are of different devices: /device:TPU:2 before, /device:TPU:8 now
where the time goes in v4:
time: 120 us; the launch traced here: 119 us
  starting transfers between devices  50 us (42%)
  waiting for transfers between devices  47 us (39%)
  Pallas kernels  14.6 us (12%)
  local copies, waits for them, and re-layouts  2.59 us (2%)
  blocking collectives  1.82 us (2%)
  other arithmetic  1.51 us (1%)
  between operations  1.48 us (1%)
    all_to_all x3, starting transfers between devices, exchange(): return lax.all_to_all(pieces, axes, 0, 0, tiled=True)  37.1 us
    ppermute x6, waiting for transfers between devices, swap(): return lax.ppermute(block, axis, [(0, 1), (1, 0)])  26.6 us
    all_to_all x3, waiting for transfers between devices, exchange(): return lax.all_to_all(pieces, axes, 0, 0, tiled=True)  20.4 us
    ppermute x6, starting transfers between devices, swap(): return lax.ppermute(block, axis, [(0, 1), (1, 0)])  12.9 us
    pallas_call x1, Pallas kernels, per_device(): pl.pallas_call(key_kernel, out_shape=(pltpu.HBM((16, FOLD, 128), jnp.bflo...  4.83 us
    pallas_call x1, Pallas kernels, per_device(): call(score_kernel, (square, shape((2 * TEAM, ROWS), jnp.float32), shape((...  3.41 us
    unnamed x14, local copies, waits for them, and re-layouts  2.51 us
  transfers between devices with their start and end apart: 9, of which 8 were waited for; matrix products, arithmetic and copies ran while one was open for 1% of the time, Pallas kernels for 4%

profile of v4, /device:TPU:8, one launch (start us, length us, event | category | flops | bytes accessed | tf_op | source)
XLA Modules:
  0.0 119.0 jit_solution(3858335895984246072)
XLA Ops:
  0.6 0.0 copy-start.6
  0.6 0.9 copy-done.6
  1.5 1.3 %spread.1 = bf16[16,288,128]{2,1,0:T(8,128)(2,1)} custom-call(s32[1]{0:T(128)} %bitcast.place_ref, bf16[576,128]{1,0:T(8,128)(2,1)S(1)} %bitcast.13), custom_call_target="tpu_custom_call" | custom-call | tf_op jit(solution)/shard_map/spread/pallas_call | solution.py:261
  2.9 0.0 copy-start.3
  2.9 0.0 copy-start.4
  2.9 0.0 copy-start.5
  2.9 13.0 %all-to-all-start = ((bf16[16,288,128]{2,1,0:T(8,128)(2,1)}), bf16[16,288,128]{2,1,0:T(8,128)(2,1)S(1)}, u32[]{:S(2)}, u32[]{:S(2)}) async-start(bf16[16,288,128]{2,1,0:T(8,128)(2,1)} %spread.1), calls=%async_computation | async-start | bytes 2359296 | tf_op jit(solution)/shard_map/all_to_all | solution.py:242
  16.6 0.0 copy-done.3
  16.6 0.0 copy-done.4
  16.6 0.0 copy-done.5
  16.6 0.3 prep.1.x0
  16.9 2.3 %collective-permute-start = (bf16[256,1152]{1,0:T(8,128)(2,1)S(1)}, bf16[256,1152]{1,0:T(8,128)(2,1)S(1)}, u32[]{:S(2)}, u32[]{:S(2)}) collective-permute-start(bf16[256,1152]{1,0:T(8,128)(2,1)S(1)} %prep.1.x0), channel_id=1, source_target_pairs={{0,1},{1,0},{2,3},{3,2},{4,5},{5,4},{6,7},{7,6},{8,9},{9,8},{10,11... | collective-permute-start | bytes 1769480 | tf_op jit(solution)/shard_map/ppermute | solution.py:238
  19.2 1.9 %collective-permute-start.1 = (bf16[256,1152]{1,0:T(8,128)(2,1)S(1)}, bf16[256,1152]{1,0:T(8,128)(2,1)S(1)}, u32[]{:S(2)}, u32[]{:S(2)}) collective-permute-start(bf16[256,1152]{1,0:T(8,128)(2,1)S(1)} %prep.1.x0), channel_id=1, source_target_pairs={{0,16},{16,0},{1,17},{17,1},{2,18},{18,2},{3,19},{19,3},{4,20},{20... | collective-permute-start | bytes 1769480 | tf_op jit(solution)/shard_map/ppermute | solution.py:238
  21.2 12.4 %collective-permute-done.x1 = bf16[256,1152]{1,0:T(8,128)(2,1)S(1)} collective-permute-done((bf16[256,1152]{1,0:T(8,128)(2,1)S(1)}, bf16[256,1152]{1,0:T(8,128)(2,1)S(1)}, u32[]{:S(2)}, u32[]{:S(2)}) %collective-permute-start) | collective-permute-done | bytes 589856 | tf_op jit(solution)/shard_map/ppermute | solution.py:238
  33.5 1.9 %collective-permute-start.2 = (bf16[256,1152]{1,0:T(8,128)(2,1)S(1)}, bf16[256,1152]{1,0:T(8,128)(2,1)S(1)}, u32[]{:S(2)}, u32[]{:S(2)}) collective-permute-start(bf16[256,1152]{1,0:T(8,128)(2,1)S(1)} %collective-permute-done.x1), channel_id=1, source_target_pairs={{0,16},{16,0},{1,17},{17,1},{2,18},{18,2},{3,19},{19,3},{4,20},{20... | collective-permute-start | bytes 1769480 | tf_op jit(solution)/shard_map/ppermute | solution.py:238
  35.5 0.0 collective-permute-done.1.x2
  35.5 2.0 %collective-permute-done.2.x3 = bf16[256,1152]{1,0:T(8,128)(2,1)S(1)} collective-permute-done((bf16[256,1152]{1,0:T(8,128)(2,1)S(1)}, bf16[256,1152]{1,0:T(8,128)(2,1)S(1)}, u32[]{:S(2)}, u32[]{:S(2)}) %collective-permute-start.2) | collective-permute-done | bytes 589856 | tf_op jit(solution)/shard_map/ppermute | solution.py:238
  37.4 4.7 %all-to-all-done.piece_ref = bf16[16,288,128]{2,1,0:T(8,128)(2,1)S(1)} async-done(((bf16[16,288,128]{2,1,0:T(8,128)(2,1)}), bf16[16,288,128]{2,1,0:T(8,128)(2,1)S(1)}, u32[]{:S(2)}, u32[]{:S(2)}) %all-to-all-start) | async-done | bytes 1179680 | tf_op jit(solution)/shard_map/all_to_all | solution.py:242
  42.1 3.4 %scores.1 = (f32[1024,1024]{1,0:T(8,128)S(1)}, f32[8,256]{1,0:T(8,128)S(1)}, bf16[1024,640]{1,0:T(8,128)(2,1)S(1)}) custom-call(s32[1]{0:T(128)} %bitcast.place_ref, bf16[16,288,128]{2,1,0:T(8,128)(2,1)S(1)} %all-to-all-done.piece_ref, bf16[256,1152]{1,0:T(8,128)(2,1)S(1)} %prep.1.x0, bf16[256,1152]{1,0:T(8,128)(2,1)S(1)} %collective-permute-done.x1, ...), custom_call_target="tpu_custom_call" | custom-call | tf_op jit(solution)/shard_map/scores/pallas_call | solution.py:278
  45.5 0.0 copy-start
  45.5 2.4 %collective-permute-start.3 = (f32[8,256]{1,0:T(8,128)S(1)}, f32[8,256]{1,0:T(8,128)S(1)}, u32[]{:S(2)}, u32[]{:S(2)}) collective-permute-start(f32[8,256]{1,0:T(8,128)S(1)} %get-tuple-element.14.own_ref), channel_id=1, source_target_pairs={{0,1},{1,0},{2,3},{3,2},{4,5},{5,4},{6,7},{7,6},{8,9},{9,8},{10,11... | collective-permute-start | bytes 24584 | tf_op jit(solution)/shard_map/ppermute | solution.py:238
  47.9 2.1 %values.1.t_ref = f32[1024,1024]{1,0:T(8,128)S(1)} custom-call(bf16[1024,640]{1,0:T(8,128)(2,1)S(1)} %get-tuple-element.13.lat_ref, bf16[256,1152]{1,0:T(8,128)(2,1)S(1)} %prep.1.x0, bf16[256,1152]{1,0:T(8,128)(2,1)S(1)} %collective-permute-done.x1, bf16[256,1152]{1,0:T(8,128)(2,1)S(1)} %collective-permute-done.1.x2, ...), custom_call_target="tpu_custom_call" | custom-call | tf_op jit(solution)/shard_map/values/pallas_call | solution.py:288
  50.0 0.0 copy-done
  50.0 1.1 collective-permute-done.3
  51.1 1.8 %all-gather = f32[32,256]{1,0:T(8,128)S(1)} all-gather(f32[16,256]{1,0:T(8,128)S(1)} %pad_maximum_fusion), channel_id=2, replica_groups=mesh['zh'=4,'x'=4,'c'=2,'zl'=2,'yh'=4,'y0'=2] {'c'}, dimensions={0}, use_global_device_ids=true | all-gather | bytes 49152 | tf_op jit(solution)/shard_map/all_gather | solution.py:290
  52.9 4.8 %keys.1 = (bf16[16,288,128]{2,1,0:T(8,128)(2,1)}, bf16[1024,1024]{1,0:T(8,128)(2,1)}) custom-call(s32[1]{0:T(128)} %bitcast.place_ref, f32[8,256]{1,0:T(8,128)S(1)} %get-tuple-element.14.own_ref, f32[2,16,256]{2,1,0:T(8,128)S(1)} %bitcast.14, bf16[256,1152]{1,0:T(8,128)(2,1)S(1)} %prep.1.x0, bf16[256,1152]{1,0:T(8,128)(2,1)S(1)} %collective-permute-done.x1, ...), custom_call_target="tpu_custom_call" | custom-call | tf_op jit(solution)/shard_map/keys/pallas_call | solution.py:292
  57.7 0.0 copy-start.1
  57.7 10.5 %all-to-all-start.1 = ((bf16[16,288,128]{2,1,0:T(8,128)(2,1)}), bf16[16,288,128]{2,1,0:T(8,128)(2,1)S(1)}, u32[]{:S(2)}, u32[]{:S(2)}) async-start(bf16[16,288,128]{2,1,0:T(8,128)(2,1)} %get-tuple-element.21), calls=%async_computation.1 | async-start | bytes 2359296 | tf_op jit(solution)/shard_map/all_to_all | solution.py:242
  68.3 0.0 copy-done.1
  68.3 0.0 copy-start.2
  68.3 1.6 %copy-done.2 = bf16[1024,1024]{1,0:T(8,128)(2,1)S(1)} copy-done((bf16[1024,1024]{1,0:T(8,128)(2,1)S(1)}, bf16[1024,1024]{1,0:T(8,128)(2,1)}, u32[]{:S(2)}) %copy-start.2) | copy-done | bytes 2097176
  69.9 1.9 %query.1 = (f32[512,640]{1,0:T(8,128)S(1)}, bf16[512,640]{1,0:T(8,128)(2,1)S(1)}) custom-call(bf16[1024,640]{1,0:T(8,128)(2,1)S(1)} %copy-done.1, bf16[1024,1024]{1,0:T(8,128)(2,1)S(1)} %copy-done.2), custom_call_target="tpu_custom_call" | custom-call | tf_op jit(solution)/shard_map/query/pallas_call | solution.py:310
  71.8 1.9 %collective-permute-start.4 = (bf16[512,640]{1,0:T(8,128)(2,1)S(1)}, bf16[512,640]{1,0:T(8,128)(2,1)S(1)}, u32[]{:S(2)}, u32[]{:S(2)}) collective-permute-start(bf16[512,640]{1,0:T(8,128)(2,1)S(1)} %get-tuple-element.20), channel_id=1, source_target_pairs={{0,16},{16,0},{1,17},{17,1},{2,18},{18,2},{3,19},{19,3},{4,20},{20... | collective-permute-start | bytes 1966088 | tf_op jit(solution)/shard_map/ppermute | solution.py:238
  73.7 2.1 %collective-permute-done.4 = bf16[512,640]{1,0:T(8,128)(2,1)S(1)} collective-permute-done((bf16[512,640]{1,0:T(8,128)(2,1)S(1)}, bf16[512,640]{1,0:T(8,128)(2,1)S(1)}, u32[]{:S(2)}, u32[]{:S(2)}) %collective-permute-start.4) | collective-permute-done | bytes 655392 | tf_op jit(solution)/shard_map/ppermute | solution.py:238
  75.8 0.1 convert_add_fusion
  75.9 2.5 %collective-permute-start.5 = (bf16[256,640]{1,0:T(8,128)(2,1)S(1)}, bf16[256,640]{1,0:T(8,128)(2,1)S(1)}, u32[]{:S(2)}, u32[]{:S(2)}) collective-permute-start(bf16[256,640]{1,0:T(8,128)(2,1)S(1)} %slice.30), channel_id=1, source_target_pairs={{0,1},{1,0},{2,3},{3,2},{4,5},{5,4},{6,7},{7,6},{8,9},{9,8},{10,11... | collective-permute-start | bytes 983048 | tf_op jit(solution)/shard_map/ppermute | solution.py:238
  78.4 9.1 %collective-permute-done.5 = bf16[256,640]{1,0:T(8,128)(2,1)S(1)} collective-permute-done((bf16[256,640]{1,0:T(8,128)(2,1)S(1)}, bf16[256,640]{1,0:T(8,128)(2,1)S(1)}, u32[]{:S(2)}, u32[]{:S(2)}) %collective-permute-start.5) | collective-permute-done | bytes 327712 | tf_op jit(solution)/shard_map/ppermute | solution.py:238
  87.6 7.4 %all-to-all-done.1.part_ref = bf16[16,288,128]{2,1,0:T(8,128)(2,1)S(1)} async-done(((bf16[16,288,128]{2,1,0:T(8,128)(2,1)}), bf16[16,288,128]{2,1,0:T(8,128)(2,1)S(1)}, u32[]{:S(2)}, u32[]{:S(2)}) %all-to-all-start.1) | async-done | bytes 1179680 | tf_op jit(solution)/shard_map/all_to_all | solution.py:242
  94.9 0.8 sum.1
  95.7 13.6 %all-to-all-start.2 = ((bf16[8,8,640]{2,1,0:T(8,128)(2,1)}), bf16[8,8,640]{2,1,0:T(8,128)(2,1)S(1)}, u32[]{:S(2)}, u32[]{:S(2)}) async-start(bf16[8,8,640]{2,1,0:T(8,128)(2,1)} %bitcast.7), calls=%async_computation.2 | async-start | bytes 163840 | tf_op jit(solution)/shard_map/all_to_all | solution.py:242
  109.3 0.8 fusion.1
  110.1 8.3 %all-to-all-done.2 = bf16[8,8,640]{2,1,0:T(8,128)(2,1)S(1)} async-done(((bf16[8,8,640]{2,1,0:T(8,128)(2,1)}), bf16[8,8,640]{2,1,0:T(8,128)(2,1)S(1)}, u32[]{:S(2)}, u32[]{:S(2)}) %all-to-all-start.2) | async-done | bytes 81952 | tf_op jit(solution)/shard_map/all_to_all | solution.py:242
  118.4 0.6 convert_reduce_fusion
  (3 shorter events, 0.1 us)
Async XLA Ops:
  0.6 0.9 copy-start.6
  2.9 13.7 %copy-start.3 = (bf16[32,8,576]{2,1,0:T(8,128)(2,1)S(1)}, bf16[32,8,576]{2,1,0:T(8,128)(2,1)}, u32[]{:S(2)}) copy-start(bf16[32,8,576]{2,1,0:T(8,128)(2,1)} %param.5) | copy-start | bytes 884740
  2.9 13.7 %copy-start.4 = (bf16[32,8,512]{2,1,0:T(8,128)(2,1)S(1)}, bf16[32,8,512]{2,1,0:T(8,128)(2,1)}, u32[]{:S(2)}) copy-start(bf16[32,8,512]{2,1,0:T(8,128)(2,1)} %param.7) | copy-start | bytes 786436
  2.9 13.7 %copy-start.5 = (bf16[32,8,512]{2,1,0:T(8,128)(2,1)S(1)}, bf16[32,8,512]{2,1,0:T(8,128)(2,1)}, u32[]{:S(2)}) copy-start(bf16[32,8,512]{2,1,0:T(8,128)(2,1)} %param.8) | copy-start | bytes 786436
  2.9 39.2 %all-to-all-start = ((bf16[16,288,128]{2,1,0:T(8,128)(2,1)}), bf16[16,288,128]{2,1,0:T(8,128)(2,1)S(1)}, u32[]{:S(2)}, u32[]{:S(2)}) async-start(bf16[16,288,128]{2,1,0:T(8,128)(2,1)} %spread.1), calls=%async_computation | async-start | bytes 2359296 | tf_op jit(solution)/shard_map/all_to_all | solution.py:242
  16.9 16.7 %collective-permute-start = (bf16[256,1152]{1,0:T(8,128)(2,1)S(1)}, bf16[256,1152]{1,0:T(8,128)(2,1)S(1)}, u32[]{:S(2)}, u32[]{:S(2)}) collective-permute-start(bf16[256,1152]{1,0:T(8,128)(2,1)S(1)} %prep.1.x0), channel_id=1, source_target_pairs={{0,1},{1,0},{2,3},{3,2},{4,5},{5,4},{6,7},{7,6},{8,9},{9,8},{10,11... | collective-permute-start | bytes 1769480 | tf_op jit(solution)/shard_map/ppermute | solution.py:238
  19.2 16.2 %collective-permute-start.1 = (bf16[256,1152]{1,0:T(8,128)(2,1)S(1)}, bf16[256,1152]{1,0:T(8,128)(2,1)S(1)}, u32[]{:S(2)}, u32[]{:S(2)}) collective-permute-start(bf16[256,1152]{1,0:T(8,128)(2,1)S(1)} %prep.1.x0), channel_id=1, source_target_pairs={{0,16},{16,0},{1,17},{17,1},{2,18},{18,2},{3,19},{19,3},{4,20},{20... | collective-permute-start | bytes 1769480 | tf_op jit(solution)/shard_map/ppermute | solution.py:238
  33.5 3.9 %collective-permute-start.2 = (bf16[256,1152]{1,0:T(8,128)(2,1)S(1)}, bf16[256,1152]{1,0:T(8,128)(2,1)S(1)}, u32[]{:S(2)}, u32[]{:S(2)}) collective-permute-start(bf16[256,1152]{1,0:T(8,128)(2,1)S(1)} %collective-permute-done.x1), channel_id=1, source_target_pairs={{0,16},{16,0},{1,17},{17,1},{2,18},{18,2},{3,19},{19,3},{4,20},{20... | collective-permute-start | bytes 1769480 | tf_op jit(solution)/shard_map/ppermute | solution.py:238
  45.5 4.5 %copy-start = (bf16[1024,640]{1,0:T(8,128)(2,1)}, bf16[1024,640]{1,0:T(8,128)(2,1)S(1)}, u32[]{:S(2)}) copy-start(bf16[1024,640]{1,0:T(8,128)(2,1)S(1)} %get-tuple-element.13.lat_ref) | copy-start | bytes 3932164
  45.5 5.5 %collective-permute-start.3 = (f32[8,256]{1,0:T(8,128)S(1)}, f32[8,256]{1,0:T(8,128)S(1)}, u32[]{:S(2)}, u32[]{:S(2)}) collective-permute-start(f32[8,256]{1,0:T(8,128)S(1)} %get-tuple-element.14.own_ref), channel_id=1, source_target_pairs={{0,1},{1,0},{2,3},{3,2},{4,5},{5,4},{6,7},{7,6},{8,9},{9,8},{10,11... | collective-permute-start | bytes 24584 | tf_op jit(solution)/shard_map/ppermute | solution.py:238
  57.7 10.6 %copy-start.1 = (bf16[1024,640]{1,0:T(8,128)(2,1)S(1)}, bf16[1024,640]{1,0:T(8,128)(2,1)}, u32[]{:S(2)}) copy-start(bf16[1024,640]{1,0:T(8,128)(2,1)} %copy-done) | copy-start | bytes 3932164
  57.7 37.2 %all-to-all-start.1 = ((bf16[16,288,128]{2,1,0:T(8,128)(2,1)}), bf16[16,288,128]{2,1,0:T(8,128)(2,1)S(1)}, u32[]{:S(2)}, u32[]{:S(2)}) async-start(bf16[16,288,128]{2,1,0:T(8,128)(2,1)} %get-tuple-element.21), calls=%async_computation.1 | async-start | bytes 2359296 | tf_op jit(solution)/shard_map/all_to_all | solution.py:242
  68.3 1.6 %copy-start.2 = (bf16[1024,1024]{1,0:T(8,128)(2,1)S(1)}, bf16[1024,1024]{1,0:T(8,128)(2,1)}, u32[]{:S(2)}) copy-start(bf16[1024,1024]{1,0:T(8,128)(2,1)} %get-tuple-element.18.ds_ref) | copy-start | bytes 6291460
  71.8 4.0 %collective-permute-start.4 = (bf16[512,640]{1,0:T(8,128)(2,1)S(1)}, bf16[512,640]{1,0:T(8,128)(2,1)S(1)}, u32[]{:S(2)}, u32[]{:S(2)}) collective-permute-start(bf16[512,640]{1,0:T(8,128)(2,1)S(1)} %get-tuple-element.20), channel_id=1, source_target_pairs={{0,16},{16,0},{1,17},{17,1},{2,18},{18,2},{3,19},{19,3},{4,20},{20... | collective-permute-start | bytes 1966088 | tf_op jit(solution)/shard_map/ppermute | solution.py:238
  75.9 11.6 %collective-permute-start.5 = (bf16[256,640]{1,0:T(8,128)(2,1)S(1)}, bf16[256,640]{1,0:T(8,128)(2,1)S(1)}, u32[]{:S(2)}, u32[]{:S(2)}) collective-permute-start(bf16[256,640]{1,0:T(8,128)(2,1)S(1)} %slice.30), channel_id=1, source_target_pairs={{0,1},{1,0},{2,3},{3,2},{4,5},{5,4},{6,7},{7,6},{8,9},{9,8},{10,11... | collective-permute-start | bytes 983048 | tf_op jit(solution)/shard_map/ppermute | solution.py:238
  95.7 22.7 %all-to-all-start.2 = ((bf16[8,8,640]{2,1,0:T(8,128)(2,1)}), bf16[8,8,640]{2,1,0:T(8,128)(2,1)S(1)}, u32[]{:S(2)}, u32[]{:S(2)}) async-start(bf16[8,8,640]{2,1,0:T(8,128)(2,1)} %bitcast.7), calls=%async_computation.2 | async-start | bytes 163840 | tf_op jit(solution)/shard_map/all_to_all | solution.py:242

commit v5 on v4

--- a/solution.py
+++ b/solution.py
@@ -59,19 +59,15 @@
     return facts[0:1], facts[1:2]
 
 
-def fold(rows):
-    return jnp.concatenate(
-        [rows[:, 128 * j:128 * j + 128] for j in range(4)]
-        + [jnp.concatenate([rows[:32, 512:576], rows[32:, 512:576]], axis=1)],
-        axis=0,
-    )
-
-
 def spread_kernel(place_ref, lat_ref, out_ref):
     odd = place_ref[0] % 2 == 1
     rows = lat_ref[...].T.reshape(8, 2, 8, 576)
     mine = jnp.where(odd, rows[:, 1], rows[:, 0]).reshape(PIECE, 576)
-    folded = fold(mine)
+    folded = jnp.concatenate(
+        [mine[:, 128 * j:128 * j + 128] for j in range(4)]
+        + [jnp.concatenate([mine[:32, 512:], mine[32:, 512:]], axis=1)],
+        axis=0,
+    )
     for peer in range(16):
         out_ref[peer] = folded
 
@@ -170,7 +166,7 @@
     factors = row_factors(place_ref, own_ref, team_ref)
 
     def leave(tile):
-        part, rows = pl.ds(tile * 4, 4), tile_rows(tile)
+        part, rows = pl.ds(tile * 2, 2), tile_rows(tile)
         return (
             pltpu.make_async_copy(held_ref.at[part], key_ref.at[part], sems.at[0, tile]),
             pltpu.make_async_copy(held_ds.at[rows], ds_ref.at[rows], sems.at[1, tile]),
@@ -191,9 +187,15 @@
             low = part if low is None else low + part
             high = tail if high is None else high + tail
         both = jnp.concatenate([low, high], axis=1)
-        both = both.astype(held_ref.dtype)
-        for zh in range(4):
-            held_ref[4 * tile + zh] = fold(both[PIECE * zh:PIECE * zh + PIECE])
+        for zl in range(2):
+            part = jnp.concatenate(
+                [both[n:n + 32] for n in range(32 * zl, TILE, 64)], axis=0
+            ).astype(held_ref.dtype)
+            for j in range(4):
+                held_ref[2 * tile + zl, 128 * j:128 * j + 128] = part[:, 128 * j:128 * j + 128]
+            held_ref[2 * tile + zl, 512:] = jnp.concatenate(
+                [part[:64, 512:576], part[64:, 512:576]], axis=1
+            )
         for copy in leave(tile):
             copy.start()
         return 0
@@ -204,10 +206,16 @@
             copy.wait()
 
 
-def query_kernel(lat_ref, ds_ref, near_ref, far_ref):
+def query_kernel(lat_ref, ds_ref, near_ref, far_ref, held_ref, sems):
+    def bring(k):
+        return pltpu.make_async_copy(ds_ref.at[:, block_cols(k)], held_ref.at[k], sems.at[k])
+
     for k in range(TEAM):
+        bring(k).start()
+    for k in (2, 3, 0, 1):
+        bring(k).wait()
         out = lax.dot_general(
-            ds_ref[:, block_cols(k)], lat_ref[...],
+            held_ref[k], lat_ref[...],
             (((0,), (0,)), ((), ())), preferred_element_type=jnp.float32,
         )
         ref = near_ref if k < 2 else far_ref
@@ -216,12 +224,12 @@
 
 def sum_kernel(part_ref, out_ref):
     def total(rows):
-        return sum(part_ref[peer, rows].astype(jnp.float32) for peer in range(16))
+        return sum(part_ref[peer, rows].astype(jnp.float32) for peer in range(8))
 
     for j in range(4):
-        chunk = total(slice(PIECE * j, PIECE * j + PIECE))
+        chunk = total(slice(128 * j, 128 * j + 128))
         out_ref[:, 128 * j:128 * j + 128] = chunk.astype(out_ref.dtype)
-    tail = total(slice(4 * PIECE, FOLD))
+    tail = total(slice(512, 576))
     tail = jnp.concatenate([tail[:, :64], tail[:, 64:]], axis=0)
     tail = jnp.concatenate([tail, jnp.zeros_like(tail)], axis=1)
     out_ref[:, 512:] = tail.astype(out_ref.dtype)
@@ -292,34 +300,45 @@
     key_part, ds = pl.pallas_call(
         key_kernel,
         out_shape=(
-            pltpu.HBM((16, FOLD, 128), jnp.bfloat16),
+            pltpu.HBM((8, 576, 128), jnp.bfloat16),
             pltpu.HBM((KEYS, TEAM * ROWS), jnp.bfloat16),
         ),
         in_specs=[SMEM] + whole(8),
         out_specs=(pl.BlockSpec(memory_space=pltpu.HBM),) * 2,
         scratch_shapes=[
-            pltpu.VMEM((16, FOLD, 128), jnp.bfloat16),
+            pltpu.VMEM((8, 576, 128), jnp.bfloat16),
             pltpu.VMEM((KEYS, TEAM * ROWS), jnp.bfloat16),
             pltpu.SemaphoreType.DMA((2, KEYS // TILE)),
         ],
         compiler_params=pltpu.CompilerParams(vmem_limit_bytes=16 * 1024 * 1024),
         name="keys",
     )(place, stats, team, *x, p, t)
-    parts = exchange(key_part, ("x", "zh"))
-
-    near, far = call(
+    parts = exchange(key_part, ("x", "zl"))
+
+    near, far = pl.pallas_call(
         query_kernel,
-        (shape((2 * ROWS, WIDE), jnp.float32), shape((2 * ROWS, WIDE), jnp.bfloat16)),
-        0, 2, "query",
-    )(lat, ds)
+        out_shape=(
+            shape((2 * ROWS, WIDE), jnp.float32),
+            shape((2 * ROWS, WIDE), jnp.bfloat16),
+        ),
+        in_specs=whole(1) + [pl.BlockSpec(memory_space=pltpu.HBM)],
+        out_specs=tuple(whole(2)),
+        scratch_shapes=[
+            pltpu.VMEM((TEAM, KEYS, ROWS), jnp.bfloat16),
+            pltpu.SemaphoreType.DMA((TEAM,)),
+        ],
+        compiler_params=pltpu.CompilerParams(vmem_limit_bytes=16 * 1024 * 1024),
+        name="query",
+    )(lat, pltpu.with_memory_space_constraint(ds, pltpu.HBM))
     both = near + swap(far, "c").astype(jnp.float32)
-    from_pair = swap(both[ROWS:].astype(jnp.bfloat16), "y0")
-    parts, from_pair = lax.optimization_barrier((parts, from_pair))
+    for_pair = both[ROWS:].astype(jnp.bfloat16)
+    parts, for_pair = lax.optimization_barrier((parts, for_pair))
+    from_pair = swap(for_pair, "y0")
     query_sum = both[:ROWS] + from_pair.astype(jnp.float32)
     query_grad = query_sum[:, :576].astype(jnp.bfloat16).reshape(queries.shape)
 
-    tile_sum = call(sum_kernel, shape((PIECE, WIDE), jnp.bfloat16), 0, 1, "sum")(parts)
-    parts = exchange(tile_sum.reshape(8, 8, WIDE), ("zl", "yh"))
+    tile_sum = call(sum_kernel, shape((128, WIDE), jnp.bfloat16), 0, 1, "sum")(parts)
+    parts = exchange(tile_sum.reshape(16, 8, WIDE), ("zh", "yh"))
     latent_grad = jnp.sum(parts.astype(jnp.float32), axis=0)[:, :576]
     return (query_grad, latent_grad)
 

time: 120 us -> 108 us (0.900)
  waiting for transfers between devices: 47 us -> 41 us
  starting transfers between devices: 50 us -> 44.2 us
  Pallas kernels: 14.6 us -> 16.7 us
  local copies, waits for them, and re-layouts: 2.59 us -> 1 us
    ppermute x6, waiting for transfers between devices: 26.6 us -> 17.5 us  [swap(): return lax.ppermute(block, axis, [(0, 1), (1, 0)])]
    all_to_all x3, starting transfers between devices: 37.1 us -> 30.5 us  [exchange(): return lax.all_to_all(pieces, axes, 0, 0, tiled=True)]
    all_to_all x3, waiting for transfers between devices: 20.4 us -> 23.5 us  [exchange(): return lax.all_to_all(pieces, axes, 0, 0, tiled=True)]
    pallas_call x3, Pallas kernels: 7.5 us -> 9.51 us  [the longest x1 4.84 us: per_device(): pl.pallas_call(key_kernel, out_shape=(pltpu.HBM((8, 576, 128), jnp.bfloat...]
    unnamed x14 -> x12, local copies, waits for them, and re-layouts: 2.51 us -> 0.92 us
  transfers between devices with their start and end apart: 9 -> 9, of which waited for: 8 -> 7; matrix products, arithmetic and copies ran while one was open for 1% -> 1% of each run, Pallas kernels for 4% -> 6%
where the time goes in v5:
time: 108 us
  starting transfers between devices  44.2 us (41%)
  waiting for transfers between devices  41 us (38%)
  Pallas kernels  16.7 us (15%)
  blocking collectives  1.82 us (2%)
  other arithmetic  1.53 us (1%)
  between operations  1.47 us (1%)
    all_to_all x3, starting transfers between devices, exchange(): return lax.all_to_all(pieces, axes, 0, 0, tiled=True)  30.5 us
    all_to_all x3, waiting for transfers between devices, exchange(): return lax.all_to_all(pieces, axes, 0, 0, tiled=True)  23.5 us
    ppermute x6, waiting for transfers between devices, swap(): return lax.ppermute(block, axis, [(0, 1), (1, 0)])  17.5 us
    ppermute x6, starting transfers between devices, swap(): return lax.ppermute(block, axis, [(0, 1), (1, 0)])  13.7 us
    pallas_call x1, Pallas kernels, per_device(): pl.pallas_call(key_kernel, out_shape=(pltpu.HBM((8, 576, 128), jnp.bfloat...  4.84 us
    pallas_call x1, Pallas kernels, per_device(): pl.pallas_call(query_kernel, out_shape=(shape((2 * ROWS, WIDE), jnp.float...  3.84 us
    pallas_call x1, Pallas kernels, per_device(): call(score_kernel, (square, shape((2 * TEAM, ROWS), jnp.float32), shape((...  3.42 us
  transfers between devices with their start and end apart: 9, of which 7 were waited for; matrix products, arithmetic and copies ran while one was open for 1% of the time, Pallas kernels for 6%

profile of v5, /device:TPU:8, one launch (start us, length us, event | category | flops | bytes accessed | tf_op | source)
XLA Modules:
  0.0 107.7 jit_solution(16982358102735450690)
XLA Ops:
  0.6 0.0 copy-start.5
  0.6 0.9 copy-done.5
  1.5 1.3 %spread.1 = bf16[16,288,128]{2,1,0:T(8,128)(2,1)} custom-call(s32[1]{0:T(128)} %bitcast.place_ref, bf16[576,128]{1,0:T(8,128)(2,1)S(1)} %bitcast.13), custom_call_target="tpu_custom_call" | custom-call | tf_op jit(solution)/shard_map/spread/pallas_call | solution.py:269
  2.9 0.0 copy-start.2
  2.9 0.0 copy-start.3
  2.9 0.0 copy-start.4
  2.9 13.0 %all-to-all-start = ((bf16[16,288,128]{2,1,0:T(8,128)(2,1)}), bf16[16,288,128]{2,1,0:T(8,128)(2,1)S(1)}, u32[]{:S(2)}, u32[]{:S(2)}) async-start(bf16[16,288,128]{2,1,0:T(8,128)(2,1)} %spread.1), calls=%async_computation | async-start | bytes 2359296 | tf_op jit(solution)/shard_map/all_to_all | solution.py:250
  16.6 0.0 copy-done.2
  16.6 0.0 copy-done.3
  16.6 0.0 copy-done.4
  16.6 0.3 prep.1.x0
  16.9 2.3 %collective-permute-start = (bf16[256,1152]{1,0:T(8,128)(2,1)S(1)}, bf16[256,1152]{1,0:T(8,128)(2,1)S(1)}, u32[]{:S(2)}, u32[]{:S(2)}) collective-permute-start(bf16[256,1152]{1,0:T(8,128)(2,1)S(1)} %prep.1.x0), channel_id=1, source_target_pairs={{0,1},{1,0},{2,3},{3,2},{4,5},{5,4},{6,7},{7,6},{8,9},{9,8},{10,11... | collective-permute-start | bytes 1769480 | tf_op jit(solution)/shard_map/ppermute | solution.py:246
  19.2 1.9 %collective-permute-start.1 = (bf16[256,1152]{1,0:T(8,128)(2,1)S(1)}, bf16[256,1152]{1,0:T(8,128)(2,1)S(1)}, u32[]{:S(2)}, u32[]{:S(2)}) collective-permute-start(bf16[256,1152]{1,0:T(8,128)(2,1)S(1)} %prep.1.x0), channel_id=1, source_target_pairs={{0,16},{16,0},{1,17},{17,1},{2,18},{18,2},{3,19},{19,3},{4,20},{20... | collective-permute-start | bytes 1769480 | tf_op jit(solution)/shard_map/ppermute | solution.py:246
  21.2 12.4 %collective-permute-done.x1 = bf16[256,1152]{1,0:T(8,128)(2,1)S(1)} collective-permute-done((bf16[256,1152]{1,0:T(8,128)(2,1)S(1)}, bf16[256,1152]{1,0:T(8,128)(2,1)S(1)}, u32[]{:S(2)}, u32[]{:S(2)}) %collective-permute-start) | collective-permute-done | bytes 589856 | tf_op jit(solution)/shard_map/ppermute | solution.py:246
  33.6 1.9 %collective-permute-start.2 = (bf16[256,1152]{1,0:T(8,128)(2,1)S(1)}, bf16[256,1152]{1,0:T(8,128)(2,1)S(1)}, u32[]{:S(2)}, u32[]{:S(2)}) collective-permute-start(bf16[256,1152]{1,0:T(8,128)(2,1)S(1)} %collective-permute-done.x1), channel_id=1, source_target_pairs={{0,16},{16,0},{1,17},{17,1},{2,18},{18,2},{3,19},{19,3},{4,20},{20... | collective-permute-start | bytes 1769480 | tf_op jit(solution)/shard_map/ppermute | solution.py:246
  35.5 0.0 collective-permute-done.1.x2
  35.5 2.0 %collective-permute-done.2.x3 = bf16[256,1152]{1,0:T(8,128)(2,1)S(1)} collective-permute-done((bf16[256,1152]{1,0:T(8,128)(2,1)S(1)}, bf16[256,1152]{1,0:T(8,128)(2,1)S(1)}, u32[]{:S(2)}, u32[]{:S(2)}) %collective-permute-start.2) | collective-permute-done | bytes 589856 | tf_op jit(solution)/shard_map/ppermute | solution.py:246
  37.4 4.7 %all-to-all-done.piece_ref = bf16[16,288,128]{2,1,0:T(8,128)(2,1)S(1)} async-done(((bf16[16,288,128]{2,1,0:T(8,128)(2,1)}), bf16[16,288,128]{2,1,0:T(8,128)(2,1)S(1)}, u32[]{:S(2)}, u32[]{:S(2)}) %all-to-all-start) | async-done | bytes 1179680 | tf_op jit(solution)/shard_map/all_to_all | solution.py:250
  42.1 3.4 %scores.1 = (f32[1024,1024]{1,0:T(8,128)S(1)}, f32[8,256]{1,0:T(8,128)S(1)}, bf16[1024,640]{1,0:T(8,128)(2,1)S(1)}) custom-call(s32[1]{0:T(128)} %bitcast.place_ref, bf16[16,288,128]{2,1,0:T(8,128)(2,1)S(1)} %all-to-all-done.piece_ref, bf16[256,1152]{1,0:T(8,128)(2,1)S(1)} %prep.1.x0, bf16[256,1152]{1,0:T(8,128)(2,1)S(1)} %collective-permute-done.x1, ...), custom_call_target="tpu_custom_call" | custom-call | tf_op jit(solution)/shard_map/scores/pallas_call | solution.py:286
  45.5 0.0 copy-start
  45.5 2.4 %collective-permute-start.3 = (f32[8,256]{1,0:T(8,128)S(1)}, f32[8,256]{1,0:T(8,128)S(1)}, u32[]{:S(2)}, u32[]{:S(2)}) collective-permute-start(f32[8,256]{1,0:T(8,128)S(1)} %get-tuple-element.14.own_ref), channel_id=1, source_target_pairs={{0,1},{1,0},{2,3},{3,2},{4,5},{5,4},{6,7},{7,6},{8,9},{9,8},{10,11... | collective-permute-start | bytes 24584 | tf_op jit(solution)/shard_map/ppermute | solution.py:246
  47.9 2.1 %values.1.t_ref = f32[1024,1024]{1,0:T(8,128)S(1)} custom-call(bf16[1024,640]{1,0:T(8,128)(2,1)S(1)} %get-tuple-element.13.lat_ref, bf16[256,1152]{1,0:T(8,128)(2,1)S(1)} %prep.1.x0, bf16[256,1152]{1,0:T(8,128)(2,1)S(1)} %collective-permute-done.x1, bf16[256,1152]{1,0:T(8,128)(2,1)S(1)} %collective-permute-done.1.x2, ...), custom_call_target="tpu_custom_call" | custom-call | tf_op jit(solution)/shard_map/values/pallas_call | solution.py:296
  50.0 0.0 copy-done
  50.0 1.1 collective-permute-done.3
  51.1 1.8 %all-gather = f32[32,256]{1,0:T(8,128)S(1)} all-gather(f32[16,256]{1,0:T(8,128)S(1)} %pad_maximum_fusion), channel_id=2, replica_groups=mesh['zh'=4,'x'=4,'c'=2,'zl'=2,'yh'=4,'y0'=2] {'c'}, dimensions={0}, use_global_device_ids=true | all-gather | bytes 49152 | tf_op jit(solution)/shard_map/all_gather | solution.py:298
  52.9 4.8 %keys.1 = (bf16[8,576,128]{2,1,0:T(8,128)(2,1)}, bf16[1024,1024]{1,0:T(8,128)(2,1)}) custom-call(s32[1]{0:T(128)} %bitcast.place_ref, f32[8,256]{1,0:T(8,128)S(1)} %get-tuple-element.14.own_ref, f32[2,16,256]{2,1,0:T(8,128)S(1)} %bitcast.14, bf16[256,1152]{1,0:T(8,128)(2,1)S(1)} %prep.1.x0, bf16[256,1152]{1,0:T(8,128)(2,1)S(1)} %collective-permute-done.x1, ...), custom_call_target="tpu_custom_call" | custom-call | tf_op jit(solution)/shard_map/keys/pallas_call | solution.py:300
  57.7 0.0 copy-start.1
  57.8 9.6 %all-to-all-start.1 = ((bf16[8,576,128]{2,1,0:T(8,128)(2,1)}), bf16[8,576,128]{2,1,0:T(8,128)(2,1)S(1)}, u32[]{:S(2)}, u32[]{:S(2)}) async-start(bf16[8,576,128]{2,1,0:T(8,128)(2,1)} %get-tuple-element.21), calls=%async_computation.1 | async-start | bytes 2359296 | tf_op jit(solution)/shard_map/all_to_all | solution.py:250
  67.4 0.0 copy-done.1
  67.4 3.8 %query.1 = (f32[512,640]{1,0:T(8,128)S(1)}, bf16[512,640]{1,0:T(8,128)(2,1)S(1)}) custom-call(bf16[1024,640]{1,0:T(8,128)(2,1)S(1)} %copy-done.1, bf16[1024,1024]{1,0:T(8,128)(2,1)} %get-tuple-element.18.ds_ref), custom_call_target="tpu_custom_call" | custom-call | tf_op jit(solution)/shard_map/query/pallas_call | solution.py:318
  71.3 1.9 %collective-permute-start.4 = (bf16[512,640]{1,0:T(8,128)(2,1)S(1)}, bf16[512,640]{1,0:T(8,128)(2,1)S(1)}, u32[]{:S(2)}, u32[]{:S(2)}) collective-permute-start(bf16[512,640]{1,0:T(8,128)(2,1)S(1)} %get-tuple-element.20), channel_id=1, source_target_pairs={{0,16},{16,0},{1,17},{17,1},{2,18},{18,2},{3,19},{19,3},{4,20},{20... | collective-permute-start | bytes 1966088 | tf_op jit(solution)/shard_map/ppermute | solution.py:246
  73.2 2.1 %collective-permute-done.4 = bf16[512,640]{1,0:T(8,128)(2,1)S(1)} collective-permute-done((bf16[512,640]{1,0:T(8,128)(2,1)S(1)}, bf16[512,640]{1,0:T(8,128)(2,1)S(1)}, u32[]{:S(2)}, u32[]{:S(2)}) %collective-permute-start.4) | collective-permute-done | bytes 655392 | tf_op jit(solution)/shard_map/ppermute | solution.py:246
  75.3 0.1 convert_add_fusion
  75.4 9.5 %all-to-all-done.1.part_ref = bf16[8,576,128]{2,1,0:T(8,128)(2,1)S(1)} async-done(((bf16[8,576,128]{2,1,0:T(8,128)(2,1)}), bf16[8,576,128]{2,1,0:T(8,128)(2,1)S(1)}, u32[]{:S(2)}, u32[]{:S(2)}) %all-to-all-start.1) | async-done | bytes 1179680 | tf_op jit(solution)/shard_map/all_to_all | solution.py:250
  84.9 0.8 sum.1
  85.7 7.8 %all-to-all-start.2 = ((bf16[16,8,640]{2,1,0:T(8,128)(2,1)}), bf16[16,8,640]{2,1,0:T(8,128)(2,1)S(1)}, u32[]{:S(2)}, u32[]{:S(2)}) async-start(bf16[16,8,640]{2,1,0:T(8,128)(2,1)} %bitcast.7), calls=%async_computation.2 | async-start | bytes 327680 | tf_op jit(solution)/shard_map/all_to_all | solution.py:250
  93.5 3.3 %collective-permute-start.5 = (bf16[256,640]{1,0:T(8,128)(2,1)S(1)}, bf16[256,640]{1,0:T(8,128)(2,1)S(1)}, u32[]{:S(2)}, u32[]{:S(2)}) collective-permute-start(bf16[256,640]{1,0:T(8,128)(2,1)S(1)} %slice.30), channel_id=1, source_target_pairs={{0,1},{1,0},{2,3},{3,2},{4,5},{5,4},{6,7},{7,6},{8,9},{9,8},{10,11... | collective-permute-start | bytes 983048 | tf_op jit(solution)/shard_map/ppermute | solution.py:246
  96.8 9.4 %all-to-all-done.2 = bf16[16,8,640]{2,1,0:T(8,128)(2,1)S(1)} async-done(((bf16[16,8,640]{2,1,0:T(8,128)(2,1)}), bf16[16,8,640]{2,1,0:T(8,128)(2,1)S(1)}, u32[]{:S(2)}, u32[]{:S(2)}) %all-to-all-start.2) | async-done | bytes 163872 | tf_op jit(solution)/shard_map/all_to_all | solution.py:250
  106.2 0.6 convert_reduce_fusion
  106.9 0.0 collective-permute-done.5
  106.9 0.8 fusion.1
  (3 shorter events, 0.1 us)
Async XLA Ops:
  0.6 0.9 copy-start.5
  2.9 13.7 %copy-start.2 = (bf16[32,8,576]{2,1,0:T(8,128)(2,1)S(1)}, bf16[32,8,576]{2,1,0:T(8,128)(2,1)}, u32[]{:S(2)}) copy-start(bf16[32,8,576]{2,1,0:T(8,128)(2,1)} %param.5) | copy-start | bytes 884740
  2.9 13.7 %copy-start.3 = (bf16[32,8,512]{2,1,0:T(8,128)(2,1)S(1)}, bf16[32,8,512]{2,1,0:T(8,128)(2,1)}, u32[]{:S(2)}) copy-start(bf16[32,8,512]{2,1,0:T(8,128)(2,1)} %param.7) | copy-start | bytes 786436
  2.9 13.7 %copy-start.4 = (bf16[32,8,512]{2,1,0:T(8,128)(2,1)S(1)}, bf16[32,8,512]{2,1,0:T(8,128)(2,1)}, u32[]{:S(2)}) copy-start(bf16[32,8,512]{2,1,0:T(8,128)(2,1)} %param.8) | copy-start | bytes 786436
  2.9 39.2 %all-to-all-start = ((bf16[16,288,128]{2,1,0:T(8,128)(2,1)}), bf16[16,288,128]{2,1,0:T(8,128)(2,1)S(1)}, u32[]{:S(2)}, u32[]{:S(2)}) async-start(bf16[16,288,128]{2,1,0:T(8,128)(2,1)} %spread.1), calls=%async_computation | async-start | bytes 2359296 | tf_op jit(solution)/shard_map/all_to_all | solution.py:250
  16.9 16.7 %collective-permute-start = (bf16[256,1152]{1,0:T(8,128)(2,1)S(1)}, bf16[256,1152]{1,0:T(8,128)(2,1)S(1)}, u32[]{:S(2)}, u32[]{:S(2)}) collective-permute-start(bf16[256,1152]{1,0:T(8,128)(2,1)S(1)} %prep.1.x0), channel_id=1, source_target_pairs={{0,1},{1,0},{2,3},{3,2},{4,5},{5,4},{6,7},{7,6},{8,9},{9,8},{10,11... | collective-permute-start | bytes 1769480 | tf_op jit(solution)/shard_map/ppermute | solution.py:246
  19.2 16.2 %collective-permute-start.1 = (bf16[256,1152]{1,0:T(8,128)(2,1)S(1)}, bf16[256,1152]{1,0:T(8,128)(2,1)S(1)}, u32[]{:S(2)}, u32[]{:S(2)}) collective-permute-start(bf16[256,1152]{1,0:T(8,128)(2,1)S(1)} %prep.1.x0), channel_id=1, source_target_pairs={{0,16},{16,0},{1,17},{17,1},{2,18},{18,2},{3,19},{19,3},{4,20},{20... | collective-permute-start | bytes 1769480 | tf_op jit(solution)/shard_map/ppermute | solution.py:246
  33.6 3.9 %collective-permute-start.2 = (bf16[256,1152]{1,0:T(8,128)(2,1)S(1)}, bf16[256,1152]{1,0:T(8,128)(2,1)S(1)}, u32[]{:S(2)}, u32[]{:S(2)}) collective-permute-start(bf16[256,1152]{1,0:T(8,128)(2,1)S(1)} %collective-permute-done.x1), channel_id=1, source_target_pairs={{0,16},{16,0},{1,17},{17,1},{2,18},{18,2},{3,19},{19,3},{4,20},{20... | collective-permute-start | bytes 1769480 | tf_op jit(solution)/shard_map/ppermute | solution.py:246
  45.5 4.5 %copy-start = (bf16[1024,640]{1,0:T(8,128)(2,1)}, bf16[1024,640]{1,0:T(8,128)(2,1)S(1)}, u32[]{:S(2)}) copy-start(bf16[1024,640]{1,0:T(8,128)(2,1)S(1)} %get-tuple-element.13.lat_ref) | copy-start | bytes 3932164
  45.5 5.5 %collective-permute-start.3 = (f32[8,256]{1,0:T(8,128)S(1)}, f32[8,256]{1,0:T(8,128)S(1)}, u32[]{:S(2)}, u32[]{:S(2)}) collective-permute-start(f32[8,256]{1,0:T(8,128)S(1)} %get-tuple-element.14.own_ref), channel_id=1, source_target_pairs={{0,1},{1,0},{2,3},{3,2},{4,5},{5,4},{6,7},{7,6},{8,9},{9,8},{10,11... | collective-permute-start | bytes 24584 | tf_op jit(solution)/shard_map/ppermute | solution.py:246
  57.7 9.7 %copy-start.1 = (bf16[1024,640]{1,0:T(8,128)(2,1)S(1)}, bf16[1024,640]{1,0:T(8,128)(2,1)}, u32[]{:S(2)}) copy-start(bf16[1024,640]{1,0:T(8,128)(2,1)} %copy-done) | copy-start | bytes 3932164
  57.8 27.1 %all-to-all-start.1 = ((bf16[8,576,128]{2,1,0:T(8,128)(2,1)}), bf16[8,576,128]{2,1,0:T(8,128)(2,1)S(1)}, u32[]{:S(2)}, u32[]{:S(2)}) async-start(bf16[8,576,128]{2,1,0:T(8,128)(2,1)} %get-tuple-element.21), calls=%async_computation.1 | async-start | bytes 2359296 | tf_op jit(solution)/shard_map/all_to_all | solution.py:250
  71.3 4.0 %collective-permute-start.4 = (bf16[512,640]{1,0:T(8,128)(2,1)S(1)}, bf16[512,640]{1,0:T(8,128)(2,1)S(1)}, u32[]{:S(2)}, u32[]{:S(2)}) collective-permute-start(bf16[512,640]{1,0:T(8,128)(2,1)S(1)} %get-tuple-element.20), channel_id=1, source_target_pairs={{0,16},{16,0},{1,17},{17,1},{2,18},{18,2},{3,19},{19,3},{4,20},{20... | collective-permute-start | bytes 1966088 | tf_op jit(solution)/shard_map/ppermute | solution.py:246
  85.7 20.5 %all-to-all-start.2 = ((bf16[16,8,640]{2,1,0:T(8,128)(2,1)}), bf16[16,8,640]{2,1,0:T(8,128)(2,1)S(1)}, u32[]{:S(2)}, u32[]{:S(2)}) async-start(bf16[16,8,640]{2,1,0:T(8,128)(2,1)} %bitcast.7), calls=%async_computation.2 | async-start | bytes 327680 | tf_op jit(solution)/shard_map/all_to_all | solution.py:250
  93.5 13.3 %collective-permute-start.5 = (bf16[256,640]{1,0:T(8,128)(2,1)S(1)}, bf16[256,640]{1,0:T(8,128)(2,1)S(1)}, u32[]{:S(2)}, u32[]{:S(2)}) collective-permute-start(bf16[256,640]{1,0:T(8,128)(2,1)S(1)} %slice.30), channel_id=1, source_target_pairs={{0,1},{1,0},{2,3},{3,2},{4,5},{5,4},{6,7},{7,6},{8,9},{9,8},{10,11... | collective-permute-start | bytes 983048 | tf_op jit(solution)/shard_map/ppermute | solution.py:246

commit v6 on v5

--- a/solution.py
+++ b/solution.py
@@ -18,6 +18,7 @@
 PIECE = 64
 FOLD = 288
 TEAM = 4
+TILES = KEYS // TILE
 
 FINE = ("zh", "x", "c", "zl", "yh", "y0")
 SIZES = (4, 4, 2, 2, 4, 2)
@@ -68,7 +69,7 @@
         + [jnp.concatenate([mine[:32, 512:], mine[32:, 512:]], axis=1)],
         axis=0,
     )
-    for peer in range(16):
+    for peer in range(4):
         out_ref[peer] = folded
 
 
@@ -87,44 +88,42 @@
     return slice(k * ROWS, (k + 1) * ROWS)
 
 
-def score_kernel(place_ref, piece_ref, x0, x1, x2, x3, p_ref, stat_ref, lat_ref):
+def score_kernel(place_ref, piece_ref, x0, x1, x2, x3, p_ref, stat_ref, lat_ref, top_ref):
     blocks = (x0, x1, x2, x3)
     core, odd = place_ref[0] // 2, place_ref[0] % 2
     poses = [row_facts(b)[1] for b in blocks]
 
-    def scores(tile, tops):
-        rows = tile_rows(tile)
+    tops, sums = [], []
+    for tile in range(TILES):
+        rows = slice(tile * TILE, tile * TILE + TILE)
         n = lax.broadcasted_iota(jnp.int32, (TILE, 1), 0)
         key_pos = (
             (n // 64) * 1024 + tile * 256 + core * 128 + ((n // 8) % 8) * 16 + odd * 8 + n % 8
         ).astype(jnp.float32)
         keys = jnp.concatenate([unfold(piece_ref.at[4 * tile + zh]) for zh in range(4)], axis=0)
         lat_ref[rows, :] = keys
-        new = []
         for k, block in enumerate(blocks):
             s = dot_nt(keys, block[:, VALUES:]) * score_scale
             s = jnp.where(key_pos <= poses[k], s, masked_score)
-            p_ref[rows, block_cols(k)] = s
-            new.append(jnp.maximum(tops[k], jnp.max(s, axis=0, keepdims=True)))
-        return tuple(new)
-
-    tops = lax.fori_loop(
-        0, KEYS // TILE, scores, (jnp.full((1, ROWS), least_top, jnp.float32),) * TEAM
-    )
-
-    def weigh(tile, sums):
-        rows = tile_rows(tile)
-        new = []
-        for k in range(TEAM):
-            p = jnp.exp(p_ref[rows, block_cols(k)] - tops[k])
+            top = jnp.maximum(jnp.max(s, axis=0, keepdims=True), least_top)
+            p = jnp.exp(s - top)
             p_ref[rows, block_cols(k)] = p
-            new.append(sums[k] + jnp.sum(p, axis=0, keepdims=True))
-        return tuple(new)
-
-    sums = lax.fori_loop(
-        0, KEYS // TILE, weigh, (jnp.zeros((1, ROWS), jnp.float32),) * TEAM
-    )
-    stat_ref[...] = jnp.concatenate(tops + sums, axis=0)
+            tops.append(top)
+            sums.append(jnp.sum(p, axis=0, keepdims=True))
+    all_tops, all_sums = [], []
+    for k in range(TEAM):
+        top = tops[k]
+        for tile in range(1, TILES):
+            top = jnp.maximum(top, tops[TEAM * tile + k])
+        all_tops.append(top)
+        all_sums.append(
+            sum(
+                sums[TEAM * tile + k] * jnp.exp(tops[TEAM * tile + k] - top)
+                for tile in range(TILES)
+            )
+        )
+    top_ref[...] = jnp.concatenate(tops, axis=0)
+    stat_ref[...] = jnp.concatenate(all_tops + all_sums, axis=0)
 
 
 def value_kernel(lat_ref, x0, x1, x2, x3, p_ref, t_ref):
@@ -139,7 +138,7 @@
             t_ref[rows, block_cols(k)] = p_ref[rows, block_cols(k)] * (pg - deltas[k])
         return 0
 
-    lax.fori_loop(0, KEYS // TILE, values, 0)
+    lax.fori_loop(0, KEYS // TILE, values, 0, unroll=True)
 
 
 def row_factors(place_ref, own_ref, team_ref):
@@ -154,7 +153,13 @@
                 sums.append(team_ref[core ^ c, TEAM + spot:TEAM + spot + 1, :])
         top = jnp.maximum(jnp.maximum(tops[0], tops[1]), jnp.maximum(tops[2], tops[3]))
         total = sum(z * jnp.exp(m - top) for m, z in zip(tops, sums))
-        factors.append(jnp.exp(own_ref[k:k + 1, :] - top) / total)
+        inverse = 1.0 / total
+        factors.append(
+            [
+                jnp.exp(own_ref[TEAM * t + k:TEAM * t + k + 1, :] - top) * inverse
+                for t in range(TILES)
+            ]
+        )
     return factors
 
 
@@ -172,13 +177,13 @@
             pltpu.make_async_copy(held_ds.at[rows], ds_ref.at[rows], sems.at[1, tile]),
         )
 
-    def keys(tile, _):
-        rows = tile_rows(tile)
+    for tile in range(TILES):
+        rows = slice(tile * TILE, tile * TILE + TILE)
         low = high = None
         for k, block in enumerate(blocks):
             cols = block_cols(k)
-            w = (p_ref[rows, cols] * factors[k]).astype(jnp.bfloat16)
-            ds = (t_ref[rows, cols] * (factors[k] * score_scale)).astype(jnp.bfloat16)
+            w = (p_ref[rows, cols] * factors[k][tile]).astype(jnp.bfloat16)
+            ds = (t_ref[rows, cols] * (factors[k][tile] * score_scale)).astype(jnp.bfloat16)
             held_ds[rows, cols] = ds
             part = jnp.dot(
                 ds, block[:, VALUES:VALUES + 512], preferred_element_type=jnp.float32
@@ -198,9 +203,6 @@
             )
         for copy in leave(tile):
             copy.start()
-        return 0
-
-    lax.fori_loop(0, KEYS // TILE, keys, 0)
     for tile in range(KEYS // TILE):
         for copy in leave(tile):
             copy.wait()
@@ -235,6 +237,16 @@
     out_ref[:, 512:] = tail.astype(out_ref.dtype)
 
 
+def copy_kernel(rows_ref, out_ref, sems):
+    copies = [
+        pltpu.make_async_copy(rows_ref, out_ref.at[peer], sems.at[peer]) for peer in range(4)
+    ]
+    for copy in copies:
+        copy.start()
+    for copy in copies:
+        copy.wait()
+
+
 def whole(n):
     return [pl.BlockSpec(memory_space=pltpu.VMEM)] * n
 
@@ -266,10 +278,21 @@
     place = (lax.axis_index("c") * 2 + lax.axis_index("y0")).astype(jnp.int32).reshape(1)
     shape = jax.ShapeDtypeStruct
 
-    pieces = call(spread_kernel, shape((16, FOLD, 128), jnp.bfloat16), 1, 1, "spread")(
+    pieces = call(spread_kernel, shape((4, FOLD, 128), jnp.bfloat16), 1, 1, "spread")(
         place, latents.T
     )
-    pieces = exchange(pieces, ("x", "zh"))
+    pieces = exchange(pieces, ("zh",))
+    pieces = pl.pallas_call(
+        copy_kernel,
+        out_shape=pltpu.HBM((4, 4, FOLD, 128), jnp.bfloat16),
+        in_specs=whole(1),
+        out_specs=pl.BlockSpec(memory_space=pltpu.HBM),
+        scratch_shapes=[pltpu.SemaphoreType.DMA((4,))],
+        compiler_params=pltpu.CompilerParams(vmem_limit_bytes=16 * 1024 * 1024),
+        name="copies",
+    )(pieces)
+    pieces = exchange(pieces, ("x",))
+    pieces = pieces.reshape(16, FOLD, 128)
 
     x0 = call(prep_kernel, shape((ROWS, PACK), jnp.bfloat16), 1, 3, "prep")(
         query_start,
@@ -283,12 +306,13 @@
     x = (x0, x1, x2, x3)
 
     square = shape((KEYS, TEAM * ROWS), jnp.float32)
-    p, stats, lat = call(
+    p, stats, lat, tops = call(
         score_kernel,
         (
             square,
             shape((2 * TEAM, ROWS), jnp.float32),
             shape((KEYS, WIDE), jnp.bfloat16),
+            shape((TILES * TEAM, ROWS), jnp.float32),
         ),
         1, 5, "scores",
     )(place, pieces, *x)
@@ -312,7 +336,7 @@
         ],
         compiler_params=pltpu.CompilerParams(vmem_limit_bytes=16 * 1024 * 1024),
         name="keys",
-    )(place, stats, team, *x, p, t)
+    )(place, tops, team, *x, p, t)
     parts = exchange(key_part, ("x", "zl"))
 
     near, far = pl.pallas_call(

time: 108 us -> 104 us (0.963)
  waiting for transfers between devices: 41 us -> 37.8 us
  local copies, waits for them, and re-layouts: 1 us -> 3.86 us
  starting transfers between devices: 44.2 us -> 41.9 us
  Pallas kernels: 16.7 us -> 15.1 us
    ppermute x6, waiting for transfers between devices: 17.5 us -> 7.22 us  [swap(): return lax.ppermute(block, axis, [(0, 1), (1, 0)])]
    all_to_all x3 -> x4, waiting for transfers between devices: 23.5 us -> 30.6 us  [exchange(): return lax.all_to_all(pieces, axes, 0, 0, tiled=True)]
    unnamed x12, local copies, waits for them, and re-layouts: 0.92 us -> 3.78 us
    all_to_all x3 -> x4, starting transfers between devices: 30.5 us -> 28.2 us  [exchange(): return lax.all_to_all(pieces, axes, 0, 0, tiled=True)]
  transfers between devices with their start and end apart: 9 -> 10, of which waited for: 7 -> 8; matrix products, arithmetic and copies ran while one was open for 1% -> 1% of each run, Pallas kernels for 6% -> 6%
where the time goes in v6:
time: 104 us; the launch traced here: 103 us
  starting transfers between devices  41.9 us (40%)
  waiting for transfers between devices  37.8 us (36%)
  Pallas kernels  15.1 us (15%)
  local copies, waits for them, and re-layouts  3.86 us (4%)
  blocking collectives  1.82 us (2%)
  other arithmetic  1.53 us (1%)
  between operations  1.46 us (1%)
    all_to_all x4, waiting for transfers between devices, exchange(): return lax.all_to_all(pieces, axes, 0, 0, tiled=True)  30.6 us
    all_to_all x4, starting transfers between devices, exchange(): return lax.all_to_all(pieces, axes, 0, 0, tiled=True)  28.2 us
    ppermute x6, starting transfers between devices, swap(): return lax.ppermute(block, axis, [(0, 1), (1, 0)])  13.7 us
    ppermute x6, waiting for transfers between devices, swap(): return lax.ppermute(block, axis, [(0, 1), (1, 0)])  7.22 us
    pallas_call x1, Pallas kernels, per_device(): pl.pallas_call(key_kernel, out_shape=(pltpu.HBM((8, 576, 128), jnp.bfloat...  4.19 us
    pallas_call x1, Pallas kernels, per_device(): pl.pallas_call(query_kernel, out_shape=(shape((2 * ROWS, WIDE), jnp.float...  3.84 us
    unnamed x12, local copies, waits for them, and re-layouts  3.78 us
    pallas_call x1, Pallas kernels, per_device(): call(score_kernel, (square, shape((2 * TEAM, ROWS), jnp.float32), shape((...  2.54 us
  transfers between devices with their start and end apart: 10, of which 8 were waited for; matrix products, arithmetic and copies ran while one was open for 1% of the time, Pallas kernels for 6%

profile of v6, /device:TPU:8, one launch (start us, length us, event | category | flops | bytes accessed | tf_op | source)
XLA Modules:
  0.0 103.4 jit_solution(2273702979732839080)
XLA Ops:
  0.6 0.0 copy-start.5
  0.6 0.9 copy-done.5
  1.5 0.9 spread.1
  2.4 10.3 %all-to-all-start = ((bf16[4,288,128]{2,1,0:T(8,128)(2,1)}), bf16[4,288,128]{2,1,0:T(8,128)(2,1)S(1)}, u32[]{:S(2)}, u32[]{:S(2)}) async-start(bf16[4,288,128]{2,1,0:T(8,128)(2,1)} %spread.1), calls=%async_computation | async-start | bytes 589824 | tf_op jit(solution)/shard_map/all_to_all | solution.py:262
  13.4 0.0 copy-start.2
  13.4 1.0 copy-done.2
  14.4 0.0 copy-start.3
  14.4 0.9 copy-done.3
  15.3 0.0 copy-start.4
  15.3 0.9 copy-done.4
  16.3 0.3 prep.1.x0
  16.6 2.3 %collective-permute-start = (bf16[256,1152]{1,0:T(8,128)(2,1)S(1)}, bf16[256,1152]{1,0:T(8,128)(2,1)S(1)}, u32[]{:S(2)}, u32[]{:S(2)}) collective-permute-start(bf16[256,1152]{1,0:T(8,128)(2,1)S(1)} %prep.1.x0), channel_id=1, source_target_pairs={{0,1},{1,0},{2,3},{3,2},{4,5},{5,4},{6,7},{7,6},{8,9},{9,8},{10,11... | collective-permute-start | bytes 1769480 | tf_op jit(solution)/shard_map/ppermute | solution.py:258
  18.9 5.6 %all-to-all-done.rows_ref = bf16[4,288,128]{2,1,0:T(8,128)(2,1)S(1)} async-done(((bf16[4,288,128]{2,1,0:T(8,128)(2,1)}), bf16[4,288,128]{2,1,0:T(8,128)(2,1)S(1)}, u32[]{:S(2)}, u32[]{:S(2)}) %all-to-all-start) | async-done | bytes 294944 | tf_op jit(solution)/shard_map/all_to_all | solution.py:262
  24.5 1.1 %copies.1 = bf16[4,4,288,128]{3,2,1,0:T(8,128)(2,1)} custom-call(bf16[4,288,128]{2,1,0:T(8,128)(2,1)S(1)} %all-to-all-done.rows_ref), custom_call_target="tpu_custom_call" | custom-call | tf_op jit(solution)/shard_map/copies/pallas_call | solution.py:285
  25.6 4.3 %all-to-all-start.1 = ((bf16[4,4,288,128]{3,2,1,0:T(8,128)(2,1)}), bf16[4,4,288,128]{3,2,1,0:T(8,128)(2,1)S(1)}, u32[]{:S(2)}, u32[]{:S(2)}) async-start(bf16[4,4,288,128]{3,2,1,0:T(8,128)(2,1)} %copies.1), calls=%async_computation.1 | async-start | bytes 2359296 | tf_op jit(solution)/shard_map/all_to_all | solution.py:262
  29.9 1.9 %collective-permute-start.1 = (bf16[256,1152]{1,0:T(8,128)(2,1)S(1)}, bf16[256,1152]{1,0:T(8,128)(2,1)S(1)}, u32[]{:S(2)}, u32[]{:S(2)}) collective-permute-start(bf16[256,1152]{1,0:T(8,128)(2,1)S(1)} %prep.1.x0), channel_id=1, source_target_pairs={{0,16},{16,0},{1,17},{17,1},{2,18},{18,2},{3,19},{19,3},{4,20},{20... | collective-permute-start | bytes 1769480 | tf_op jit(solution)/shard_map/ppermute | solution.py:258
  31.8 1.4 %collective-permute-done.x1 = bf16[256,1152]{1,0:T(8,128)(2,1)S(1)} collective-permute-done((bf16[256,1152]{1,0:T(8,128)(2,1)S(1)}, bf16[256,1152]{1,0:T(8,128)(2,1)S(1)}, u32[]{:S(2)}, u32[]{:S(2)}) %collective-permute-start) | collective-permute-done | bytes 589856 | tf_op jit(solution)/shard_map/ppermute | solution.py:258
  33.2 1.9 %collective-permute-start.2 = (bf16[256,1152]{1,0:T(8,128)(2,1)S(1)}, bf16[256,1152]{1,0:T(8,128)(2,1)S(1)}, u32[]{:S(2)}, u32[]{:S(2)}) collective-permute-start(bf16[256,1152]{1,0:T(8,128)(2,1)S(1)} %collective-permute-done.x1), channel_id=1, source_target_pairs={{0,16},{16,0},{1,17},{17,1},{2,18},{18,2},{3,19},{19,3},{4,20},{20... | collective-permute-start | bytes 1769480 | tf_op jit(solution)/shard_map/ppermute | solution.py:258
  35.2 0.0 collective-permute-done.1.x2
  35.2 2.0 %collective-permute-done.2.x3 = bf16[256,1152]{1,0:T(8,128)(2,1)S(1)} collective-permute-done((bf16[256,1152]{1,0:T(8,128)(2,1)S(1)}, bf16[256,1152]{1,0:T(8,128)(2,1)S(1)}, u32[]{:S(2)}, u32[]{:S(2)}) %collective-permute-start.2) | collective-permute-done | bytes 589856 | tf_op jit(solution)/shard_map/ppermute | solution.py:258
  37.1 5.9 %all-to-all-done.1 = bf16[4,4,288,128]{3,2,1,0:T(8,128)(2,1)S(1)} async-done(((bf16[4,4,288,128]{3,2,1,0:T(8,128)(2,1)}), bf16[4,4,288,128]{3,2,1,0:T(8,128)(2,1)S(1)}, u32[]{:S(2)}, u32[]{:S(2)}) %all-to-all-start.1) | async-done | bytes 1179680 | tf_op jit(solution)/shard_map/all_to_all | solution.py:262
  43.0 2.5 %scores.1 = (f32[1024,1024]{1,0:T(8,128)S(1)}, f32[8,256]{1,0:T(8,128)S(1)}, bf16[1024,640]{1,0:T(8,128)(2,1)S(1)}, f32[16,256]{1,0:T(8,128)S(1)}) custom-call(s32[1]{0:T(128)} %bitcast.place_ref, bf16[16,288,128]{2,1,0:T(8,128)(2,1)S(1)} %bitcast.11, bf16[256,1152]{1,0:T(8,128)(2,1)S(1)} %prep.1.x0, bf16[256,1152]{1,0:T(8,128)(2,1)S(1)} %collective-permute-done.x1, ...), custom_call_target="tpu_custom_call" | custom-call | tf_op jit(solution)/shard_map/scores/pallas_call | solution.py:309
  45.5 0.0 copy-start
  45.6 2.3 %collective-permute-start.3 = (f32[8,256]{1,0:T(8,128)S(1)}, f32[8,256]{1,0:T(8,128)S(1)}, u32[]{:S(2)}, u32[]{:S(2)}) collective-permute-start(f32[8,256]{1,0:T(8,128)S(1)} %get-tuple-element.16), channel_id=1, source_target_pairs={{0,1},{1,0},{2,3},{3,2},{4,5},{5,4},{6,7},{7,6},{8,9},{9,8},{10,11... | collective-permute-start | bytes 24584 | tf_op jit(solution)/shard_map/ppermute | solution.py:258
  47.9 1.4 %values.1.t_ref = f32[1024,1024]{1,0:T(8,128)S(1)} custom-call(bf16[1024,640]{1,0:T(8,128)(2,1)S(1)} %get-tuple-element.14.lat_ref, bf16[256,1152]{1,0:T(8,128)(2,1)S(1)} %prep.1.x0, bf16[256,1152]{1,0:T(8,128)(2,1)S(1)} %collective-permute-done.x1, bf16[256,1152]{1,0:T(8,128)(2,1)S(1)} %collective-permute-done.1.x2, ...), custom_call_target="tpu_custom_call" | custom-call | tf_op jit(solution)/shard_map/values/pallas_call | solution.py:320
  49.3 0.0 copy-done
  49.3 1.8 %collective-permute-done.3 = f32[8,256]{1,0:T(8,128)S(1)} collective-permute-done((f32[8,256]{1,0:T(8,128)S(1)}, f32[8,256]{1,0:T(8,128)S(1)}, u32[]{:S(2)}, u32[]{:S(2)}) %collective-permute-start.3) | collective-permute-done | bytes 8224 | tf_op jit(solution)/shard_map/ppermute | solution.py:258
  51.1 1.8 %all-gather = f32[32,256]{1,0:T(8,128)S(1)} all-gather(f32[16,256]{1,0:T(8,128)S(1)} %pad_maximum_fusion), channel_id=2, replica_groups=mesh['zh'=4,'x'=4,'c'=2,'zl'=2,'yh'=4,'y0'=2] {'c'}, dimensions={0}, use_global_device_ids=true | all-gather | bytes 49152 | tf_op jit(solution)/shard_map/all_gather | solution.py:322
  52.9 4.2 %keys.1 = (bf16[8,576,128]{2,1,0:T(8,128)(2,1)}, bf16[1024,1024]{1,0:T(8,128)(2,1)}) custom-call(s32[1]{0:T(128)} %bitcast.place_ref, f32[16,256]{1,0:T(8,128)S(1)} %get-tuple-element.15.own_ref, f32[2,16,256]{2,1,0:T(8,128)S(1)} %bitcast.16, bf16[256,1152]{1,0:T(8,128)(2,1)S(1)} %prep.1.x0, bf16[256,1152]{1,0:T(8,128)(2,1)S(1)} %collective-permute-done.x1, ...), custom_call_target="tpu_custom_call" | custom-call | tf_op jit(solution)/shard_map/keys/pallas_call | solution.py:324
  57.1 0.0 copy-start.1
  57.1 5.6 %all-to-all-start.2 = ((bf16[8,576,128]{2,1,0:T(8,128)(2,1)}), bf16[8,576,128]{2,1,0:T(8,128)(2,1)S(1)}, u32[]{:S(2)}, u32[]{:S(2)}) async-start(bf16[8,576,128]{2,1,0:T(8,128)(2,1)} %get-tuple-element.23), calls=%async_computation.2 | async-start | bytes 2359296 | tf_op jit(solution)/shard_map/all_to_all | solution.py:262
  62.8 0.0 copy-done.1
  62.8 3.8 %query.1 = (f32[512,640]{1,0:T(8,128)S(1)}, bf16[512,640]{1,0:T(8,128)(2,1)S(1)}) custom-call(bf16[1024,640]{1,0:T(8,128)(2,1)S(1)} %copy-done.1, bf16[1024,1024]{1,0:T(8,128)(2,1)} %get-tuple-element.20.ds_ref), custom_call_target="tpu_custom_call" | custom-call | tf_op jit(solution)/shard_map/query/pallas_call | solution.py:342
  66.6 1.9 %collective-permute-start.4 = (bf16[512,640]{1,0:T(8,128)(2,1)S(1)}, bf16[512,640]{1,0:T(8,128)(2,1)S(1)}, u32[]{:S(2)}, u32[]{:S(2)}) collective-permute-start(bf16[512,640]{1,0:T(8,128)(2,1)S(1)} %get-tuple-element.22), channel_id=1, source_target_pairs={{0,16},{16,0},{1,17},{17,1},{2,18},{18,2},{3,19},{19,3},{4,20},{20... | collective-permute-start | bytes 1966088 | tf_op jit(solution)/shard_map/ppermute | solution.py:258
  68.6 2.1 %collective-permute-done.4 = bf16[512,640]{1,0:T(8,128)(2,1)S(1)} collective-permute-done((bf16[512,640]{1,0:T(8,128)(2,1)S(1)}, bf16[512,640]{1,0:T(8,128)(2,1)S(1)}, u32[]{:S(2)}, u32[]{:S(2)}) %collective-permute-start.4) | collective-permute-done | bytes 655392 | tf_op jit(solution)/shard_map/ppermute | solution.py:258
  70.6 0.1 convert_add_fusion
  70.8 9.5 %all-to-all-done.2.part_ref = bf16[8,576,128]{2,1,0:T(8,128)(2,1)S(1)} async-done(((bf16[8,576,128]{2,1,0:T(8,128)(2,1)}), bf16[8,576,128]{2,1,0:T(8,128)(2,1)S(1)}, u32[]{:S(2)}, u32[]{:S(2)}) %all-to-all-start.2) | async-done | bytes 1179680 | tf_op jit(solution)/shard_map/all_to_all | solution.py:262
  80.3 0.8 sum.1
  81.1 7.9 %all-to-all-start.3 = ((bf16[16,8,640]{2,1,0:T(8,128)(2,1)}), bf16[16,8,640]{2,1,0:T(8,128)(2,1)S(1)}, u32[]{:S(2)}, u32[]{:S(2)}) async-start(bf16[16,8,640]{2,1,0:T(8,128)(2,1)} %bitcast.8), calls=%async_computation.3 | async-start | bytes 327680 | tf_op jit(solution)/shard_map/all_to_all | solution.py:262
  89.0 3.2 %collective-permute-start.5 = (bf16[256,640]{1,0:T(8,128)(2,1)S(1)}, bf16[256,640]{1,0:T(8,128)(2,1)S(1)}, u32[]{:S(2)}, u32[]{:S(2)}) collective-permute-start(bf16[256,640]{1,0:T(8,128)(2,1)S(1)} %slice.30), channel_id=1, source_target_pairs={{0,1},{1,0},{2,3},{3,2},{4,5},{5,4},{6,7},{7,6},{8,9},{9,8},{10,11... | collective-permute-start | bytes 983048 | tf_op jit(solution)/shard_map/ppermute | solution.py:258
  92.4 9.6 %all-to-all-done.3 = bf16[16,8,640]{2,1,0:T(8,128)(2,1)S(1)} async-done(((bf16[16,8,640]{2,1,0:T(8,128)(2,1)}), bf16[16,8,640]{2,1,0:T(8,128)(2,1)S(1)}, u32[]{:S(2)}, u32[]{:S(2)}) %all-to-all-start.3) | async-done | bytes 163872 | tf_op jit(solution)/shard_map/all_to_all | solution.py:262
  102.0 0.6 convert_reduce_fusion
  102.6 0.0 collective-permute-done.5
  102.6 0.8 fusion.1
  (3 shorter events, 0.1 us)
Async XLA Ops:
  0.6 0.9 copy-start.5
  2.4 22.1 %all-to-all-start = ((bf16[4,288,128]{2,1,0:T(8,128)(2,1)}), bf16[4,288,128]{2,1,0:T(8,128)(2,1)S(1)}, u32[]{:S(2)}, u32[]{:S(2)}) async-start(bf16[4,288,128]{2,1,0:T(8,128)(2,1)} %spread.1), calls=%async_computation | async-start | bytes 589824 | tf_op jit(solution)/shard_map/all_to_all | solution.py:262
  13.4 1.0 copy-start.2
  14.4 0.9 copy-start.3
  15.3 0.9 copy-start.4
  16.6 16.7 %collective-permute-start = (bf16[256,1152]{1,0:T(8,128)(2,1)S(1)}, bf16[256,1152]{1,0:T(8,128)(2,1)S(1)}, u32[]{:S(2)}, u32[]{:S(2)}) collective-permute-start(bf16[256,1152]{1,0:T(8,128)(2,1)S(1)} %prep.1.x0), channel_id=1, source_target_pairs={{0,1},{1,0},{2,3},{3,2},{4,5},{5,4},{6,7},{7,6},{8,9},{9,8},{10,11... | collective-permute-start | bytes 1769480 | tf_op jit(solution)/shard_map/ppermute | solution.py:258
  25.6 17.4 %all-to-all-start.1 = ((bf16[4,4,288,128]{3,2,1,0:T(8,128)(2,1)}), bf16[4,4,288,128]{3,2,1,0:T(8,128)(2,1)S(1)}, u32[]{:S(2)}, u32[]{:S(2)}) async-start(bf16[4,4,288,128]{3,2,1,0:T(8,128)(2,1)} %copies.1), calls=%async_computation.1 | async-start | bytes 2359296 | tf_op jit(solution)/shard_map/all_to_all | solution.py:262
  29.9 5.3 %collective-permute-start.1 = (bf16[256,1152]{1,0:T(8,128)(2,1)S(1)}, bf16[256,1152]{1,0:T(8,128)(2,1)S(1)}, u32[]{:S(2)}, u32[]{:S(2)}) collective-permute-start(bf16[256,1152]{1,0:T(8,128)(2,1)S(1)} %prep.1.x0), channel_id=1, source_target_pairs={{0,16},{16,0},{1,17},{17,1},{2,18},{18,2},{3,19},{19,3},{4,20},{20... | collective-permute-start | bytes 1769480 | tf_op jit(solution)/shard_map/ppermute | solution.py:258
  33.2 3.9 %collective-permute-start.2 = (bf16[256,1152]{1,0:T(8,128)(2,1)S(1)}, bf16[256,1152]{1,0:T(8,128)(2,1)S(1)}, u32[]{:S(2)}, u32[]{:S(2)}) collective-permute-start(bf16[256,1152]{1,0:T(8,128)(2,1)S(1)} %collective-permute-done.x1), channel_id=1, source_target_pairs={{0,16},{16,0},{1,17},{17,1},{2,18},{18,2},{3,19},{19,3},{4,20},{20... | collective-permute-start | bytes 1769480 | tf_op jit(solution)/shard_map/ppermute | solution.py:258
  45.5 3.8 %copy-start = (bf16[1024,640]{1,0:T(8,128)(2,1)}, bf16[1024,640]{1,0:T(8,128)(2,1)S(1)}, u32[]{:S(2)}) copy-start(bf16[1024,640]{1,0:T(8,128)(2,1)S(1)} %get-tuple-element.14.lat_ref) | copy-start | bytes 3932164
  45.6 5.5 %collective-permute-start.3 = (f32[8,256]{1,0:T(8,128)S(1)}, f32[8,256]{1,0:T(8,128)S(1)}, u32[]{:S(2)}, u32[]{:S(2)}) collective-permute-start(f32[8,256]{1,0:T(8,128)S(1)} %get-tuple-element.16), channel_id=1, source_target_pairs={{0,1},{1,0},{2,3},{3,2},{4,5},{5,4},{6,7},{7,6},{8,9},{9,8},{10,11... | collective-permute-start | bytes 24584 | tf_op jit(solution)/shard_map/ppermute | solution.py:258
  57.1 5.7 %copy-start.1 = (bf16[1024,640]{1,0:T(8,128)(2,1)S(1)}, bf16[1024,640]{1,0:T(8,128)(2,1)}, u32[]{:S(2)}) copy-start(bf16[1024,640]{1,0:T(8,128)(2,1)} %copy-done) | copy-start | bytes 3932164
  57.1 23.1 %all-to-all-start.2 = ((bf16[8,576,128]{2,1,0:T(8,128)(2,1)}), bf16[8,576,128]{2,1,0:T(8,128)(2,1)S(1)}, u32[]{:S(2)}, u32[]{:S(2)}) async-start(bf16[8,576,128]{2,1,0:T(8,128)(2,1)} %get-tuple-element.23), calls=%async_computation.2 | async-start | bytes 2359296 | tf_op jit(solution)/shard_map/all_to_all | solution.py:262
  66.6 4.0 %collective-permute-start.4 = (bf16[512,640]{1,0:T(8,128)(2,1)S(1)}, bf16[512,640]{1,0:T(8,128)(2,1)S(1)}, u32[]{:S(2)}, u32[]{:S(2)}) collective-permute-start(bf16[512,640]{1,0:T(8,128)(2,1)S(1)} %get-tuple-element.22), channel_id=1, source_target_pairs={{0,16},{16,0},{1,17},{17,1},{2,18},{18,2},{3,19},{19,3},{4,20},{20... | collective-permute-start | bytes 1966088 | tf_op jit(solution)/shard_map/ppermute | solution.py:258
  81.1 20.9 %all-to-all-start.3 = ((bf16[16,8,640]{2,1,0:T(8,128)(2,1)}), bf16[16,8,640]{2,1,0:T(8,128)(2,1)S(1)}, u32[]{:S(2)}, u32[]{:S(2)}) async-start(bf16[16,8,640]{2,1,0:T(8,128)(2,1)} %bitcast.8), calls=%async_computation.3 | async-start | bytes 327680 | tf_op jit(solution)/shard_map/all_to_all | solution.py:262
  89.0 13.6 %collective-permute-start.5 = (bf16[256,640]{1,0:T(8,128)(2,1)S(1)}, bf16[256,640]{1,0:T(8,128)(2,1)S(1)}, u32[]{:S(2)}, u32[]{:S(2)}) collective-permute-start(bf16[256,640]{1,0:T(8,128)(2,1)S(1)} %slice.30), channel_id=1, source_target_pairs={{0,1},{1,0},{2,3},{3,2},{4,5},{5,4},{6,7},{7,6},{8,9},{9,8},{10,11... | collective-permute-start | bytes 983048 | tf_op jit(solution)/shard_map/ppermute | solution.py:258

commit v7 on v6

--- a/solution.py
+++ b/solution.py
@@ -141,14 +141,14 @@
     lax.fori_loop(0, KEYS // TILE, values, 0, unroll=True)
 
 
-def row_factors(place_ref, own_ref, team_ref):
+def row_factors(place_ref, own_ref, here_ref, there_ref):
     core = place_ref[0] // 2
     factors = []
     for k in range(TEAM):
         tops, sums = [], []
-        for y in range(2):
+        for y, team_ref in enumerate((here_ref, there_ref)):
             for c in range(2):
-                spot = 8 * y + ((2 * c + y) ^ k)
+                spot = (2 * c + y) ^ k
                 tops.append(team_ref[core ^ c, spot:spot + 1, :])
                 sums.append(team_ref[core ^ c, TEAM + spot:TEAM + spot + 1, :])
         top = jnp.maximum(jnp.maximum(tops[0], tops[1]), jnp.maximum(tops[2], tops[3]))
@@ -164,11 +164,11 @@
 
 
 def key_kernel(
-    place_ref, own_ref, team_ref, x0, x1, x2, x3, p_ref, t_ref, key_ref, ds_ref,
+    place_ref, own_ref, here_ref, there_ref, x0, x1, x2, x3, p_ref, t_ref, key_ref, ds_ref,
     held_ref, held_ds, sems,
 ):
     blocks = (x0, x1, x2, x3)
-    factors = row_factors(place_ref, own_ref, team_ref)
+    factors = row_factors(place_ref, own_ref, here_ref, there_ref)
 
     def leave(tile):
         part, rows = pl.ds(tile * 2, 2), tile_rows(tile)
@@ -316,10 +316,9 @@
         ),
         1, 5, "scores",
     )(place, pieces, *x)
-    there = swap(stats, "y0")
+    here = lax.all_gather(stats, "c", axis=0, tiled=False)
+    there = swap(here, "y0")
     t = call(value_kernel, square, 0, 6, "values")(lat, *x, p)
-    there, t = lax.optimization_barrier((there, t))
-    team = lax.all_gather(jnp.concatenate([stats, there], axis=0), "c", axis=0, tiled=False)
 
     key_part, ds = pl.pallas_call(
         key_kernel,
@@ -327,7 +326,7 @@
             pltpu.HBM((8, 576, 128), jnp.bfloat16),
             pltpu.HBM((KEYS, TEAM * ROWS), jnp.bfloat16),
         ),
-        in_specs=[SMEM] + whole(8),
+        in_specs=[SMEM] + whole(9),
         out_specs=(pl.BlockSpec(memory_space=pltpu.HBM),) * 2,
         scratch_shapes=[
             pltpu.VMEM((8, 576, 128), jnp.bfloat16),
@@ -336,7 +335,7 @@
         ],
         compiler_params=pltpu.CompilerParams(vmem_limit_bytes=16 * 1024 * 1024),
         name="keys",
-    )(place, tops, team, *x, p, t)
+    )(place, tops, here, there, *x, p, t)
     parts = exchange(key_part, ("x", "zl"))
 
     near, far = pl.pallas_call(

time: 104 us -> 103 us (level)
  no operation moved by 1% of the time
where the time goes in v7:
time: 103 us; the launch traced here: 102 us
  starting transfers between devices  41.9 us (41%)
  waiting for transfers between devices  36.9 us (36%)
  Pallas kernels  15 us (15%)
  local copies, waits for them, and re-layouts  3.86 us (4%)
  blocking collectives  1.81 us (2%)
  other arithmetic  1.52 us (1%)
  between operations  1.46 us (1%)
    all_to_all x4, waiting for transfers between devices, exchange(): return lax.all_to_all(pieces, axes, 0, 0, tiled=True)  29.6 us
    all_to_all x4, starting transfers between devices, exchange(): return lax.all_to_all(pieces, axes, 0, 0, tiled=True)  28.2 us
    ppermute x6, starting transfers between devices, swap(): return lax.ppermute(block, axis, [(0, 1), (1, 0)])  13.7 us
    ppermute x6, waiting for transfers between devices, swap(): return lax.ppermute(block, axis, [(0, 1), (1, 0)])  7.33 us
    pallas_call x1, Pallas kernels, per_device(): pl.pallas_call(key_kernel, out_shape=(pltpu.HBM((8, 576, 128), jnp.bfloat...  4.15 us
    pallas_call x1, Pallas kernels, per_device(): pl.pallas_call(query_kernel, out_shape=(shape((2 * ROWS, WIDE), jnp.float...  3.86 us
    unnamed x12, local copies, waits for them, and re-layouts  3.78 us
    pallas_call x1, Pallas kernels, per_device(): call(score_kernel, (square, shape((2 * TEAM, ROWS), jnp.float32), shape((...  2.54 us
  transfers between devices with their start and end apart: 10, of which 8 were waited for; matrix products, arithmetic and copies ran while one was open for 1% of the time, Pallas kernels for 6%

profile of v7, /device:TPU:8, one launch (start us, length us, event | category | flops | bytes accessed | tf_op | source)
XLA Modules:
  0.0 102.5 jit_solution(6250831750451669268)
XLA Ops:
  0.6 0.0 copy-start.5
  0.6 0.9 copy-done.5
  1.5 0.9 spread.1
  2.4 10.3 %all-to-all-start = ((bf16[4,288,128]{2,1,0:T(8,128)(2,1)}), bf16[4,288,128]{2,1,0:T(8,128)(2,1)S(1)}, u32[]{:S(2)}, u32[]{:S(2)}) async-start(bf16[4,288,128]{2,1,0:T(8,128)(2,1)} %spread.1), calls=%async_computation | async-start | bytes 589824 | tf_op jit(solution)/shard_map/all_to_all | solution.py:262
  13.4 0.0 copy-start.2
  13.4 1.0 copy-done.2
  14.4 0.0 copy-start.3
  14.4 0.9 copy-done.3
  15.3 0.0 copy-start.4
  15.3 0.9 copy-done.4
  16.3 0.3 prep.1.x0
  16.6 2.3 %collective-permute-start = (bf16[256,1152]{1,0:T(8,128)(2,1)S(1)}, bf16[256,1152]{1,0:T(8,128)(2,1)S(1)}, u32[]{:S(2)}, u32[]{:S(2)}) collective-permute-start(bf16[256,1152]{1,0:T(8,128)(2,1)S(1)} %prep.1.x0), channel_id=1, source_target_pairs={{0,1},{1,0},{2,3},{3,2},{4,5},{5,4},{6,7},{7,6},{8,9},{9,8},{10,11... | collective-permute-start | bytes 1769480 | tf_op jit(solution)/shard_map/ppermute | solution.py:258
  18.9 5.6 %all-to-all-done.rows_ref = bf16[4,288,128]{2,1,0:T(8,128)(2,1)S(1)} async-done(((bf16[4,288,128]{2,1,0:T(8,128)(2,1)}), bf16[4,288,128]{2,1,0:T(8,128)(2,1)S(1)}, u32[]{:S(2)}, u32[]{:S(2)}) %all-to-all-start) | async-done | bytes 294944 | tf_op jit(solution)/shard_map/all_to_all | solution.py:262
  24.5 1.1 %copies.1 = bf16[4,4,288,128]{3,2,1,0:T(8,128)(2,1)} custom-call(bf16[4,288,128]{2,1,0:T(8,128)(2,1)S(1)} %all-to-all-done.rows_ref), custom_call_target="tpu_custom_call" | custom-call | tf_op jit(solution)/shard_map/copies/pallas_call | solution.py:285
  25.6 4.3 %all-to-all-start.1 = ((bf16[4,4,288,128]{3,2,1,0:T(8,128)(2,1)}), bf16[4,4,288,128]{3,2,1,0:T(8,128)(2,1)S(1)}, u32[]{:S(2)}, u32[]{:S(2)}) async-start(bf16[4,4,288,128]{3,2,1,0:T(8,128)(2,1)} %copies.1), calls=%async_computation.1 | async-start | bytes 2359296 | tf_op jit(solution)/shard_map/all_to_all | solution.py:262
  29.9 1.9 %collective-permute-start.1 = (bf16[256,1152]{1,0:T(8,128)(2,1)S(1)}, bf16[256,1152]{1,0:T(8,128)(2,1)S(1)}, u32[]{:S(2)}, u32[]{:S(2)}) collective-permute-start(bf16[256,1152]{1,0:T(8,128)(2,1)S(1)} %prep.1.x0), channel_id=1, source_target_pairs={{0,16},{16,0},{1,17},{17,1},{2,18},{18,2},{3,19},{19,3},{4,20},{20... | collective-permute-start | bytes 1769480 | tf_op jit(solution)/shard_map/ppermute | solution.py:258
  31.8 1.4 %collective-permute-done.x1 = bf16[256,1152]{1,0:T(8,128)(2,1)S(1)} collective-permute-done((bf16[256,1152]{1,0:T(8,128)(2,1)S(1)}, bf16[256,1152]{1,0:T(8,128)(2,1)S(1)}, u32[]{:S(2)}, u32[]{:S(2)}) %collective-permute-start) | collective-permute-done | bytes 589856 | tf_op jit(solution)/shard_map/ppermute | solution.py:258
  33.2 1.9 %collective-permute-start.2 = (bf16[256,1152]{1,0:T(8,128)(2,1)S(1)}, bf16[256,1152]{1,0:T(8,128)(2,1)S(1)}, u32[]{:S(2)}, u32[]{:S(2)}) collective-permute-start(bf16[256,1152]{1,0:T(8,128)(2,1)S(1)} %collective-permute-done.x1), channel_id=1, source_target_pairs={{0,16},{16,0},{1,17},{17,1},{2,18},{18,2},{3,19},{19,3},{4,20},{20... | collective-permute-start | bytes 1769480 | tf_op jit(solution)/shard_map/ppermute | solution.py:258
  35.2 0.0 collective-permute-done.1.x2
  35.2 2.0 %collective-permute-done.2.x3 = bf16[256,1152]{1,0:T(8,128)(2,1)S(1)} collective-permute-done((bf16[256,1152]{1,0:T(8,128)(2,1)S(1)}, bf16[256,1152]{1,0:T(8,128)(2,1)S(1)}, u32[]{:S(2)}, u32[]{:S(2)}) %collective-permute-start.2) | collective-permute-done | bytes 589856 | tf_op jit(solution)/shard_map/ppermute | solution.py:258
  37.1 5.9 %all-to-all-done.1 = bf16[4,4,288,128]{3,2,1,0:T(8,128)(2,1)S(1)} async-done(((bf16[4,4,288,128]{3,2,1,0:T(8,128)(2,1)}), bf16[4,4,288,128]{3,2,1,0:T(8,128)(2,1)S(1)}, u32[]{:S(2)}, u32[]{:S(2)}) %all-to-all-start.1) | async-done | bytes 1179680 | tf_op jit(solution)/shard_map/all_to_all | solution.py:262
  43.0 2.5 %scores.1 = (f32[1024,1024]{1,0:T(8,128)S(1)}, f32[8,256]{1,0:T(8,128)S(1)}, bf16[1024,640]{1,0:T(8,128)(2,1)S(1)}, f32[16,256]{1,0:T(8,128)S(1)}) custom-call(s32[1]{0:T(128)} %bitcast.place_ref, bf16[16,288,128]{2,1,0:T(8,128)(2,1)S(1)} %bitcast.11, bf16[256,1152]{1,0:T(8,128)(2,1)S(1)} %prep.1.x0, bf16[256,1152]{1,0:T(8,128)(2,1)S(1)} %collective-permute-done.x1, ...), custom_call_target="tpu_custom_call" | custom-call | tf_op jit(solution)/shard_map/scores/pallas_call | solution.py:309
  45.5 0.0 copy-start
  45.6 1.8 %all-gather = f32[16,256]{1,0:T(8,128)S(1)} all-gather(f32[8,256]{1,0:T(8,128)S(1)} %get-tuple-element.14), channel_id=2, replica_groups=mesh['zh'=4,'x'=4,'c'=2,'zl'=2,'yh'=4,'y0'=2] {'c'}, dimensions={0}, use_global_device_ids=true | all-gather | bytes 24576 | tf_op jit(solution)/shard_map/all_gather | solution.py:319
  47.4 2.3 %collective-permute-start.3 = (f32[2,8,256]{2,1,0:T(8,128)S(1)}, f32[2,8,256]{2,1,0:T(8,128)S(1)}, u32[]{:S(2)}, u32[]{:S(2)}) collective-permute-start(f32[2,8,256]{2,1,0:T(8,128)S(1)} %bitcast.16), channel_id=1, source_target_pairs={{0,1},{1,0},{2,3},{3,2},{4,5},{5,4},{6,7},{7,6},{8,9},{9,8},{10,11... | collective-permute-start | bytes 49160 | tf_op jit(solution)/shard_map/ppermute | solution.py:258
  49.7 1.4 %values.1.t_ref = f32[1024,1024]{1,0:T(8,128)S(1)} custom-call(bf16[1024,640]{1,0:T(8,128)(2,1)S(1)} %get-tuple-element.12.lat_ref, bf16[256,1152]{1,0:T(8,128)(2,1)S(1)} %prep.1.x0, bf16[256,1152]{1,0:T(8,128)(2,1)S(1)} %collective-permute-done.x1, bf16[256,1152]{1,0:T(8,128)(2,1)S(1)} %collective-permute-done.1.x2, ...), custom_call_target="tpu_custom_call" | custom-call | tf_op jit(solution)/shard_map/values/pallas_call | solution.py:321
  51.1 0.0 copy-done
  51.1 1.9 %collective-permute-done.3.there_ref = f32[2,8,256]{2,1,0:T(8,128)S(1)} collective-permute-done((f32[2,8,256]{2,1,0:T(8,128)S(1)}, f32[2,8,256]{2,1,0:T(8,128)S(1)}, u32[]{:S(2)}, u32[]{:S(2)}) %collective-permute-start.3) | collective-permute-done | bytes 16416 | tf_op jit(solution)/shard_map/ppermute | solution.py:258
  53.0 4.2 %keys.1 = (bf16[8,576,128]{2,1,0:T(8,128)(2,1)}, bf16[1024,1024]{1,0:T(8,128)(2,1)}) custom-call(s32[1]{0:T(128)} %bitcast.place_ref, f32[16,256]{1,0:T(8,128)S(1)} %get-tuple-element.13.own_ref, f32[2,8,256]{2,1,0:T(8,128)S(1)} %bitcast.17, f32[2,8,256]{2,1,0:T(8,128)S(1)} %collective-permute-done.3.there_ref, bf16[256,1152]{1,0:T(8,128)(2,1)S(1)} %prep.1.x0, ...), custom_call_target="tpu_custom_call" | custom-call | tf_op jit(solution)/shard_map/keys/pallas_call | solution.py:323
  57.1 0.0 copy-start.1
  57.2 5.6 %all-to-all-start.2 = ((bf16[8,576,128]{2,1,0:T(8,128)(2,1)}), bf16[8,576,128]{2,1,0:T(8,128)(2,1)S(1)}, u32[]{:S(2)}, u32[]{:S(2)}) async-start(bf16[8,576,128]{2,1,0:T(8,128)(2,1)} %get-tuple-element.19), calls=%async_computation.2 | async-start | bytes 2359296 | tf_op jit(solution)/shard_map/all_to_all | solution.py:262
  62.8 0.0 copy-done.1
  62.8 3.9 %query.1 = (f32[512,640]{1,0:T(8,128)S(1)}, bf16[512,640]{1,0:T(8,128)(2,1)S(1)}) custom-call(bf16[1024,640]{1,0:T(8,128)(2,1)S(1)} %copy-done.1, bf16[1024,1024]{1,0:T(8,128)(2,1)} %get-tuple-element.16.ds_ref), custom_call_target="tpu_custom_call" | custom-call | tf_op jit(solution)/shard_map/query/pallas_call | solution.py:341
  66.7 1.9 %collective-permute-start.4 = (bf16[512,640]{1,0:T(8,128)(2,1)S(1)}, bf16[512,640]{1,0:T(8,128)(2,1)S(1)}, u32[]{:S(2)}, u32[]{:S(2)}) collective-permute-start(bf16[512,640]{1,0:T(8,128)(2,1)S(1)} %get-tuple-element.18), channel_id=1, source_target_pairs={{0,16},{16,0},{1,17},{17,1},{2,18},{18,2},{3,19},{19,3},{4,20},{20... | collective-permute-start | bytes 1966088 | tf_op jit(solution)/shard_map/ppermute | solution.py:258
  68.6 2.1 %collective-permute-done.4 = bf16[512,640]{1,0:T(8,128)(2,1)S(1)} collective-permute-done((bf16[512,640]{1,0:T(8,128)(2,1)S(1)}, bf16[512,640]{1,0:T(8,128)(2,1)S(1)}, u32[]{:S(2)}, u32[]{:S(2)}) %collective-permute-start.4) | collective-permute-done | bytes 655392 | tf_op jit(solution)/shard_map/ppermute | solution.py:258
  70.7 0.1 convert_add_fusion
  70.8 8.3 %all-to-all-done.2.part_ref = bf16[8,576,128]{2,1,0:T(8,128)(2,1)S(1)} async-done(((bf16[8,576,128]{2,1,0:T(8,128)(2,1)}), bf16[8,576,128]{2,1,0:T(8,128)(2,1)S(1)}, u32[]{:S(2)}, u32[]{:S(2)}) %all-to-all-start.2) | async-done | bytes 1179680 | tf_op jit(solution)/shard_map/all_to_all | solution.py:262
  79.1 0.8 sum.1
  79.9 8.0 %all-to-all-start.3 = ((bf16[16,8,640]{2,1,0:T(8,128)(2,1)}), bf16[16,8,640]{2,1,0:T(8,128)(2,1)S(1)}, u32[]{:S(2)}, u32[]{:S(2)}) async-start(bf16[16,8,640]{2,1,0:T(8,128)(2,1)} %bitcast.8), calls=%async_computation.3 | async-start | bytes 327680 | tf_op jit(solution)/shard_map/all_to_all | solution.py:262
  87.9 3.3 %collective-permute-start.5 = (bf16[256,640]{1,0:T(8,128)(2,1)S(1)}, bf16[256,640]{1,0:T(8,128)(2,1)S(1)}, u32[]{:S(2)}, u32[]{:S(2)}) collective-permute-start(bf16[256,640]{1,0:T(8,128)(2,1)S(1)} %slice.30), channel_id=1, source_target_pairs={{0,1},{1,0},{2,3},{3,2},{4,5},{5,4},{6,7},{7,6},{8,9},{9,8},{10,11... | collective-permute-start | bytes 983048 | tf_op jit(solution)/shard_map/ppermute | solution.py:258
  91.2 9.8 %all-to-all-done.3 = bf16[16,8,640]{2,1,0:T(8,128)(2,1)S(1)} async-done(((bf16[16,8,640]{2,1,0:T(8,128)(2,1)}), bf16[16,8,640]{2,1,0:T(8,128)(2,1)S(1)}, u32[]{:S(2)}, u32[]{:S(2)}) %all-to-all-start.3) | async-done | bytes 163872 | tf_op jit(solution)/shard_map/all_to_all | solution.py:262
  101.1 0.6 convert_reduce_fusion
  101.7 0.0 collective-permute-done.5
  101.7 0.8 fusion.1
  (2 shorter events, 0.1 us)
Async XLA Ops:
  0.6 0.9 copy-start.5
  2.4 22.1 %all-to-all-start = ((bf16[4,288,128]{2,1,0:T(8,128)(2,1)}), bf16[4,288,128]{2,1,0:T(8,128)(2,1)S(1)}, u32[]{:S(2)}, u32[]{:S(2)}) async-start(bf16[4,288,128]{2,1,0:T(8,128)(2,1)} %spread.1), calls=%async_computation | async-start | bytes 589824 | tf_op jit(solution)/shard_map/all_to_all | solution.py:262
  13.4 1.0 copy-start.2
  14.4 0.9 copy-start.3
  15.3 0.9 copy-start.4
  16.6 16.7 %collective-permute-start = (bf16[256,1152]{1,0:T(8,128)(2,1)S(1)}, bf16[256,1152]{1,0:T(8,128)(2,1)S(1)}, u32[]{:S(2)}, u32[]{:S(2)}) collective-permute-start(bf16[256,1152]{1,0:T(8,128)(2,1)S(1)} %prep.1.x0), channel_id=1, source_target_pairs={{0,1},{1,0},{2,3},{3,2},{4,5},{5,4},{6,7},{7,6},{8,9},{9,8},{10,11... | collective-permute-start | bytes 1769480 | tf_op jit(solution)/shard_map/ppermute | solution.py:258
  25.6 17.4 %all-to-all-start.1 = ((bf16[4,4,288,128]{3,2,1,0:T(8,128)(2,1)}), bf16[4,4,288,128]{3,2,1,0:T(8,128)(2,1)S(1)}, u32[]{:S(2)}, u32[]{:S(2)}) async-start(bf16[4,4,288,128]{3,2,1,0:T(8,128)(2,1)} %copies.1), calls=%async_computation.1 | async-start | bytes 2359296 | tf_op jit(solution)/shard_map/all_to_all | solution.py:262
  29.9 5.3 %collective-permute-start.1 = (bf16[256,1152]{1,0:T(8,128)(2,1)S(1)}, bf16[256,1152]{1,0:T(8,128)(2,1)S(1)}, u32[]{:S(2)}, u32[]{:S(2)}) collective-permute-start(bf16[256,1152]{1,0:T(8,128)(2,1)S(1)} %prep.1.x0), channel_id=1, source_target_pairs={{0,16},{16,0},{1,17},{17,1},{2,18},{18,2},{3,19},{19,3},{4,20},{20... | collective-permute-start | bytes 1769480 | tf_op jit(solution)/shard_map/ppermute | solution.py:258
  33.2 3.9 %collective-permute-start.2 = (bf16[256,1152]{1,0:T(8,128)(2,1)S(1)}, bf16[256,1152]{1,0:T(8,128)(2,1)S(1)}, u32[]{:S(2)}, u32[]{:S(2)}) collective-permute-start(bf16[256,1152]{1,0:T(8,128)(2,1)S(1)} %collective-permute-done.x1), channel_id=1, source_target_pairs={{0,16},{16,0},{1,17},{17,1},{2,18},{18,2},{3,19},{19,3},{4,20},{20... | collective-permute-start | bytes 1769480 | tf_op jit(solution)/shard_map/ppermute | solution.py:258
  45.5 5.5 %copy-start = (bf16[1024,640]{1,0:T(8,128)(2,1)}, bf16[1024,640]{1,0:T(8,128)(2,1)S(1)}, u32[]{:S(2)}) copy-start(bf16[1024,640]{1,0:T(8,128)(2,1)S(1)} %get-tuple-element.12.lat_ref) | copy-start | bytes 3932164
  47.4 5.6 %collective-permute-start.3 = (f32[2,8,256]{2,1,0:T(8,128)S(1)}, f32[2,8,256]{2,1,0:T(8,128)S(1)}, u32[]{:S(2)}, u32[]{:S(2)}) collective-permute-start(f32[2,8,256]{2,1,0:T(8,128)S(1)} %bitcast.16), channel_id=1, source_target_pairs={{0,1},{1,0},{2,3},{3,2},{4,5},{5,4},{6,7},{7,6},{8,9},{9,8},{10,11... | collective-permute-start | bytes 49160 | tf_op jit(solution)/shard_map/ppermute | solution.py:258
  57.1 5.7 %copy-start.1 = (bf16[1024,640]{1,0:T(8,128)(2,1)S(1)}, bf16[1024,640]{1,0:T(8,128)(2,1)}, u32[]{:S(2)}) copy-start(bf16[1024,640]{1,0:T(8,128)(2,1)} %copy-done) | copy-start | bytes 3932164
  57.2 22.0 %all-to-all-start.2 = ((bf16[8,576,128]{2,1,0:T(8,128)(2,1)}), bf16[8,576,128]{2,1,0:T(8,128)(2,1)S(1)}, u32[]{:S(2)}, u32[]{:S(2)}) async-start(bf16[8,576,128]{2,1,0:T(8,128)(2,1)} %get-tuple-element.19), calls=%async_computation.2 | async-start | bytes 2359296 | tf_op jit(solution)/shard_map/all_to_all | solution.py:262
  66.7 4.0 %collective-permute-start.4 = (bf16[512,640]{1,0:T(8,128)(2,1)S(1)}, bf16[512,640]{1,0:T(8,128)(2,1)S(1)}, u32[]{:S(2)}, u32[]{:S(2)}) collective-permute-start(bf16[512,640]{1,0:T(8,128)(2,1)S(1)} %get-tuple-element.18), channel_id=1, source_target_pairs={{0,16},{16,0},{1,17},{17,1},{2,18},{18,2},{3,19},{19,3},{4,20},{20... | collective-permute-start | bytes 1966088 | tf_op jit(solution)/shard_map/ppermute | solution.py:258
  79.9 21.1 %all-to-all-start.3 = ((bf16[16,8,640]{2,1,0:T(8,128)(2,1)}), bf16[16,8,640]{2,1,0:T(8,128)(2,1)S(1)}, u32[]{:S(2)}, u32[]{:S(2)}) async-start(bf16[16,8,640]{2,1,0:T(8,128)(2,1)} %bitcast.8), calls=%async_computation.3 | async-start | bytes 327680 | tf_op jit(solution)/shard_map/all_to_all | solution.py:262
  87.9 13.8 %collective-permute-start.5 = (bf16[256,640]{1,0:T(8,128)(2,1)S(1)}, bf16[256,640]{1,0:T(8,128)(2,1)S(1)}, u32[]{:S(2)}, u32[]{:S(2)}) collective-permute-start(bf16[256,640]{1,0:T(8,128)(2,1)S(1)} %slice.30), channel_id=1, source_target_pairs={{0,1},{1,0},{2,3},{3,2},{4,5},{5,4},{6,7},{7,6},{8,9},{9,8},{10,11... | collective-permute-start | bytes 983048 | tf_op jit(solution)/shard_map/ppermute | solution.py:258

commit v8 on v7

--- a/solution.py
+++ b/solution.py
@@ -24,7 +24,15 @@
 SIZES = (4, 4, 2, 2, 4, 2)
 
 
-def prep_kernel(start_ref, q_ref, do_ref, lo_ref, out_ref):
+def prep_kernel(start_ref, far_q, far_do, far_lo, out_ref, q_ref, do_ref, lo_ref, sems):
+    copies = [
+        pltpu.make_async_copy(far, near, sems.at[i])
+        for i, (far, near) in enumerate(((far_q, q_ref), (far_do, do_ref), (far_lo, lo_ref)))
+    ]
+    for copy in copies:
+        copy.start()
+    for copy in copies:
+        copy.wait()
     grad = do_ref[...]
     delta = jnp.sum(
         grad.astype(jnp.float32) * lo_ref[...].astype(jnp.float32), axis=1, keepdims=True
@@ -294,12 +302,24 @@
     pieces = exchange(pieces, ("x",))
     pieces = pieces.reshape(16, FOLD, 128)
 
-    x0 = call(prep_kernel, shape((ROWS, PACK), jnp.bfloat16), 1, 3, "prep")(
-        query_start,
-        queries.reshape(ROWS, 576),
-        out_grad.reshape(ROWS, VALUES),
-        layer_out.reshape(ROWS, VALUES),
-    )
+    own = [
+        pltpu.with_memory_space_constraint(array, pltpu.HBM)
+        for array in (
+            queries.reshape(ROWS, 576),
+            out_grad.reshape(ROWS, VALUES),
+            layer_out.reshape(ROWS, VALUES),
+        )
+    ]
+    x0 = pl.pallas_call(
+        prep_kernel,
+        out_shape=shape((ROWS, PACK), jnp.bfloat16),
+        in_specs=[SMEM] + [pl.BlockSpec(memory_space=pltpu.HBM)] * 3,
+        out_specs=whole(1)[0],
+        scratch_shapes=[pltpu.VMEM(array.shape, array.dtype) for array in own]
+        + [pltpu.SemaphoreType.DMA((3,))],
+        compiler_params=pltpu.CompilerParams(vmem_limit_bytes=16 * 1024 * 1024),
+        name="prep",
+    )(query_start, *own)
     x1 = swap(x0, "y0")
     x2 = swap(x0, "c")
     x3 = swap(x1, "c")

time: 103 us -> 103 us (level)
  local copies, waits for them, and re-layouts: 3.86 us -> 0.99 us
  waiting for transfers between devices: 36.9 us -> 38.1 us
  Pallas kernels: 15 us -> 16.2 us
    all_to_all x4, waiting for transfers between devices: 29.6 us -> 32.5 us  [exchange(): return lax.all_to_all(pieces, axes, 0, 0, tiled=True)]
    unnamed x12 -> x6, local copies, waits for them, and re-layouts: 3.78 us -> 0.91 us
    ppermute x6, waiting for transfers between devices: 7.33 us -> 5.55 us  [swap(): return lax.ppermute(block, axis, [(0, 1), (1, 0)])]
    pallas_call x1, Pallas kernels: 0.3 us -> 1.47 us  [per_device(): pl.pallas_call(prep_kernel, out_shape=shape((ROWS, PACK), jnp.bfloat16),...]
  transfers between devices with their start and end apart: 10 -> 10, of which waited for: 8 -> 7; matrix products, arithmetic and copies ran while one was open for 1% -> 1% of each run, Pallas kernels for 6% -> 8%
where the time goes in v8:
time: 103 us; the launch traced here: 102 us
  starting transfers between devices  42.4 us (41%)
  waiting for transfers between devices  38.1 us (37%)
  Pallas kernels  16.2 us (16%)
  blocking collectives  1.81 us (2%)
  other arithmetic  1.52 us (1%)
  between operations  1.46 us (1%)
    all_to_all x4, waiting for transfers between devices, exchange(): return lax.all_to_all(pieces, axes, 0, 0, tiled=True)  32.5 us
    all_to_all x4, starting transfers between devices, exchange(): return lax.all_to_all(pieces, axes, 0, 0, tiled=True)  28.2 us
    ppermute x6, starting transfers between devices, swap(): return lax.ppermute(block, axis, [(0, 1), (1, 0)])  14.2 us
    ppermute x6, waiting for transfers between devices, swap(): return lax.ppermute(block, axis, [(0, 1), (1, 0)])  5.55 us
    pallas_call x1, Pallas kernels, per_device(): pl.pallas_call(key_kernel, out_shape=(pltpu.HBM((8, 576, 128), jnp.bfloat...  4.17 us
    pallas_call x1, Pallas kernels, per_device(): pl.pallas_call(query_kernel, out_shape=(shape((2 * ROWS, WIDE), jnp.float...  3.86 us
    pallas_call x1, Pallas kernels, per_device(): call(score_kernel, (square, shape((2 * TEAM, ROWS), jnp.float32), shape((...  2.53 us
  transfers between devices with their start and end apart: 10, of which 7 were waited for; matrix products, arithmetic and copies ran while one was open for 1% of the time, Pallas kernels for 8%

profile of v8, /device:TPU:8, one launch (start us, length us, event | category | flops | bytes accessed | tf_op | source)
XLA Modules:
  0.0 102.5 jit_solution(1239323706715914176)
XLA Ops:
  0.6 0.0 copy-start.2
  0.6 0.9 copy-done.2
  1.5 0.9 spread.1
  2.4 10.3 %all-to-all-start = ((bf16[4,288,128]{2,1,0:T(8,128)(2,1)}), bf16[4,288,128]{2,1,0:T(8,128)(2,1)S(1)}, u32[]{:S(2)}, u32[]{:S(2)}) async-start(bf16[4,288,128]{2,1,0:T(8,128)(2,1)} %spread.1), calls=%async_computation | async-start | bytes 589824 | tf_op jit(solution)/shard_map/all_to_all | solution.py:270
  13.4 1.5 %prep.1.x0 = bf16[256,1152]{1,0:T(8,128)(2,1)S(1)} custom-call(s32[1]{0:T(128)S(6)} %copy.7.start_ref, bf16[256,576]{1,0:T(8,128)(2,1)} %bitcast.15, bf16[256,512]{1,0:T(8,128)(2,1)} %bitcast.16, bf16[256,512]{1,0:T(8,128)(2,1)} %bitcast.17), custom_call_target="tpu_custom_call" | custom-call | tf_op jit(solution)/shard_map/prep/pallas_call | solution.py:313
  14.9 2.4 %collective-permute-start = (bf16[256,1152]{1,0:T(8,128)(2,1)S(1)}, bf16[256,1152]{1,0:T(8,128)(2,1)S(1)}, u32[]{:S(2)}, u32[]{:S(2)}) collective-permute-start(bf16[256,1152]{1,0:T(8,128)(2,1)S(1)} %prep.1.x0), channel_id=1, source_target_pairs={{0,1},{1,0},{2,3},{3,2},{4,5},{5,4},{6,7},{7,6},{8,9},{9,8},{10,11... | collective-permute-start | bytes 1769480 | tf_op jit(solution)/shard_map/ppermute | solution.py:266
  17.2 7.3 %all-to-all-done.rows_ref = bf16[4,288,128]{2,1,0:T(8,128)(2,1)S(1)} async-done(((bf16[4,288,128]{2,1,0:T(8,128)(2,1)}), bf16[4,288,128]{2,1,0:T(8,128)(2,1)S(1)}, u32[]{:S(2)}, u32[]{:S(2)}) %all-to-all-start) | async-done | bytes 294944 | tf_op jit(solution)/shard_map/all_to_all | solution.py:270
  24.5 1.1 %copies.1 = bf16[4,4,288,128]{3,2,1,0:T(8,128)(2,1)} custom-call(bf16[4,288,128]{2,1,0:T(8,128)(2,1)S(1)} %all-to-all-done.rows_ref), custom_call_target="tpu_custom_call" | custom-call | tf_op jit(solution)/shard_map/copies/pallas_call | solution.py:293
  25.6 4.3 %all-to-all-start.1 = ((bf16[4,4,288,128]{3,2,1,0:T(8,128)(2,1)}), bf16[4,4,288,128]{3,2,1,0:T(8,128)(2,1)S(1)}, u32[]{:S(2)}, u32[]{:S(2)}) async-start(bf16[4,4,288,128]{3,2,1,0:T(8,128)(2,1)} %copies.1), calls=%async_computation.1 | async-start | bytes 2359296 | tf_op jit(solution)/shard_map/all_to_all | solution.py:270
  29.9 1.9 %collective-permute-start.1 = (bf16[256,1152]{1,0:T(8,128)(2,1)S(1)}, bf16[256,1152]{1,0:T(8,128)(2,1)S(1)}, u32[]{:S(2)}, u32[]{:S(2)}) collective-permute-start(bf16[256,1152]{1,0:T(8,128)(2,1)S(1)} %prep.1.x0), channel_id=1, source_target_pairs={{0,16},{16,0},{1,17},{17,1},{2,18},{18,2},{3,19},{19,3},{4,20},{20... | collective-permute-start | bytes 1769480 | tf_op jit(solution)/shard_map/ppermute | solution.py:266
  31.8 0.0 collective-permute-done.x1
  31.8 2.4 %collective-permute-start.2 = (bf16[256,1152]{1,0:T(8,128)(2,1)S(1)}, bf16[256,1152]{1,0:T(8,128)(2,1)S(1)}, u32[]{:S(2)}, u32[]{:S(2)}) collective-permute-start(bf16[256,1152]{1,0:T(8,128)(2,1)S(1)} %collective-permute-done.x1), channel_id=1, source_target_pairs={{0,16},{16,0},{1,17},{17,1},{2,18},{18,2},{3,19},{19,3},{4,20},{20... | collective-permute-start | bytes 1769480 | tf_op jit(solution)/shard_map/ppermute | solution.py:266
  34.2 0.0 collective-permute-done.1.x2
  34.3 1.6 %collective-permute-done.2.x3 = bf16[256,1152]{1,0:T(8,128)(2,1)S(1)} collective-permute-done((bf16[256,1152]{1,0:T(8,128)(2,1)S(1)}, bf16[256,1152]{1,0:T(8,128)(2,1)S(1)}, u32[]{:S(2)}, u32[]{:S(2)}) %collective-permute-start.2) | collective-permute-done | bytes 589856 | tf_op jit(solution)/shard_map/ppermute | solution.py:266
  35.9 7.2 %all-to-all-done.1 = bf16[4,4,288,128]{3,2,1,0:T(8,128)(2,1)S(1)} async-done(((bf16[4,4,288,128]{3,2,1,0:T(8,128)(2,1)}), bf16[4,4,288,128]{3,2,1,0:T(8,128)(2,1)S(1)}, u32[]{:S(2)}, u32[]{:S(2)}) %all-to-all-start.1) | async-done | bytes 1179680 | tf_op jit(solution)/shard_map/all_to_all | solution.py:270
  43.0 2.5 %scores.1 = (f32[1024,1024]{1,0:T(8,128)S(1)}, f32[8,256]{1,0:T(8,128)S(1)}, bf16[1024,640]{1,0:T(8,128)(2,1)S(1)}, f32[16,256]{1,0:T(8,128)S(1)}) custom-call(s32[1]{0:T(128)} %bitcast.place_ref, bf16[16,288,128]{2,1,0:T(8,128)(2,1)S(1)} %bitcast.11, bf16[256,1152]{1,0:T(8,128)(2,1)S(1)} %prep.1.x0, bf16[256,1152]{1,0:T(8,128)(2,1)S(1)} %collective-permute-done.x1, ...), custom_call_target="tpu_custom_call" | custom-call | tf_op jit(solution)/shard_map/scores/pallas_call | solution.py:329
  45.5 0.0 copy-start
  45.5 1.8 %all-gather = f32[16,256]{1,0:T(8,128)S(1)} all-gather(f32[8,256]{1,0:T(8,128)S(1)} %get-tuple-element.14), channel_id=2, replica_groups=mesh['zh'=4,'x'=4,'c'=2,'zl'=2,'yh'=4,'y0'=2] {'c'}, dimensions={0}, use_global_device_ids=true | all-gather | bytes 24576 | tf_op jit(solution)/shard_map/all_gather | solution.py:339
  47.4 2.4 %collective-permute-start.3 = (f32[2,8,256]{2,1,0:T(8,128)S(1)}, f32[2,8,256]{2,1,0:T(8,128)S(1)}, u32[]{:S(2)}, u32[]{:S(2)}) collective-permute-start(f32[2,8,256]{2,1,0:T(8,128)S(1)} %bitcast.13), channel_id=1, source_target_pairs={{0,1},{1,0},{2,3},{3,2},{4,5},{5,4},{6,7},{7,6},{8,9},{9,8},{10,11... | collective-permute-start | bytes 49160 | tf_op jit(solution)/shard_map/ppermute | solution.py:266
  49.7 1.4 %values.1.t_ref = f32[1024,1024]{1,0:T(8,128)S(1)} custom-call(bf16[1024,640]{1,0:T(8,128)(2,1)S(1)} %get-tuple-element.12.lat_ref, bf16[256,1152]{1,0:T(8,128)(2,1)S(1)} %prep.1.x0, bf16[256,1152]{1,0:T(8,128)(2,1)S(1)} %collective-permute-done.x1, bf16[256,1152]{1,0:T(8,128)(2,1)S(1)} %collective-permute-done.1.x2, ...), custom_call_target="tpu_custom_call" | custom-call | tf_op jit(solution)/shard_map/values/pallas_call | solution.py:341
  51.1 0.0 copy-done
  51.1 1.9 %collective-permute-done.3.there_ref = f32[2,8,256]{2,1,0:T(8,128)S(1)} collective-permute-done((f32[2,8,256]{2,1,0:T(8,128)S(1)}, f32[2,8,256]{2,1,0:T(8,128)S(1)}, u32[]{:S(2)}, u32[]{:S(2)}) %collective-permute-start.3) | collective-permute-done | bytes 16416 | tf_op jit(solution)/shard_map/ppermute | solution.py:266
  53.0 4.2 %keys.1 = (bf16[8,576,128]{2,1,0:T(8,128)(2,1)}, bf16[1024,1024]{1,0:T(8,128)(2,1)}) custom-call(s32[1]{0:T(128)} %bitcast.place_ref, f32[16,256]{1,0:T(8,128)S(1)} %get-tuple-element.13.own_ref, f32[2,8,256]{2,1,0:T(8,128)S(1)} %bitcast.14, f32[2,8,256]{2,1,0:T(8,128)S(1)} %collective-permute-done.3.there_ref, bf16[256,1152]{1,0:T(8,128)(2,1)S(1)} %prep.1.x0, ...), custom_call_target="tpu_custom_call" | custom-call | tf_op jit(solution)/shard_map/keys/pallas_call | solution.py:343
  57.2 0.0 copy-start.1
  57.2 5.7 %all-to-all-start.2 = ((bf16[8,576,128]{2,1,0:T(8,128)(2,1)}), bf16[8,576,128]{2,1,0:T(8,128)(2,1)S(1)}, u32[]{:S(2)}, u32[]{:S(2)}) async-start(bf16[8,576,128]{2,1,0:T(8,128)(2,1)} %get-tuple-element.19), calls=%async_computation.2 | async-start | bytes 2359296 | tf_op jit(solution)/shard_map/all_to_all | solution.py:270
  62.8 0.0 copy-done.1
  62.8 3.9 %query.1 = (f32[512,640]{1,0:T(8,128)S(1)}, bf16[512,640]{1,0:T(8,128)(2,1)S(1)}) custom-call(bf16[1024,640]{1,0:T(8,128)(2,1)S(1)} %copy-done.1, bf16[1024,1024]{1,0:T(8,128)(2,1)} %get-tuple-element.16.ds_ref), custom_call_target="tpu_custom_call" | custom-call | tf_op jit(solution)/shard_map/query/pallas_call | solution.py:361
  66.7 1.9 %collective-permute-start.4 = (bf16[512,640]{1,0:T(8,128)(2,1)S(1)}, bf16[512,640]{1,0:T(8,128)(2,1)S(1)}, u32[]{:S(2)}, u32[]{:S(2)}) collective-permute-start(bf16[512,640]{1,0:T(8,128)(2,1)S(1)} %get-tuple-element.18), channel_id=1, source_target_pairs={{0,16},{16,0},{1,17},{17,1},{2,18},{18,2},{3,19},{19,3},{4,20},{20... | collective-permute-start | bytes 1966088 | tf_op jit(solution)/shard_map/ppermute | solution.py:266
  68.6 2.1 %collective-permute-done.4 = bf16[512,640]{1,0:T(8,128)(2,1)S(1)} collective-permute-done((bf16[512,640]{1,0:T(8,128)(2,1)S(1)}, bf16[512,640]{1,0:T(8,128)(2,1)S(1)}, u32[]{:S(2)}, u32[]{:S(2)}) %collective-permute-start.4) | collective-permute-done | bytes 655392 | tf_op jit(solution)/shard_map/ppermute | solution.py:266
  70.7 0.1 convert_add_fusion
  70.8 8.3 %all-to-all-done.2.part_ref = bf16[8,576,128]{2,1,0:T(8,128)(2,1)S(1)} async-done(((bf16[8,576,128]{2,1,0:T(8,128)(2,1)}), bf16[8,576,128]{2,1,0:T(8,128)(2,1)S(1)}, u32[]{:S(2)}, u32[]{:S(2)}) %all-to-all-start.2) | async-done | bytes 1179680 | tf_op jit(solution)/shard_map/all_to_all | solution.py:270
  79.1 0.8 sum.1
  80.0 7.9 %all-to-all-start.3 = ((bf16[16,8,640]{2,1,0:T(8,128)(2,1)}), bf16[16,8,640]{2,1,0:T(8,128)(2,1)S(1)}, u32[]{:S(2)}, u32[]{:S(2)}) async-start(bf16[16,8,640]{2,1,0:T(8,128)(2,1)} %bitcast.8), calls=%async_computation.3 | async-start | bytes 327680 | tf_op jit(solution)/shard_map/all_to_all | solution.py:270
  87.9 3.3 %collective-permute-start.5 = (bf16[256,640]{1,0:T(8,128)(2,1)S(1)}, bf16[256,640]{1,0:T(8,128)(2,1)S(1)}, u32[]{:S(2)}, u32[]{:S(2)}) collective-permute-start(bf16[256,640]{1,0:T(8,128)(2,1)S(1)} %slice.30), channel_id=1, source_target_pairs={{0,1},{1,0},{2,3},{3,2},{4,5},{5,4},{6,7},{7,6},{8,9},{9,8},{10,11... | collective-permute-start | bytes 983048 | tf_op jit(solution)/shard_map/ppermute | solution.py:266
  91.2 9.8 %all-to-all-done.3 = bf16[16,8,640]{2,1,0:T(8,128)(2,1)S(1)} async-done(((bf16[16,8,640]{2,1,0:T(8,128)(2,1)}), bf16[16,8,640]{2,1,0:T(8,128)(2,1)S(1)}, u32[]{:S(2)}, u32[]{:S(2)}) %all-to-all-start.3) | async-done | bytes 163872 | tf_op jit(solution)/shard_map/all_to_all | solution.py:270
  101.1 0.6 convert_reduce_fusion
  101.7 0.0 collective-permute-done.5
  101.7 0.8 fusion.1
  (2 shorter events, 0.1 us)
Async XLA Ops:
  0.6 0.9 copy-start.2
  2.4 22.1 %all-to-all-start = ((bf16[4,288,128]{2,1,0:T(8,128)(2,1)}), bf16[4,288,128]{2,1,0:T(8,128)(2,1)S(1)}, u32[]{:S(2)}, u32[]{:S(2)}) async-start(bf16[4,288,128]{2,1,0:T(8,128)(2,1)} %spread.1), calls=%async_computation | async-start | bytes 589824 | tf_op jit(solution)/shard_map/all_to_all | solution.py:270
  14.9 17.0 %collective-permute-start = (bf16[256,1152]{1,0:T(8,128)(2,1)S(1)}, bf16[256,1152]{1,0:T(8,128)(2,1)S(1)}, u32[]{:S(2)}, u32[]{:S(2)}) collective-permute-start(bf16[256,1152]{1,0:T(8,128)(2,1)S(1)} %prep.1.x0), channel_id=1, source_target_pairs={{0,1},{1,0},{2,3},{3,2},{4,5},{5,4},{6,7},{7,6},{8,9},{9,8},{10,11... | collective-permute-start | bytes 1769480 | tf_op jit(solution)/shard_map/ppermute | solution.py:266
  25.6 17.4 %all-to-all-start.1 = ((bf16[4,4,288,128]{3,2,1,0:T(8,128)(2,1)}), bf16[4,4,288,128]{3,2,1,0:T(8,128)(2,1)S(1)}, u32[]{:S(2)}, u32[]{:S(2)}) async-start(bf16[4,4,288,128]{3,2,1,0:T(8,128)(2,1)} %copies.1), calls=%async_computation.1 | async-start | bytes 2359296 | tf_op jit(solution)/shard_map/all_to_all | solution.py:270
  29.9 4.3 %collective-permute-start.1 = (bf16[256,1152]{1,0:T(8,128)(2,1)S(1)}, bf16[256,1152]{1,0:T(8,128)(2,1)S(1)}, u32[]{:S(2)}, u32[]{:S(2)}) collective-permute-start(bf16[256,1152]{1,0:T(8,128)(2,1)S(1)} %prep.1.x0), channel_id=1, source_target_pairs={{0,16},{16,0},{1,17},{17,1},{2,18},{18,2},{3,19},{19,3},{4,20},{20... | collective-permute-start | bytes 1769480 | tf_op jit(solution)/shard_map/ppermute | solution.py:266
  31.8 4.0 %collective-permute-start.2 = (bf16[256,1152]{1,0:T(8,128)(2,1)S(1)}, bf16[256,1152]{1,0:T(8,128)(2,1)S(1)}, u32[]{:S(2)}, u32[]{:S(2)}) collective-permute-start(bf16[256,1152]{1,0:T(8,128)(2,1)S(1)} %collective-permute-done.x1), channel_id=1, source_target_pairs={{0,16},{16,0},{1,17},{17,1},{2,18},{18,2},{3,19},{19,3},{4,20},{20... | collective-permute-start | bytes 1769480 | tf_op jit(solution)/shard_map/ppermute | solution.py:266
  45.5 5.6 %copy-start = (bf16[1024,640]{1,0:T(8,128)(2,1)}, bf16[1024,640]{1,0:T(8,128)(2,1)S(1)}, u32[]{:S(2)}) copy-start(bf16[1024,640]{1,0:T(8,128)(2,1)S(1)} %get-tuple-element.12.lat_ref) | copy-start | bytes 3932164
  47.4 5.6 %collective-permute-start.3 = (f32[2,8,256]{2,1,0:T(8,128)S(1)}, f32[2,8,256]{2,1,0:T(8,128)S(1)}, u32[]{:S(2)}, u32[]{:S(2)}) collective-permute-start(f32[2,8,256]{2,1,0:T(8,128)S(1)} %bitcast.13), channel_id=1, source_target_pairs={{0,1},{1,0},{2,3},{3,2},{4,5},{5,4},{6,7},{7,6},{8,9},{9,8},{10,11... | collective-permute-start | bytes 49160 | tf_op jit(solution)/shard_map/ppermute | solution.py:266
  57.2 5.7 %copy-start.1 = (bf16[1024,640]{1,0:T(8,128)(2,1)S(1)}, bf16[1024,640]{1,0:T(8,128)(2,1)}, u32[]{:S(2)}) copy-start(bf16[1024,640]{1,0:T(8,128)(2,1)} %copy-done) | copy-start | bytes 3932164
  57.2 22.0 %all-to-all-start.2 = ((bf16[8,576,128]{2,1,0:T(8,128)(2,1)}), bf16[8,576,128]{2,1,0:T(8,128)(2,1)S(1)}, u32[]{:S(2)}, u32[]{:S(2)}) async-start(bf16[8,576,128]{2,1,0:T(8,128)(2,1)} %get-tuple-element.19), calls=%async_computation.2 | async-start | bytes 2359296 | tf_op jit(solution)/shard_map/all_to_all | solution.py:270
  66.7 4.0 %collective-permute-start.4 = (bf16[512,640]{1,0:T(8,128)(2,1)S(1)}, bf16[512,640]{1,0:T(8,128)(2,1)S(1)}, u32[]{:S(2)}, u32[]{:S(2)}) collective-permute-start(bf16[512,640]{1,0:T(8,128)(2,1)S(1)} %get-tuple-element.18), channel_id=1, source_target_pairs={{0,16},{16,0},{1,17},{17,1},{2,18},{18,2},{3,19},{19,3},{4,20},{20... | collective-permute-start | bytes 1966088 | tf_op jit(solution)/shard_map/ppermute | solution.py:266
  80.0 21.1 %all-to-all-start.3 = ((bf16[16,8,640]{2,1,0:T(8,128)(2,1)}), bf16[16,8,640]{2,1,0:T(8,128)(2,1)S(1)}, u32[]{:S(2)}, u32[]{:S(2)}) async-start(bf16[16,8,640]{2,1,0:T(8,128)(2,1)} %bitcast.8), calls=%async_computation.3 | async-start | bytes 327680 | tf_op jit(solution)/shard_map/all_to_all | solution.py:270
  87.9 13.8 %collective-permute-start.5 = (bf16[256,640]{1,0:T(8,128)(2,1)S(1)}, bf16[256,640]{1,0:T(8,128)(2,1)S(1)}, u32[]{:S(2)}, u32[]{:S(2)}) collective-permute-start(bf16[256,640]{1,0:T(8,128)(2,1)S(1)} %slice.30), channel_id=1, source_target_pairs={{0,1},{1,0},{2,3},{3,2},{4,5},{5,4},{6,7},{7,6},{8,9},{9,8},{10,11... | collective-permute-start | bytes 983048 | tf_op jit(solution)/shard_map/ppermute | solution.py:266
